TPU v7x, 256 devices: a whole 4x4x8 slice. The times are simulated.
256 devices in a mesh: lat: 8 (over x_lo, y), lon: 32 (over x_hi, z, core).
Axes of the slice: x: 4 (x_hi: 2, x_lo: 2; x = x_hi * 2 + x_lo), y: 4, z: 8, core: 2. Of those that a mesh axis runs over, the one named last changes fastest.
Arguments:
- tokens: bfloat16 [2, 48, 384, 512], P(None, 'lat', 'lon'), may hold values from -6 to 6
- coarse: bfloat16 [2, 24, 192, 1024], P(None, 'lat', 'lon'), may hold values from -6 to 6
- output_cotangent: bfloat16 [2, 48, 384, 512], P(None, 'lat', 'lon'), may hold values from -6 to 6
- token_class: int32 [2, 48, 384], P(None, 'lat', 'lon'), may hold values 0 or 1
- relative_index: int32 [144, 144], replicated, may hold values from 0 to 758
- encoder_gain: float32 [512], replicated, may hold values from 0.1 to 1.9
- encoder_offset: float32 [512], replicated, may hold values from -3 to 3
- encoder_projection: bfloat16 [512, 1536], replicated, may hold values from -0.25 to 0.25
- encoder_projection_bias: float32 [1536], replicated, may hold values from -3 to 3
- encoder_output_weight: bfloat16 [512, 512], replicated, may hold values from -0.25 to 0.25
- encoder_output_bias: float32 [512], replicated, may hold values from -3 to 3
- encoder_table: float32 [8, 759], replicated, may hold values from -6 to 323, as said below
- decoder_gain: float32 [512], replicated, may hold values from 0.1 to 1.9
- decoder_offset: float32 [512], replicated, may hold values from -3 to 3
- decoder_projection: bfloat16 [512, 1536], replicated, may hold values from -0.25 to 0.25
- decoder_projection_bias: float32 [1536], replicated, may hold values from -3 to 3
- decoder_output_weight: bfloat16 [512, 512], replicated, may hold values from -0.25 to 0.25
- decoder_output_bias: float32 [512], replicated, may hold values from -3 to 3
- decoder_table: float32 [8, 759], replicated, may hold values from -6 to 323, as said below
- split_weight: bfloat16 [1024, 2048], replicated, may hold values from -0.1875 to 0.1875
- split_bias: float32 [2048], replicated, may hold values from -3 to 3
Outputs:
- decoded: bfloat16 [2, 48, 384, 512], P(None, 'lat', 'lon')
- tokens_gradient: bfloat16 [2, 48, 384, 512], P(None, 'lat', 'lon')
- coarse_gradient: bfloat16 [2, 24, 192, 1024], P(None, 'lat', 'lon')
Inputs may be any that keep to these rules, and one draw needn't show every extreme that they name: `encoder_table`: learned relative-position biases. `decoder_table`: learned relative-position biases.
All inputs are finite; a program needn't handle non-finite values. No bound on the sum of `token_class` on one device may be relied on, other than what follows from the above.
Results may differ from a plain program's by a relative error of at most 0.025.
Values may be sent and summed in bfloat16 or wider, within the bound.
No kernel may reach another device: no remote copies, remote signals or barrier semaphores. Data moves between devices by JAX's collectives and lax.ppermute only.
A program may use at most 64 MiB of HBM per device.

v0:
```python
import jax
import jax.numpy as jnp
from jax import lax
from jax.sharding import PartitionSpec as P

HEADS = 8
LEVELS = 2
WIN_LAT = 6
WIN_LON = 12


eps = 1e-05


def shifted(value, axis, steps):
    count = lax.axis_size(axis)
    pairs = [(source, (source + steps) % count) for source in range(count)]
    return lax.ppermute(value, axis, pairs)


def layer_norm(values, gain, offset):
    widened = values.astype(jnp.float32)
    centred = widened - jnp.mean(widened, axis=-1, keepdims=True)
    variance = jnp.mean(centred * centred, axis=-1, keepdims=True)
    return centred * lax.rsqrt(variance + eps) * gain + offset


def project(values, gain, offset, weight, bias):
    normed = layer_norm(values, gain, offset).astype(jnp.bfloat16)
    flat = normed.reshape(-1, normed.shape[-1])
    mixed = jnp.dot(flat, weight, preferred_element_type=jnp.float32) + bias
    return mixed.astype(jnp.bfloat16).reshape(values.shape[:-1] + (weight.shape[1],))


def lookup_biases(stacked_tables, relative_index):
    span = relative_index.shape[0]
    entries = stacked_tables.shape[1]
    block_rows = 8
    entry_ids = jnp.arange(entries, dtype=jnp.int32)

    def one_block(rows):
        selector = (rows[:, :, None] == entry_ids[None, None, :]).astype(jnp.float32)
        return jnp.einsum("qke,he->hqk", selector, stacked_tables, precision=lax.Precision.HIGHEST)

    blocks = lax.map(one_block, relative_index.reshape(span // block_rows, block_rows, span))
    looked = blocks.transpose(1, 0, 2, 3).reshape(stacked_tables.shape[0], span, span)
    return lax.optimization_barrier(looked)


def to_windows(grid):
    levels, height, breadth, features = grid.shape
    split = grid.reshape(levels, height // WIN_LAT, WIN_LAT, breadth // WIN_LON, WIN_LON, features)
    split = split.transpose(1, 3, 0, 2, 4, 5)
    return split.reshape(
        height // WIN_LAT * (breadth // WIN_LON), levels * WIN_LAT * WIN_LON, features
    )


def from_windows(windows, height, breadth):
    features = windows.shape[-1]
    split = windows.reshape(
        height // WIN_LAT, breadth // WIN_LON, LEVELS, WIN_LAT, WIN_LON, features
    )
    return split.transpose(2, 0, 3, 1, 4, 5).reshape(LEVELS, height, breadth, features)


def attend_windows(projected, allowed, bias_full):
    count, span, triple = projected.shape
    features = triple // 3
    head_size = features // HEADS
    queries = projected[..., :features].reshape(count, span, HEADS, head_size)
    keys_part = projected[..., features : 2 * features].reshape(count, span, HEADS, head_size)
    values_part = projected[..., 2 * features :].reshape(count, span, HEADS, head_size)
    scores = jnp.einsum("wqhd,wkhd->whqk", queries, keys_part, preferred_element_type=jnp.float32)
    scores = scores * head_size ** (-0.5) + bias_full[None]
    scores = jnp.where(allowed[:, None], scores, -1e30)
    probs = jax.nn.softmax(scores, axis=-1).astype(jnp.bfloat16)
    mixed = jnp.einsum("whqk,wkhd->wqhd", probs, values_part, preferred_element_type=jnp.float32)
    return mixed.reshape(count, span, features).astype(jnp.bfloat16)


def attend_region(projected, labels, bias_full):
    height, breadth = (projected.shape[1], projected.shape[2])
    window_labels = to_windows(labels[..., None])[..., 0]
    allowed = window_labels[:, :, None] == window_labels[:, None, :]
    mixed = attend_windows(to_windows(projected), allowed, bias_full)
    return from_windows(mixed, height, breadth)


def widen(payload, classes):
    half_lat = WIN_LAT // 2
    half_lon = WIN_LON // 2
    row_rim = shifted((payload[:, :half_lat], classes[:, :half_lat]), "lat", -1)
    lifted = jnp.concatenate([payload, row_rim[0]], axis=1)[:, half_lat:]
    lifted_class = jnp.concatenate([classes, row_rim[1]], axis=1)[:, half_lat:]
    col_rim = shifted((lifted[:, :, :half_lon], lifted_class[:, :, :half_lon]), "lon", -1)
    region = jnp.concatenate([lifted[:, :, half_lon:], col_rim[0]], axis=2)
    region_class = jnp.concatenate([lifted_class[:, :, half_lon:], col_rim[1]], axis=2)
    return (region, region_class)


def settle(region):
    half_lat = WIN_LAT // 2
    half_lon = WIN_LON // 2
    height = region.shape[1]
    breadth = region.shape[2]
    from_right = shifted(region[:, :, breadth - half_lon :], "lon", 1)
    interior = jnp.concatenate([from_right, region[:, :, : breadth - half_lon]], axis=2)
    upper_rows = shifted(interior[:, height - half_lat :], "lat", 1)
    return jnp.concatenate([upper_rows, interior[:, : height - half_lat]], axis=1)


def expand(coarse, weight, bias):
    levels, height, breadth, features = coarse.shape
    flat = jnp.dot(coarse.reshape(-1, features), weight, preferred_element_type=jnp.float32) + bias
    fine = flat.reshape(levels, height, breadth, 2, 2, features // 2)
    return fine.transpose(0, 1, 3, 2, 4, 5).reshape(levels, 2 * height, 2 * breadth, features // 2)


def swin_pass(
    tokens, classes, seam_flag, gain, offset, weight, bias, out_weight, out_bias, bias_full
):
    features = tokens.shape[-1]
    projected, project_back = jax.vjp(
        lambda inputs: project(inputs, gain, offset, weight, bias), tokens
    )
    region, region_class = widen(projected, classes)
    labels = region_class * 2 + seam_flag
    mixed, local_back = jax.vjp(lambda inputs: attend_region(inputs, labels, bias_full), region)

    def to_input(grad_region):
        return project_back(settle(local_back(grad_region)[0]))[0]

    heads_out = settle(mixed)

    def finish(inputs):
        attended = (
            jnp.dot(inputs.reshape(-1, features), out_weight, preferred_element_type=jnp.float32)
            + out_bias
        )
        return (tokens.astype(jnp.float32) + attended.reshape(tokens.shape)).astype(jnp.bfloat16)

    result, finish_back = jax.vjp(finish, heads_out)

    def backward(grad_result):
        grad_heads = finish_back(grad_result)[0]
        grad_region, ignored = widen(grad_heads, classes)
        return grad_result + to_input(grad_region)

    return (result, backward)


def per_device(
    tokens,
    coarse,
    output_cotangent,
    token_class,
    relative_index,
    encoder_gain,
    encoder_offset,
    encoder_projection,
    encoder_projection_bias,
    encoder_output_weight,
    encoder_output_bias,
    encoder_table,
    decoder_gain,
    decoder_offset,
    decoder_projection,
    decoder_projection_bias,
    decoder_output_weight,
    decoder_output_bias,
    decoder_table,
    split_weight,
    split_bias,
):
    half_lat = WIN_LAT // 2
    height = tokens.shape[1]
    head_count = encoder_table.shape[0]
    is_last = lax.axis_index("lat") == lax.axis_size("lat") - 1
    seam_flag = jnp.logical_and(jnp.arange(height) >= height - half_lat, is_last).astype(jnp.int32)[
        None, :, None
    ]
    both_biases = lookup_biases(
        jnp.concatenate([encoder_table, decoder_table], axis=0), relative_index
    )
    encoder_bias = both_biases[:head_count]
    decoder_bias = both_biases[head_count:]
    encoded, encoder_back = swin_pass(
        tokens,
        token_class,
        seam_flag,
        encoder_gain,
        encoder_offset,
        encoder_projection,
        encoder_projection_bias,
        encoder_output_weight,
        encoder_output_bias,
        encoder_bias,
    )
    upsampled, expand_back = jax.vjp(
        lambda lowres: expand(lowres, split_weight, split_bias), coarse
    )
    joined = (encoded.astype(jnp.float32) + upsampled).astype(jnp.bfloat16)
    decoded, decoder_back = swin_pass(
        joined,
        token_class,
        seam_flag,
        decoder_gain,
        decoder_offset,
        decoder_projection,
        decoder_projection_bias,
        decoder_output_weight,
        decoder_output_bias,
        decoder_bias,
    )
    joined_grad = decoder_back(output_cotangent)
    coarse_gradient = expand_back(joined_grad.astype(jnp.float32))[0]
    tokens_gradient = encoder_back(joined_grad)
    return (decoded, tokens_gradient, coarse_gradient)


def solution(mesh):
    in_specs = (
        P(None, "lat", "lon", None),
        P(None, "lat", "lon", None),
        P(None, "lat", "lon", None),
        P(None, "lat", "lon"),
        P(),
        P(),
        P(),
        P(),
        P(),
        P(),
        P(),
        P(),
        P(),
        P(),
        P(),
        P(),
        P(),
        P(),
        P(),
        P(),
        P(),
    )
    out_specs = (
        P(None, "lat", "lon", None),
        P(None, "lat", "lon", None),
        P(None, "lat", "lon", None),
    )
    return jax.shard_map(
        per_device, mesh=mesh, in_specs=in_specs, out_specs=out_specs, check_vma=False
    )
```

profile of v0, /device:TPU:24, one launch (start us, length us, event | category | flops | bytes accessed | tf_op | source)
XLA Modules:
  0.0 269.2 jit_solution(3781515896086844535)
XLA Ops:
  13.5 57.7 %while.11 = (s32[]{:T(128)}, f32[18,16,8,144]{3,2,0,1:T(8,128)}, s32[18,8,144]{2,1,0:T(8,128)}, f32[16,759]{1,0:T(8,128)S(1)}, s32[]{:T(128)}) while((s32[]{:T(128)}, f32[18,16,8,144]{3,2,0,1:T(8,128)}, s32[18,8,144]{2,1,0:T(8,128)}, f32[16,759]{1,0:T(8,128)S(1)}, s32[]{:T(128)}) %tuple.54), condition=%wide.region_3.4_spmd.clone, body=%wide.region_2.3_spmd.clone.sunk | while | flops 168753024 | bytes 341005 | solution.py:45
  71.3 2.9 %fusion.79 = (f32[8,144,144]{2,1,0:T(8,128)}, f32[8,144,144]{2,1,0:T(8,128)S(1)}) fusion(f32[16,144,144]{2,1,0:T(8,128)} %bitcast.133), kind=kLoop, calls=%fused_computation.157 | loop fusion | bytes 2654208 | tf_op jit(solution)/shard_map/slice | solution.py:187
  74.2 3.0 %convolution_add_fusion.2 = f32[36,2048]{1,0:T(8,128)S(1)} fusion(bf16[36,1024]{1,0:T(8,128)(2,1)S(1)} %reshape.454, bf16[1024,2048]{1,0:T(8,128)(2,1)} %param.42, f32[2048]{0:T(1024)S(1)} %copy-done.44), kind=kOutput, calls=%fused_computation.14 | convolution fusion | flops 151068672 | bytes 4571136 | tf_op jit(solution)/shard_map/jvp()/dot_general | solution.py:115
  77.3 5.2 %collective-permute-start.3 = (s32[2,6,6]{2,0,1:T(2,128)S(1)}, s32[2,6,6]{2,0,1:T(2,128)S(1)}, u32[]{:S(2)}, u32[]{:S(2)}) collective-permute-start(s32[2,6,6]{2,0,1:T(2,128)S(1)} %get-tuple-element.87), channel_id=1, source_target_pairs={{0,31},{1,0},{2,1},{3,2},{4,3},{5,4},{6,5},{7,6},{8,7},{9,8},{10,9... | collective-permute-start | bytes 872 | tf_op jit(solution)/shard_map/ppermute | solution.py:18
  88.5 3.9 %collective-permute-start.1 = (bf16[2,6,6,1536]{3,2,1,0:T(8,128)(2,1)S(1)}, bf16[2,6,6,1536]{3,2,1,0:T(8,128)(2,1)S(1)}, u32[]{:S(2)}, u32[]{:S(2)}) collective-permute-start(bf16[2,6,6,1536]{3,2,1,0:T(8,128)(2,1)S(1)} %get-tuple-element.65), channel_id=1, source_target_pairs={{0,31},{1,0},{2,1},{3,2},{4,3},{5,4},{6,5},{7,6},{8,7},{9,8},{10,9... | collective-permute-start | bytes 663560 | tf_op jit(solution)/shard_map/ppermute | solution.py:18
  92.5 4.1 %collective-permute-done.1 = bf16[2,6,6,1536]{3,2,1,0:T(8,128)(2,1)S(1)} collective-permute-done((bf16[2,6,6,1536]{3,2,1,0:T(8,128)(2,1)S(1)}, bf16[2,6,6,1536]{3,2,1,0:T(8,128)(2,1)S(1)}, u32[]{:S(2)}, u32[]{:S(2)}) %collective-permute-start.1) | collective-permute-done | bytes 221216 | tf_op jit(solution)/shard_map/ppermute | solution.py:18
  106.5 6.3 %collective-permute-done.4 = bf16[2,6,6,512]{3,2,1,0:T(8,128)(2,1)S(1)} collective-permute-done((bf16[2,6,6,512]{3,2,1,0:T(8,128)(2,1)S(1)}, bf16[2,6,6,512]{3,2,1,0:T(8,128)(2,1)S(1)}, u32[]{:S(2)}, u32[]{:S(2)}) %collective-permute-start.4) | collective-permute-done | bytes 73760 | tf_op jit(solution)/shard_map/ppermute | solution.py:18
  112.8 3.3 %collective-permute-start.5 = (bf16[2,3,12,512]{3,2,1,0:T(8,128)(2,1)S(1)}, bf16[2,3,12,512]{3,2,1,0:T(8,128)(2,1)S(1)}, u32[]{:S(2)}, u32[]{:S(2)}) collective-permute-start(bf16[2,3,12,512]{3,2,1,0:T(8,128)(2,1)S(1)} %fusion.70), channel_id=1, source_target_pairs={{0,32},{32,64},{64,96},{96,128},{128,160},{160,192},{192,224},{224... | collective-permute-start | bytes 221192 | tf_op jit(solution)/shard_map/ppermute | solution.py:18
  134.2 5.7 %collective-permute-done.6 = bf16[2,3,12,1536]{3,2,1,0:T(8,128)(2,1)S(1)} collective-permute-done((bf16[2,3,12,1536]{3,2,1,0:T(8,128)(2,1)S(1)}, bf16[2,3,12,1536]{3,2,1,0:T(8,128)(2,1)S(1)}, u32[]{:S(2)}, u32[]{:S(2)}) %collective-permute-start.6) | collective-permute-done | bytes 221216 | tf_op jit(solution)/shard_map/ppermute | solution.py:18
  143.8 2.9 %copy.134 = f32[8,144,144]{1,2,0:T(8,128)} copy(f32[8,144,144]{2,1,0:T(8,128)} %get-tuple-element.60) | data formatting | bytes 1327104
  160.5 2.6 fusion.23
  163.0 3.2 %convolution_convert_fusion.4 = bf16[8,144,64]{1,2,0:T(8,128)(2,1)} fusion(bf16[144,8,64]{0,2,1:T(8,128)(2,1)} %bitcast.142, bf16[8,144,144]{1,2,0:T(8,128)(2,1)} %get-tuple-element.93, f32[8,144]{1,0:T(8,128)S(1)} %neg.20, f32[8,144]{1,0:T(8,128)S(1)} %get-tuple-element.90, pred[144,144]{0,1:T(8,128)(4,1)S(1)} %copy-done.23, f32[8,144,144]{1,2,0:T(8,128)} %copy-done.3), kind=kOutput, calls=%fused_computation.33 | convolution fusion | flops 22469904 | bytes 1320192 | tf_op jit(solution)/shard_map/transpose(jvp(wqhd,wkhd->whqk))/dot_general | solution.py:74
  166.2 3.3 %convolution_convert_fusion.5 = bf16[8,144,64]{1,2,0:T(8,128)(2,1)} fusion(bf16[144,8,64]{0,2,1:T(8,128)(2,1)} %bitcast.144, bf16[8,144,144]{1,2,0:T(8,128)(2,1)} %get-tuple-element.93, f32[8,144]{1,0:T(8,128)S(1)} %neg.20, f32[8,144]{1,0:T(8,128)S(1)} %get-tuple-element.90, pred[144,144]{0,1:T(8,128)(4,1)S(1)} %copy-done.23, f32[8,144,144]{1,2,0:T(8,128)} %copy-done.3), kind=kOutput, calls=%fused_computation.34 | convolution fusion | flops 22469904 | bytes 1320192 | tf_op jit(solution)/shard_map/transpose(jvp(wqhd,wkhd->whqk))/dot_general | solution.py:74
  169.5 2.8 %convolution_convert_fusion.7 = bf16[8,64,144]{2,1,0:T(8,128)(2,1)} fusion(bf16[1,144,8,64]{1,3,2,0:T(8,128)(2,1)S(1)} %copy-done.15, f32[8,144]{1,0:T(8,128)S(1)} %get-tuple-element.90, f32[8,144,144]{1,2,0:T(8,128)} %copy-done.3), kind=kOutput, calls=%fused_computation.36 | convolution fusion | flops 21806352 | bytes 963072 | tf_op jit(solution)/shard_map/transpose(jvp(whqk,wkhd->wqhd))/dot_general | solution.py:78
  172.3 2.9 %fusion.31 = bf16[1,144,8,64]{1,3,2,0:T(8,128)(2,1)} fusion(bf16[144,8,64]{0,2,1:T(8,128)(2,1)} %bitcast.146, f32[8,144]{1,0:T(8,128)S(1)} %get-tuple-element.90, f32[8,144,144]{1,2,0:T(8,128)} %copy-done.3), kind=kOutput, calls=%fused_computation.56 | convolution fusion | flops 21806352 | bytes 963072 | tf_op jit(solution)/shard_map/jvp(whqk,wkhd->wqhd)/dot_general | solution.py:78
  187.1 5.3 %collective-permute-done.8 = bf16[2,6,6,512]{3,2,1,0:T(8,128)(2,1)S(1)} collective-permute-done((bf16[2,6,6,512]{3,2,1,0:T(8,128)(2,1)S(1)}, bf16[2,6,6,512]{3,2,1,0:T(8,128)(2,1)S(1)}, u32[]{:S(2)}, u32[]{:S(2)}) %collective-permute-start.8) | collective-permute-done | bytes 73760 | tf_op jit(solution)/shard_map/ppermute | solution.py:18
  193.7 3.4 %collective-permute-done.9 = bf16[2,3,12,512]{3,2,1,0:T(8,128)(2,1)S(1)} collective-permute-done((bf16[2,3,12,512]{3,2,1,0:T(8,128)(2,1)S(1)}, bf16[2,3,12,512]{3,2,1,0:T(8,128)(2,1)S(1)}, u32[]{:S(2)}, u32[]{:S(2)}) %collective-permute-start.9) | collective-permute-done | bytes 73760 | tf_op jit(solution)/shard_map/ppermute | solution.py:18
  200.6 3.3 %collective-permute-start.13 = (bf16[2,3,12,1536]{3,2,1,0:T(8,128)(2,1)}, bf16[2,3,12,1536]{3,2,1,0:T(8,128)(2,1)}, u32[]{:S(2)}, u32[]{:S(2)}) collective-permute-start(bf16[2,3,12,1536]{3,2,1,0:T(8,128)(2,1)} %fusion.58), channel_id=1, source_target_pairs={{0,32},{32,64},{64,96},{96,128},{128,160},{160,192},{192,224},{224... | collective-permute-start | bytes 663560 | tf_op jit(solution)/shard_map/ppermute | solution.py:18
  220.3 7.1 %collective-permute-done.14 = bf16[2,3,12,512]{3,2,1,0:T(8,128)(2,1)S(1)} collective-permute-done((bf16[2,3,12,512]{3,2,1,0:T(8,128)(2,1)S(1)}, bf16[2,3,12,512]{3,2,1,0:T(8,128)(2,1)S(1)}, u32[]{:S(2)}, u32[]{:S(2)}) %collective-permute-start.14) | collective-permute-done | bytes 73760 | tf_op jit(solution)/shard_map/ppermute | solution.py:18
  231.0 2.7 %fusion.29 = (f32[8,144]{1,0:T(8,128)S(1)}, bf16[8,144,144]{1,2,0:T(8,128)(2,1)}) fusion(f32[8,144,144]{1,2,0:T(8,128)} %get-tuple-element.89, f32[8,144]{1,0:T(8,128)S(1)} %multiply_divide_fusion, bf16[144,8,64]{0,2,1:T(8,128)(2,1)} %bitcast.140, bf16[1,144,8,64]{1,3,2,0:T(8,128)(2,1)} %copy.111), kind=kOutput, calls=%fused_computation.50 | convolution fusion | flops 22061952 | bytes 1299456 | tf_op jit(solution)/shard_map/transpose(jvp(whqk,wkhd->wqhd))/dot_general | solution.py:78
  233.7 2.4 convolution_convert_fusion.2
  236.2 2.4 convolution_convert_fusion.3
  244.2 8.1 %collective-permute-done.16 = bf16[2,6,6,1536]{3,2,1,0:T(8,128)(2,1)S(1)} collective-permute-done((bf16[2,6,6,1536]{3,2,1,0:T(8,128)(2,1)S(1)}, bf16[2,6,6,1536]{3,2,1,0:T(8,128)(2,1)S(1)}, u32[]{:S(2)}, u32[]{:S(2)}) %collective-permute-start.16) | collective-permute-done | bytes 221216 | tf_op jit(solution)/shard_map/ppermute | solution.py:18
  255.0 3.5 %convolution_convert_fusion.14 = bf16[36,1024]{1,0:T(8,128)(2,1)S(1)} fusion(bf16[36,2048]{1,0:T(8,128)(2,1)S(1)} %reshape.484, bf16[1024,2048]{1,0:T(8,128)(2,1)} %param.42), kind=kOutput, calls=%fused_computation.63 | convolution fusion | flops 151031808 | bytes 4415488 | tf_op jit(solution)/shard_map/transpose(jvp())/dot_general | solution.py:115
  (311 shorter events, 177.1 us)
Async XLA Ops:
  0.6 127.1 %copy-start = (bf16[512,1536]{1,0:T(8,128)(2,1)S(1)}, bf16[512,1536]{1,0:T(8,128)(2,1)}, u32[]{:S(2)}) copy-start(bf16[512,1536]{1,0:T(8,128)(2,1)} %param.37) | copy-start | bytes 4718596
  7.9 77.6 %collective-permute-start = (bf16[2,3,12,1536]{3,2,1,0:T(8,128)(2,1)}, bf16[2,3,12,1536]{3,2,1,0:T(8,128)(2,1)}, u32[]{:S(2)}, u32[]{:S(2)}) collective-permute-start(bf16[2,3,12,1536]{3,2,1,0:T(8,128)(2,1)} %slice.175), channel_id=1, source_target_pairs={{0,224},{32,0},{64,32},{96,64},{128,96},{160,128},{192,160},{224,1... | collective-permute-start | bytes 663560 | tf_op jit(solution)/shard_map/ppermute | solution.py:18
  8.7 68.5 %collective-permute-start.2 = (s32[2,3,12]{2,0,1:T(2,128)S(1)}, s32[2,3,12]{2,0,1:T(2,128)S(1)}, u32[]{:S(2)}, u32[]{:S(2)}) collective-permute-start(s32[2,3,12]{2,0,1:T(2,128)S(1)} %slice.140), channel_id=1, source_target_pairs={{0,224},{32,0},{64,32},{96,64},{128,96},{160,128},{192,160},{224,1... | collective-permute-start | bytes 872 | tf_op jit(solution)/shard_map/ppermute | solution.py:18
  10.3 105.7 %collective-permute-start.10 = (bf16[2,3,12,512]{3,2,1,0:T(8,128)(2,1)}, bf16[2,3,12,512]{3,2,1,0:T(8,128)(2,1)}, u32[]{:S(2)}, u32[]{:S(2)}) collective-permute-start(bf16[2,3,12,512]{3,2,1,0:T(8,128)(2,1)} %slice.199), channel_id=1, source_target_pairs={{0,224},{32,0},{64,32},{96,64},{128,96},{160,128},{192,160},{224,1... | collective-permute-start | bytes 221192 | tf_op jit(solution)/shard_map/ppermute | solution.py:18
  77.3 8.0 %collective-permute-start.3 = (s32[2,6,6]{2,0,1:T(2,128)S(1)}, s32[2,6,6]{2,0,1:T(2,128)S(1)}, u32[]{:S(2)}, u32[]{:S(2)}) collective-permute-start(s32[2,6,6]{2,0,1:T(2,128)S(1)} %get-tuple-element.87), channel_id=1, source_target_pairs={{0,31},{1,0},{2,1},{3,2},{4,3},{5,4},{6,5},{7,6},{8,7},{9,8},{10,9... | collective-permute-start | bytes 872 | tf_op jit(solution)/shard_map/ppermute | solution.py:18
  88.5 8.1 %collective-permute-start.1 = (bf16[2,6,6,1536]{3,2,1,0:T(8,128)(2,1)S(1)}, bf16[2,6,6,1536]{3,2,1,0:T(8,128)(2,1)S(1)}, u32[]{:S(2)}, u32[]{:S(2)}) collective-permute-start(bf16[2,6,6,1536]{3,2,1,0:T(8,128)(2,1)S(1)} %get-tuple-element.65), channel_id=1, source_target_pairs={{0,31},{1,0},{2,1},{3,2},{4,3},{5,4},{6,5},{7,6},{8,7},{9,8},{10,9... | collective-permute-start | bytes 663560 | tf_op jit(solution)/shard_map/ppermute | solution.py:18
  103.7 17.9 %copy-start.8 = (bf16[512,512]{1,0:T(8,128)(2,1)S(1)}, bf16[512,512]{1,0:T(8,128)(2,1)}, u32[]{:S(2)}) copy-start(bf16[512,512]{1,0:T(8,128)(2,1)} %param.32) | copy-start | bytes 1572868
  103.7 17.9 %copy-start.45 = (f32[512]{0:T(512)S(1)}, f32[512]{0:T(512)}, u32[]{:S(2)}) copy-start(f32[512]{0:T(512)} %param.33) | copy-start | bytes 6148
  104.8 8.0 %collective-permute-start.4 = (bf16[2,6,6,512]{3,2,1,0:T(8,128)(2,1)S(1)}, bf16[2,6,6,512]{3,2,1,0:T(8,128)(2,1)S(1)}, u32[]{:S(2)}, u32[]{:S(2)}) collective-permute-start(bf16[2,6,6,512]{3,2,1,0:T(8,128)(2,1)S(1)} %get-tuple-element.84), channel_id=1, source_target_pairs={{0,1},{1,2},{2,3},{3,4},{4,5},{5,6},{6,7},{7,8},{8,9},{9,10},{10,1... | collective-permute-start | bytes 221192 | tf_op jit(solution)/shard_map/ppermute | solution.py:18
  112.8 6.4 %collective-permute-start.5 = (bf16[2,3,12,512]{3,2,1,0:T(8,128)(2,1)S(1)}, bf16[2,3,12,512]{3,2,1,0:T(8,128)(2,1)S(1)}, u32[]{:S(2)}, u32[]{:S(2)}) collective-permute-start(bf16[2,3,12,512]{3,2,1,0:T(8,128)(2,1)S(1)} %fusion.70), channel_id=1, source_target_pairs={{0,32},{32,64},{64,96},{96,128},{128,160},{160,192},{192,224},{224... | collective-permute-start | bytes 221192 | tf_op jit(solution)/shard_map/ppermute | solution.py:18
  117.6 6.9 %copy-start.1 = (bf16[2,6,12,512]{3,0,2,1:T(2,128)(2,1)S(1)}, bf16[2,6,12,512]{3,0,2,1:T(2,128)(2,1)}, u32[]{:S(2)}) copy-start(bf16[2,6,12,512]{3,0,2,1:T(2,128)(2,1)} %param.23) | copy-start | bytes 442372
  131.0 8.9 %collective-permute-start.6 = (bf16[2,3,12,1536]{3,2,1,0:T(8,128)(2,1)S(1)}, bf16[2,3,12,1536]{3,2,1,0:T(8,128)(2,1)S(1)}, u32[]{:S(2)}, u32[]{:S(2)}) collective-permute-start(bf16[2,3,12,1536]{3,2,1,0:T(8,128)(2,1)S(1)} %slice.188), channel_id=1, source_target_pairs={{0,224},{32,0},{64,32},{96,64},{128,96},{160,128},{192,160},{224,1... | collective-permute-start | bytes 663560 | tf_op jit(solution)/shard_map/ppermute | solution.py:18
  140.8 8.8 %collective-permute-start.7 = (bf16[2,6,6,1536]{3,2,1,0:T(8,128)(2,1)}, bf16[2,6,6,1536]{3,2,1,0:T(8,128)(2,1)}, u32[]{:S(2)}, u32[]{:S(2)}) collective-permute-start(bf16[2,6,6,1536]{3,2,1,0:T(8,128)(2,1)} %get-tuple-element.63), channel_id=1, source_target_pairs={{0,31},{1,0},{2,1},{3,2},{4,3},{5,4},{6,5},{7,6},{8,7},{9,8},{10,9... | collective-permute-start | bytes 663560 | tf_op jit(solution)/shard_map/ppermute | solution.py:18
  141.8 4.8 %collective-permute-start.11 = (bf16[2,6,6,512]{3,2,1,0:T(8,128)(2,1)S(1)}, bf16[2,6,6,512]{3,2,1,0:T(8,128)(2,1)S(1)}, u32[]{:S(2)}, u32[]{:S(2)}) collective-permute-start(bf16[2,6,6,512]{3,2,1,0:T(8,128)(2,1)S(1)} %get-tuple-element.79), channel_id=1, source_target_pairs={{0,31},{1,0},{2,1},{3,2},{4,3},{5,4},{6,5},{7,6},{8,7},{9,8},{10,9... | collective-permute-start | bytes 221192 | tf_op jit(solution)/shard_map/ppermute | solution.py:18
  184.6 7.8 %collective-permute-start.8 = (bf16[2,6,6,512]{3,2,1,0:T(8,128)(2,1)S(1)}, bf16[2,6,6,512]{3,2,1,0:T(8,128)(2,1)S(1)}, u32[]{:S(2)}, u32[]{:S(2)}) collective-permute-start(bf16[2,6,6,512]{3,2,1,0:T(8,128)(2,1)S(1)} %get-tuple-element.82), channel_id=1, source_target_pairs={{0,1},{1,2},{2,3},{3,4},{4,5},{5,6},{6,7},{7,8},{8,9},{9,10},{10,1... | collective-permute-start | bytes 221192 | tf_op jit(solution)/shard_map/ppermute | solution.py:18
  186.7 12.1 %collective-permute-start.12 = (bf16[2,6,6,1536]{3,2,1,0:T(8,128)(2,1)}, bf16[2,6,6,1536]{3,2,1,0:T(8,128)(2,1)}, u32[]{:S(2)}, u32[]{:S(2)}) collective-permute-start(bf16[2,6,6,1536]{3,2,1,0:T(8,128)(2,1)} %get-tuple-element.68), channel_id=1, source_target_pairs={{0,1},{1,2},{2,3},{3,4},{4,5},{5,6},{6,7},{7,8},{8,9},{9,10},{10,1... | collective-permute-start | bytes 663560 | tf_op jit(solution)/shard_map/ppermute | solution.py:18
  192.4 4.7 %collective-permute-start.9 = (bf16[2,3,12,512]{3,2,1,0:T(8,128)(2,1)S(1)}, bf16[2,3,12,512]{3,2,1,0:T(8,128)(2,1)S(1)}, u32[]{:S(2)}, u32[]{:S(2)}) collective-permute-start(bf16[2,3,12,512]{3,2,1,0:T(8,128)(2,1)S(1)} %fusion.69), channel_id=1, source_target_pairs={{0,32},{32,64},{64,96},{96,128},{128,160},{160,192},{192,224},{224... | collective-permute-start | bytes 221192 | tf_op jit(solution)/shard_map/ppermute | solution.py:18
  200.6 7.9 %collective-permute-start.13 = (bf16[2,3,12,1536]{3,2,1,0:T(8,128)(2,1)}, bf16[2,3,12,1536]{3,2,1,0:T(8,128)(2,1)}, u32[]{:S(2)}, u32[]{:S(2)}) collective-permute-start(bf16[2,3,12,1536]{3,2,1,0:T(8,128)(2,1)} %fusion.58), channel_id=1, source_target_pairs={{0,32},{32,64},{64,96},{96,128},{128,160},{160,192},{192,224},{224... | collective-permute-start | bytes 663560 | tf_op jit(solution)/shard_map/ppermute | solution.py:18
  218.7 8.8 %copy-start.40 = (f32[8,144]{1,0:T(8,128)S(1)}, f32[8,144]{1,0:T(8,128)}, u32[]{:S(2)}) copy-start(f32[8,144]{1,0:T(8,128)} %copy-done.39) | copy-start | bytes 13828
  220.2 7.3 %collective-permute-start.14 = (bf16[2,3,12,512]{3,2,1,0:T(8,128)(2,1)S(1)}, bf16[2,3,12,512]{3,2,1,0:T(8,128)(2,1)S(1)}, u32[]{:S(2)}, u32[]{:S(2)}) collective-permute-start(bf16[2,3,12,512]{3,2,1,0:T(8,128)(2,1)S(1)} %slice.206), channel_id=1, source_target_pairs={{0,224},{32,0},{64,32},{96,64},{128,96},{160,128},{192,160},{224,1... | collective-permute-start | bytes 221192 | tf_op jit(solution)/shard_map/ppermute | solution.py:18
  227.5 2.3 collective-permute-start.15
  242.3 16.3 %copy-start.5 = (bf16[2,6,6,1536]{3,2,1,0:T(8,128)(2,1)}, bf16[2,6,6,1536]{3,2,1,0:T(8,128)(2,1)S(1)}, u32[]{:S(2)}) copy-start(bf16[2,6,6,1536]{3,2,1,0:T(8,128)(2,1)S(1)} %get-tuple-element.67) | copy-start | bytes 663556
  242.3 10.0 %collective-permute-start.16 = (bf16[2,6,6,1536]{3,2,1,0:T(8,128)(2,1)S(1)}, bf16[2,6,6,1536]{3,2,1,0:T(8,128)(2,1)S(1)}, u32[]{:S(2)}, u32[]{:S(2)}) collective-permute-start(bf16[2,6,6,1536]{3,2,1,0:T(8,128)(2,1)S(1)} %get-tuple-element.66), channel_id=1, source_target_pairs={{0,1},{1,2},{2,3},{3,4},{4,5},{5,6},{6,7},{7,8},{8,9},{9,10},{10,1... | collective-permute-start | bytes 663560 | tf_op jit(solution)/shard_map/ppermute | solution.py:18
  253.1 7.0 %collective-permute-start.17 = (bf16[2,3,12,1536]{3,2,1,0:T(8,128)(2,1)}, bf16[2,3,12,1536]{3,2,1,0:T(8,128)(2,1)}, u32[]{:S(2)}, u32[]{:S(2)}) collective-permute-start(bf16[2,3,12,1536]{3,2,1,0:T(8,128)(2,1)} %fusion.57), channel_id=1, source_target_pairs={{0,32},{32,64},{64,96},{96,128},{128,160},{160,192},{192,224},{224... | collective-permute-start | bytes 663560 | tf_op jit(solution)/shard_map/ppermute | solution.py:18
  (41 other events, 100.7 us)
where the time goes:
time: 275 us; the launch traced here: 269 us
  local copies, waits for them, and re-layouts  92.2 us (34%)
  matrix products  78.1 us (28%)
  waiting for transfers between devices  45.9 us (17%)
  starting transfers between devices  27.1 us (10%)
  other arithmetic  24.3 us (9%)
    ppermute x18, waiting for transfers between devices, shifted(): return lax.ppermute(value, axis, pairs)  45.9 us
    dot_general x18, matrix products, one_block(): jnp.einsum('qke,he->hqk', selector, stacked_tables, precision=lax.Precisi...  31.2 us
    ppermute x18, starting transfers between devices, shifted(): return lax.ppermute(value, axis, pairs)  27.1 us
    dot_general x6, matrix products, attend_windows(): jnp.einsum('wqhd,wkhd->whqk', queries, keys_part, preferred_element_type=...  14.8 us
    dynamic_update_slice x18, local copies, waits for them, and re-layouts, lookup_biases(): lax.map(one_block, relative_index.reshape(span // block_rows, block_rows,...  13.9 us
    unnamed x106, local copies, waits for them, and re-layouts  13.6 us
    dot_general x6, matrix products, attend_windows(): jnp.einsum('whqk,wkhd->wqhd', probs, values_part, preferred_element_type=...  13.4 us
    eq x18, local copies, waits for them, and re-layouts, one_block(): rows[:, :, None] == entry_ids[None, None, :]  12.6 us
  transfers between devices with their start and end apart: 18, of which 11 were waited for; matrix products, arithmetic and copies ran while one was open for 38% of the time, Pallas kernels for 0%

commit v1 on v0

v1 whole, which is shorter than its diff:
```python
import functools

import jax
import jax.numpy as jnp
from jax import lax
from jax.experimental import pallas as pl
from jax.experimental.pallas import tpu as pltpu
from jax.sharding import PartitionSpec as P

HEADS = 8
LEVELS = 2
WIN_LAT = 6
WIN_LON = 12
SPAN = LEVELS * WIN_LAT * WIN_LON
D = 512
HEAD = D // HEADS
WIDE = 256
HL, HN = WIN_LAT // 2, WIN_LON // 2
PAIRS = HL * HN
GROUP = 4
BLANK = -1e30
eps = 1e-05

f32, bf16 = jnp.float32, jnp.bfloat16
NT = (((1,), (1,)), ((), ()))
TN = (((0,), (0,)), ((), ()))


def dot(a, b):
    return jnp.dot(a, b, preferred_element_type=f32)


def dot_nt(a, b):
    return lax.dot_general(a, b, NT, preferred_element_type=f32)


def dot_tn(a, b):
    return lax.dot_general(a, b, TN, preferred_element_type=f32)


def gather_quadrants(refs, base, scratch):
    for q, ref in enumerate(refs):
        for t in range(PAIRS):
            scratch[pl.ds(2 * (q * PAIRS + t), 2), :] = ref[base + t].astype(f32)


def scatter_quadrants(scratch, refs, base):
    for q, ref in enumerate(refs):
        for t in range(PAIRS):
            ref[base + t] = scratch[pl.ds(2 * (q * PAIRS + t), 2), :].astype(bf16)


def token_place(t):
    rest = t % (2 * PAIRS)
    return t // (2 * PAIRS), rest // (2 * HN), rest % (2 * HN) // 2, rest % 2


def normalise(x):
    centred = x - jnp.mean(x, axis=-1, keepdims=True)
    variance = jnp.mean(centred * centred, axis=-1, keepdims=True)
    rstd = lax.rsqrt(variance + eps)
    return centred * rstd, rstd


def head_masks(dtype):
    lane = lax.broadcasted_iota(jnp.int32, (1, GROUP * HEAD), 1) // HEAD
    return [(lane == h).astype(dtype) for h in range(GROUP)]


def stack_heads(x):
    return jnp.concatenate([x * m for m in head_masks(x.dtype)], axis=0)


def merge_heads(y):
    masks = head_masks(f32)
    total = y[:SPAN] * masks[0]
    for h in range(1, GROUP):
        total = total + y[h * SPAN : (h + 1) * SPAN] * masks[h]
    return total


def mask_bias(refs, is_last):
    token = lax.broadcasted_iota(jnp.int32, (1, WIDE), 1)
    quadrant, r, c, level = token_place(token)
    lane = HN * (1 - quadrant % 2) + c
    hot = lax.broadcasted_iota(jnp.int32, (128, WIDE), 0) == lane
    rows = jnp.concatenate([ref[CLASS_AT + r, :, :128].astype(f32) for ref in refs for r in range(HL)], axis=0)
    spread = dot(rows.astype(bf16), hot.astype(f32).astype(bf16))
    mine = lax.broadcasted_iota(jnp.int32, (4 * HL * LEVELS, WIDE), 0) == (quadrant * HL + r) * LEVELS + level
    seam = (quadrant // 2).astype(f32) * is_last.astype(f32)
    label = 2.0 * jnp.sum(jnp.where(mine, spread, 0.0), axis=0, keepdims=True) + seam
    label = jnp.where(token < SPAN, label, 9.0)
    eye = lax.broadcasted_iota(jnp.int32, (SPAN, WIDE), 0) == lax.broadcasted_iota(jnp.int32, (SPAN, WIDE), 1)
    column = jnp.sum(jnp.where(eye, label, 0.0), axis=1, keepdims=True)
    return jnp.where(column == label, 0.0, BLANK)


def pad_keys(x):
    return jnp.concatenate([x, jnp.zeros((WIDE - SPAN, x.shape[1]), x.dtype)], axis=0)


def block_forward(x, blank, bias_of, gain, offset, weight, bias, out_weight, out_bias, qkv_ref, probs_ref):
    xhat, _ = normalise(x)
    normed = (xhat * gain + offset).astype(bf16)
    queries = (dot(normed, weight[:, :D]) + bias[:, :D]).astype(bf16) * jnp.array(HEAD**-0.5, bf16)
    qkv_ref[:, :D] = queries
    qkv_ref[:, D:] = (dot(normed, weight[:, D:]) + bias[:, D:]).astype(bf16)
    mixed = []
    for g in range(HEADS // GROUP):
        lanes = pl.ds(g * GROUP * HEAD, GROUP * HEAD)
        q4 = stack_heads(qkv_ref[:, pl.ds(g * 256, 256)])
        k4 = pad_keys(qkv_ref[:, pl.ds(D + g * 256, 256)])
        v4 = pad_keys(qkv_ref[:, pl.ds(2 * D + g * 256, 256)])
        scores = dot_nt(q4, k4)
        for h in range(GROUP):
            s = scores[h * SPAN : (h + 1) * SPAN] + bias_of(g * GROUP + h) + blank
            e = jnp.exp(s - jnp.max(s, axis=-1, keepdims=True))
            p = e * (1.0 / jnp.sum(e, axis=-1, keepdims=True))
            probs_ref[pl.ds((g * GROUP + h) * SPAN, SPAN), :] = p.astype(bf16)
        p4 = probs_ref[pl.ds(g * GROUP * SPAN, GROUP * SPAN), :]
        mixed.append(merge_heads(dot(p4, v4)))
    heads_out = jnp.concatenate(mixed, axis=1).astype(bf16)
    return x + dot(heads_out, out_weight) + out_bias


def block_backward(grad, x, gain, weight, out_weight, qkv_ref, probs_ref, dqkv_ref):
    dheads = dot_nt(grad, out_weight).astype(bf16)
    for g in range(HEADS // GROUP):
        q4 = stack_heads(qkv_ref[:, pl.ds(g * 256, 256)])
        k4 = pad_keys(qkv_ref[:, pl.ds(D + g * 256, 256)])
        v4 = pad_keys(qkv_ref[:, pl.ds(2 * D + g * 256, 256)])
        do4 = stack_heads(dheads[:, g * 256 : (g + 1) * 256])
        p4 = probs_ref[pl.ds(g * GROUP * SPAN, GROUP * SPAN), :]
        dprobs = dot_nt(do4, v4)
        pf = p4.astype(f32)
        weighted = pf * dprobs
        ds = (weighted - pf * jnp.sum(weighted, axis=-1, keepdims=True)).astype(bf16)
        dq = merge_heads(dot(ds, k4)) * HEAD**-0.5
        dk = dot_tn(ds[:, :SPAN], q4)
        dv = dot_tn(p4[:, :SPAN], do4)
        dqkv_ref[:, pl.ds(g * 256, 256)] = dq.astype(bf16)
        dqkv_ref[:, pl.ds(D + g * 256, 256)] = dk.astype(bf16)
        dqkv_ref[:, pl.ds(2 * D + g * 256, 256)] = dv.astype(bf16)
    dnormed = dot_nt(dqkv_ref[...], weight).astype(bf16).astype(f32)
    xhat, rstd = normalise(x)
    dxhat = dnormed * gain
    dx = rstd * (
        dxhat
        - jnp.mean(dxhat, axis=-1, keepdims=True)
        - xhat * jnp.mean(dxhat * xhat, axis=-1, keepdims=True)
    )
    return grad.astype(f32) + dx.astype(bf16).astype(f32)


COARSE_ROWS, COARSE_COLS = HL // 2 + 1, HN // 2
POINTS = COARSE_ROWS * COARSE_COLS
COTANGENT_AT = PAIRS
COARSE_AT = 2 * PAIRS
CLASS_AT = 2 * PAIRS + 2 * POINTS


TILES = CLASS_AT + HL


def pack_kernel(tokens, cotangent, coarse, classes, o0, o1, o2, o3, kinds, tiles, sems, first_sem):
    outs = (o0, o1, o2, o3)
    fetch = pltpu.make_async_copy(classes, kinds, first_sem)
    fetch.start()
    copies = []

    def send(src, dst):
        copy = pltpu.make_async_copy(src, dst, sems.at[len(copies)])
        copy.start()
        copies.append(copy)

    for q in (3, 2, 1, 0):
        qr, qc = divmod(q, 2)
        lat, lon = HL * (1 - qr), HN * (1 - qc)
        low_lat = (coarse.shape[0] - COARSE_ROWS) * (1 - qr)
        for r in range(HL):
            send(tokens.at[lat + r, pl.ds(lon, HN)], outs[q].at[pl.ds(r * HN, HN)])
            send(cotangent.at[lat + r, pl.ds(lon, HN)], outs[q].at[pl.ds(COTANGENT_AT + r * HN, HN)])
        for r in range(COARSE_ROWS):
            for half in range(2):
                send(
                    coarse.at[low_lat + r, pl.ds(COARSE_COLS * (1 - qc), COARSE_COLS), :, pl.ds(D * half, D)],
                    outs[q].at[pl.ds(COARSE_AT + POINTS * half + r * COARSE_COLS, COARSE_COLS)],
                )
    tiles[...] = jnp.zeros_like(tiles)
    fetch.wait()
    for r in range(WIN_LAT):
        tiles[r, :, pl.ds(0, WIN_LON)] = kinds[r].astype(f32).astype(bf16)
    for q in (3, 2, 1, 0):
        send(tiles.at[pl.ds(HL * (1 - q // 2), HL)], outs[q].at[pl.ds(CLASS_AT, HL)])
    for copy in copies:
        copy.wait()


def lookup_kernel(inputs_ref, out_ref, rest_ref, low, high, packed_low, packed_high, parts):
    token = lax.broadcasted_iota(jnp.int32, (SPAN, 1), 0)
    quadrant, r, c, level = token_place(token)
    old = level * (WIN_LAT * WIN_LON) + (quadrant // 2 * HL + r) * WIN_LON + quadrant % 2 * HN + c
    order = (lax.broadcasted_iota(jnp.int32, (SPAN, SPAN), 1) == old).astype(f32).astype(bf16)
    index = inputs_ref[:SPAN, :SPAN].astype(jnp.int32)
    rest = SPAN - 128

    lane = lax.broadcasted_iota(jnp.int32, (rest, WIDE), 1)
    spread = (lane % rest == lax.broadcasted_iota(jnp.int32, (rest, WIDE), 0)).astype(f32).astype(bf16)
    own = (
        lax.broadcasted_iota(jnp.int32, (SPAN, WIDE), 1) // rest
        == lax.broadcasted_iota(jnp.int32, (SPAN, WIDE), 0) % rest
    )
    for part, full, packed in ((index % WIDE, low, packed_low), (index // WIDE, high, packed_high)):
        moved = dot_nt(dot(order, part.astype(f32).astype(bf16)).astype(bf16), order)
        full[...] = moved[:, :128]
        tail = jnp.where(own, dot(moved[:, 128:].astype(bf16), spread), 0.0)
        for g in range(SPAN // rest):
            packed[pl.ds(g, 1), :] = jnp.sum(tail[rest * g : rest * (g + 1)], axis=0, keepdims=True)

    left = inputs_ref[SPAN:]
    blocks = left.shape[1] // WIDE
    for k in range(3):
        piece = left.astype(bf16)
        left = left - piece.astype(f32)
        for b in range(blocks):
            parts[pl.ds((b * 3 + k) * 2 * HEADS, 2 * HEADS), :] = piece[:, b * WIDE : (b + 1) * WIDE]
    entries = parts[...]
    ids = lax.broadcasted_iota(jnp.int32, (16, WIDE), 0).astype(f32)
    ids = [(ids + 16 * n).astype(bf16) for n in range(WIDE // 16)]
    one, zero = jnp.ones((16, WIDE), bf16), jnp.zeros((16, WIDE), bf16)

    def look(low_row, high_row):
        wanted = jnp.broadcast_to(low_row, (16, WIDE)).astype(bf16)
        hot = jnp.concatenate([jnp.where(wanted == i, one, zero) for i in ids], axis=0)
        found = dot(entries, hot)
        sums = []
        for b in range(blocks):
            at = [found[(b * 3 + k) * 2 * HEADS : (b * 3 + k + 1) * 2 * HEADS] for k in range(3)]
            sums.append(at[0] + at[1] + at[2])
        result = sums[0]
        for b in range(1, blocks):
            result = jnp.where(high_row == b, sums[b], result)
        return result

    def two_rows(i):
        def pair(ref):
            return jnp.concatenate([ref[pl.ds(i, 1), :], ref[pl.ds(i + 1, 1), :]], axis=1)

        result = look(pair(low), pair(high))
        for n in range(2):
            for half in range(2):
                out_ref[pl.ds(half * HEADS * SPAN + i + n, HEADS, stride=SPAN), :] = result[
                    half * HEADS : (half + 1) * HEADS, n * 128 : (n + 1) * 128
                ]

    @pl.loop(0, SPAN // 8)
    def _(step):
        for n in range(4):
            two_rows(8 * step + 2 * n)

    for g in range(SPAN // rest):
        result = look(packed_low[pl.ds(g, 1), :], packed_high[pl.ds(g, 1), :])
        for n in range(rest):
            first = n * rest // 128 * 128
            for half in range(2):
                rest_ref[pl.ds(half * HEADS * SPAN + rest * g + n, HEADS, stride=SPAN), :] = pltpu.roll(
                    result[half * HEADS : (half + 1) * HEADS, first : first + 128], (first - n * rest) % 128, axis=1
                )


def lookup(relative_index, encoder_table, decoder_table):
    blocks = -(-encoder_table.shape[1] // WIDE)

    def widen(rows):
        return jnp.pad(rows, ((0, 0), (0, blocks * WIDE - rows.shape[1])))

    inputs = jnp.concatenate([widen(relative_index.astype(f32)), widen(encoder_table), widen(decoder_table)], axis=0)
    return pl.pallas_call(
        lookup_kernel,
        out_shape=[jax.ShapeDtypeStruct((2 * HEADS * SPAN, 128), f32)] * 2,
        scratch_shapes=[
            pltpu.VMEM((SPAN, 128), f32),
            pltpu.VMEM((SPAN, 128), f32),
            pltpu.VMEM((16, WIDE), f32),
            pltpu.VMEM((16, WIDE), f32),
            pltpu.VMEM((blocks * 3 * 2 * HEADS, WIDE), bf16),
        ],
        compiler_params=pltpu.CompilerParams(vmem_limit_bytes=32 * 2**20),
        cost_estimate=pl.CostEstimate(flops=3_000_000_000, bytes_accessed=4_000_000, transcendentals=0),
        name="lookup",
    )(inputs)


def main_kernel(
    b0, b1, b2, b3, bias_main, bias_rest, is_last,
    e_gain, e_offset, e_bias, e_out_bias, d_gain, d_offset, d_bias, d_out_bias, split_bias,
    e_weight, e_out_weight, d_weight, d_out_weight, split,
    o0, o1, o2, o3, joined_grad, tokens, e_qkv, e_probs,
    scratch, coarse, fine, d_qkv, d_probs, dqkv,
):
    def bias_rows(h):
        rows = pl.ds(h * SPAN, SPAN)
        return jnp.concatenate([bias_main[rows, :], bias_rest[rows, :]], axis=1)

    parts = (b0, b1, b2, b3)
    gather_quadrants(parts, 0, scratch)
    x = scratch[...]
    tokens[...] = x.astype(bf16)
    blank = mask_bias(parts, is_last[0])
    encoded = block_forward(
        x, blank, lambda h: bias_rows(h), e_gain[...], e_offset[...], e_weight,
        e_bias[...].reshape(1, -1), e_out_weight[...], e_out_bias[...], e_qkv, e_probs,
    ).astype(bf16)

    for q, ref in enumerate(parts):
        qr, qc = divmod(q, 2)
        for r in range(COARSE_ROWS):
            for c in range(COARSE_COLS):
                at = (qr * COARSE_ROWS + r) * 2 * COARSE_COLS + qc * COARSE_COLS + c
                for half in range(2):
                    coarse[pl.ds(2 * at, 2), pl.ds(D * half, D)] = ref[
                        COARSE_AT + POINTS * half + r * COARSE_COLS + c
                    ].astype(f32)
    lowres = coarse[...].astype(bf16)
    fine[...] = dot(lowres, split[...]) + split_bias[...]
    for q in range(4):
        qr, qc = divmod(q, 2)
        for r in range(HL):
            for c in range(HN):
                row, column = qr * HL + r + HL % 2, qc * HN + c + HN % 2
                at = (row // 2) * 2 * COARSE_COLS + column // 2
                kind = (row % 2) * 2 + column % 2
                scratch[pl.ds(2 * (q * PAIRS + r * HN + c), 2), :] = fine[pl.ds(2 * at, 2), pl.ds(kind * D, D)]
    x = (encoded.astype(f32) + scratch[...]).astype(bf16).astype(f32)
    decoded = block_forward(
        x, blank, lambda h: bias_rows(HEADS + h), d_gain[...], d_offset[...], d_weight,
        d_bias[...].reshape(1, -1), d_out_weight[...], d_out_bias[...], d_qkv, d_probs,
    )
    outs = (o0, o1, o2, o3)
    scratch[...] = decoded
    scatter_quadrants(scratch, outs, 0)
    gather_quadrants(parts, COTANGENT_AT, scratch)
    grad = scratch[...].astype(bf16)
    dx = block_backward(grad, x, d_gain[...], d_weight[...], d_out_weight[...], d_qkv, d_probs, dqkv)
    scratch[...] = dx
    joined_grad[...] = dx.astype(bf16)
    scatter_quadrants(scratch, outs, PAIRS)


def encoder_back_kernel(grad, tokens, qkv, probs, gain, weight, out_weight, t0, t1, t2, t3, scratch, dqkv):
    x = tokens[...].astype(f32)
    scratch[...] = block_backward(grad[...], x, gain[...], weight[...], out_weight[...], qkv, probs, dqkv)
    scatter_quadrants(scratch, (t0, t1, t2, t3), 0)


def coarse_kernel(j0, j1, j2, j3, split, out, decoded, fine, result, sems):
    copies = []
    for q, ref in enumerate((j0, j1, j2, j3)):
        for r in range(HL):
            copy = pltpu.make_async_copy(
                ref.at[pl.ds(r * HN, HN)],
                decoded.at[q // 2 * HL + r, pl.ds(q % 2 * HN, HN)],
                sems.at[len(copies)],
            )
            copy.start()
            copies.append(copy)
    columns = WIN_LON // 2
    for q, ref in enumerate((j0, j1, j2, j3)):
        qr, qc = divmod(q, 2)
        for r in range(HL):
            for c in range(HN):
                row, column = qr * HL + r, qc * HN + c
                at = (row // 2) * columns + column // 2
                kind = (row % 2) * 2 + column % 2
                fine[pl.ds(2 * at, 2), pl.ds(kind * D, D)] = ref[PAIRS + r * HN + c].astype(f32)
    result[...] = dot_nt(fine[...].astype(bf16), split[...])
    for t in range(out.shape[0]):
        out[t] = result[pl.ds(2 * t, 2), :].astype(bf16)
    for copy in copies:
        copy.wait()


VM = pl.BlockSpec(memory_space=pltpu.VMEM)


ANY = pl.BlockSpec(memory_space=pl.ANY)


def call(kernel, name, inputs, outs, scratch, flops, in_specs=None, out_specs=None, vmem=32):
    return pl.pallas_call(
        kernel,
        out_shape=outs,
        in_specs=in_specs or [VM] * len(inputs),
        out_specs=out_specs or [VM] * len(outs),
        scratch_shapes=scratch,
        compiler_params=pltpu.CompilerParams(vmem_limit_bytes=vmem * 2**20),
        cost_estimate=pl.CostEstimate(flops=flops, bytes_accessed=flops // 1000, transcendentals=0),
        name=name,
    )(*inputs)


def shift_pairs(lat, lon, lats, lons):
    return [
        (i * lons + j, ((i + lat) % lats) * lons + (j + lon) % lons) for i in range(lats) for j in range(lons)
    ]


def exchange(pieces, steps, lats, lons):
    out = [pieces[0]]
    for q in range(1, 4):
        qr, qc = divmod(q, 2)
        out.append(lax.ppermute(pieces[q], ("lat", "lon"), shift_pairs(qr * steps, qc * steps, lats, lons)))
    return out


def per_device(
    lats, lons,
    tokens, coarse, output_cotangent, token_class, relative_index,
    encoder_gain, encoder_offset, encoder_projection, encoder_projection_bias,
    encoder_output_weight, encoder_output_bias, encoder_table,
    decoder_gain, decoder_offset, decoder_projection, decoder_projection_bias,
    decoder_output_weight, decoder_output_bias, decoder_table,
    split_weight, split_bias,
):
    def row(v):
        return v.reshape(1, -1)

    s = jax.ShapeDtypeStruct
    packed = call(
        pack_kernel,
        "pack",
        [
            jnp.transpose(tokens, (1, 2, 0, 3)),
            jnp.transpose(output_cotangent, (1, 2, 0, 3)),
            jnp.transpose(coarse, (1, 2, 0, 3)),
            jnp.transpose(token_class, (1, 0, 2)),
        ],
        [s((TILES, LEVELS, D), bf16)] * 4,
        [
            pltpu.VMEM((WIN_LAT, LEVELS, WIN_LON), jnp.int32),
            pltpu.VMEM((WIN_LAT, LEVELS, D), bf16),
            pltpu.SemaphoreType.DMA((4 * (2 * HL + 2 * COARSE_ROWS + 1),)),
            pltpu.SemaphoreType.DMA(()),
        ],
        100_000_000,
        [ANY] * 4,
        [ANY] * 4,
        60,
    )
    parts = exchange(packed, -1, lats, lons)
    biases = lookup(relative_index, encoder_table, decoder_table)
    is_last = (lax.axis_index("lat") == lats - 1).astype(jnp.int32).reshape(1)
    half = s((2 * PAIRS, LEVELS, D), bf16)
    quarter = s((PAIRS, LEVELS, D), bf16)
    points = 4 * LEVELS * POINTS
    outs = call(
        main_kernel,
        "main",
        [
            *parts, *biases, is_last,
            row(encoder_gain), row(encoder_offset), encoder_projection_bias, row(encoder_output_bias),
            row(decoder_gain), row(decoder_offset), decoder_projection_bias, row(decoder_output_bias),
            row(split_bias),
            encoder_projection, encoder_output_weight, decoder_projection, decoder_output_weight, split_weight,
        ],
        [half] * 4
        + [s((SPAN, D), bf16), s((SPAN, D), bf16), s((SPAN, 3 * D), bf16), s((HEADS * SPAN, WIDE), bf16)],
        [
            pltpu.VMEM((SPAN, D), f32),
            pltpu.VMEM((points, 2 * D), f32),
            pltpu.VMEM((points, 4 * D), f32),
            pltpu.VMEM((SPAN, 3 * D), bf16),
            pltpu.VMEM((HEADS * SPAN, WIDE), bf16),
            pltpu.VMEM((SPAN, 3 * D), bf16),
        ],
        5_000_000_000,
        [VM] * 6 + [pl.BlockSpec(memory_space=pltpu.SMEM)] + [VM] * 14,
    )
    home = exchange(outs[:4], 1, lats, lons)
    joined_grad, kept_tokens, qkv, probs = outs[4:]
    token_grads = call(
        encoder_back_kernel,
        "encoder_back",
        [joined_grad, kept_tokens, qkv, probs, row(encoder_gain), encoder_projection, encoder_output_weight],
        [quarter] * 4,
        [pltpu.VMEM((SPAN, D), f32), pltpu.VMEM((SPAN, 3 * D), bf16)],
        3_000_000_000,
    )
    home, token_grads = lax.optimization_barrier((home, token_grads))
    home_tokens = exchange(token_grads, 1, lats, lons)
    low_tokens = SPAN // 4
    coarse_gradient, decoded = call(
        coarse_kernel,
        "coarse_back",
        [home[3 - q] for q in range(4)] + [split_weight],
        [s((low_tokens // LEVELS, LEVELS, 2 * D), bf16), s((WIN_LAT, WIN_LON, LEVELS, D), bf16)],
        [
            pltpu.VMEM((low_tokens, 4 * D), f32),
            pltpu.VMEM((low_tokens, 2 * D), f32),
            pltpu.SemaphoreType.DMA((4 * HL,)),
        ],
        1_000_000,
        None,
        [VM, ANY],
    )
    coarse_gradient = jnp.transpose(
        coarse_gradient.reshape(WIN_LAT // 2, WIN_LON // 2, LEVELS, 2 * D), (2, 0, 1, 3)
    )

    def assemble(parts):
        parts = [p.reshape(HL, HN, LEVELS, D) for p in parts]
        upper = jnp.concatenate([parts[3], parts[2]], axis=1)
        lower = jnp.concatenate([parts[1], parts[0]], axis=1)
        return jnp.transpose(jnp.concatenate([upper, lower], axis=0), (2, 0, 1, 3))

    return jnp.transpose(decoded, (2, 0, 1, 3)), assemble(home_tokens), coarse_gradient


def solution(mesh):
    cut = P(None, "lat", "lon", None)
    in_specs = (cut, cut, cut, P(None, "lat", "lon")) + (P(),) * 17
    return jax.shard_map(
        functools.partial(per_device, mesh.shape["lat"], mesh.shape["lon"]),
        mesh=mesh,
        in_specs=in_specs,
        out_specs=(cut, cut, cut),
        check_vma=False,
    )
```

time: 275 us -> 70 us (0.25); the launches traced: 269 us -> 68.8 us
  local copies, waits for them, and re-layouts: 92.2 us -> 8.94 us
  matrix products: 78.1 us -> 0 us
  waiting for transfers between devices: 45.9 us -> 10.5 us
  Pallas kernels: 0 us -> 31.3 us
  other arithmetic: 24.3 us -> 2.59 us
  starting transfers between devices: 27.1 us -> 14.6 us
    dot_general x40 -> x0, matrix products: 78.1 us -> none  [the longest x18 31.2 us: one_block(): jnp.einsum('qke,he->hqk', selector, stacked_tables, precision=lax.Precisi...]
    ppermute x18 -> x9, waiting for transfers between devices: 45.9 us -> 10.5 us  [exchange(): lax.ppermute(pieces[q], ('lat', 'lon'), shift_pairs(qr * steps, qc * step...]
    pallas_call x0 -> x5, Pallas kernels: none -> 31.3 us  [the longest x4 24.8 us: call(): pl.pallas_call(kernel, out_shape=outs, in_specs=in_specs or [VM] * len(in...]
    reshape x33 -> x0, local copies, waits for them, and re-layouts: 24.7 us -> none  [the longest x4 4.17 us: project(): mixed.astype(jnp.bfloat16).reshape(values.shape[:-1] + (weight.shape[1],))]
    slice x23 -> x0, local copies, waits for them, and re-layouts: 18.6 us -> none  [the longest x4 4.25 us: settle(): from_right = shifted(region[:, :, breadth - half_lon:], 'lon', 1)]
    dynamic_update_slice x18 -> x0, local copies, waits for them, and re-layouts: 13.9 us -> none  [lookup_biases(): lax.map(one_block, relative_index.reshape(span // block_rows, block_rows,...]
    eq x18 -> x0, local copies, waits for them, and re-layouts: 12.6 us -> none  [one_block(): rows[:, :, None] == entry_ids[None, None, :]]
    ppermute x18 -> x9, starting transfers between devices: 27.1 us -> 14.6 us  [exchange(): lax.ppermute(pieces[q], ('lat', 'lon'), shift_pairs(qr * steps, qc * step...]
  transfers between devices with their start and end apart: 18 -> 9, of which waited for: 11 -> 4; matrix products, arithmetic and copies ran while one was open for 38% -> 2% of each run, Pallas kernels for 0% -> 16%
where the time goes in v1:
time: 70 us; the launch traced here: 68.8 us
  Pallas kernels  31.3 us (45%)
  starting transfers between devices  14.6 us (21%)
  waiting for transfers between devices  10.5 us (15%)
  local copies, waits for them, and re-layouts  8.94 us (13%)
  other arithmetic  2.59 us (4%)
  between operations  0.9 us (1%)
    pallas_call x4, Pallas kernels, call(): pl.pallas_call(kernel, out_shape=outs, in_specs=in_specs or [VM] * len(in...  24.8 us
    ppermute x9, starting transfers between devices, exchange(): lax.ppermute(pieces[q], ('lat', 'lon'), shift_pairs(qr * steps, qc * step...  14.6 us
    ppermute x9, waiting for transfers between devices, exchange(): lax.ppermute(pieces[q], ('lat', 'lon'), shift_pairs(qr * steps, qc * step...  10.5 us
    unnamed x40, local copies, waits for them, and re-layouts  8.94 us
    pallas_call x1, Pallas kernels, lookup(): pl.pallas_call(lookup_kernel, out_shape=[jax.ShapeDtypeStruct((2 * HEADS...  6.46 us
  transfers between devices with their start and end apart: 9, of which 4 were waited for; matrix products, arithmetic and copies ran while one was open for 2% of the time, Pallas kernels for 16%

profile of v1, /device:TPU:24, one launch (start us, length us, event | category | flops | bytes accessed | tf_op | source)
XLA Modules:
  0.0 68.8 jit_solution(4576309082162027174)
XLA Ops:
  0.6 13.4 %pack.1 = (bf16[51,2,512]{2,1,0:T(2,128)(2,1)}, bf16[51,2,512]{2,1,0:T(2,128)(2,1)}, bf16[51,2,512]{2,1,0:T(2,128)(2,1)}, bf16[51,2,512]{2,1,0:T(2,128)(2,1)}) custom-call(bf16[6,12,2,512]{3,2,1,0:T(2,128)(2,1)} %bitcast.31, bf16[6,12,2,512]{3,2,1,0:T(2,128)(2,1)} %bitcast.32, bf16[3,6,2,1024]{3,2,1,0:T(2,128)(2,1)} %bitcast.33, s32[6,2,12]{2,1,0:T(2,128)} %bitcast.37), custom_call_target="tpu_custom_call" | custom-call | flops 100000000 | bytes 100000 | tf_op jit(solution)/shard_map/pack/pallas_call | solution.py:390
  14.1 7.8 %collective-permute-start = (bf16[51,2,512]{2,1,0:T(2,128)(2,1)}, bf16[51,2,512]{2,1,0:T(2,128)(2,1)S(1)}, u32[]{:S(2)}, u32[]{:S(2)}) collective-permute-start(bf16[51,2,512]{2,1,0:T(2,128)(2,1)} %get-tuple-element.32), channel_id=1, source_target_pairs={{0,31},{1,0},{2,1},{3,2},{4,3},{5,4},{6,5},{7,6},{8,7},{9,8},{10,9... | collective-permute-start | bytes 313352 | tf_op jit(solution)/shard_map/ppermute | solution.py:412
  21.9 0.7 %collective-permute-start.1 = (bf16[51,2,512]{2,1,0:T(2,128)(2,1)}, bf16[51,2,512]{2,1,0:T(2,128)(2,1)S(1)}, u32[]{:S(2)}, u32[]{:S(2)}) collective-permute-start(bf16[51,2,512]{2,1,0:T(2,128)(2,1)} %get-tuple-element.33), channel_id=1, source_target_pairs={{0,224},{1,225},{2,226},{3,227},{4,228},{5,229},{6,230},{7,231},{8... | collective-permute-start | bytes 313352 | tf_op jit(solution)/shard_map/ppermute | solution.py:412
  22.9 0.9 %convert_element_type.9 = f32[144,144]{1,0:T(8,128)S(1)} convert(s32[144,144]{1,0:T(8,128)} %param.25) | non-fusion elementwise | flops 20736 | bytes 165888 | tf_op jit(solution)/shard_map/convert_element_type | solution.py:277
  23.9 0.8 %select_maximum_fusion.inputs_ref = f32[160,768]{1,0:T(8,128)S(1)} fusion(f32[8,759]{1,0:T(8,128)} %param.39, f32[8,759]{1,0:T(8,128)} %param.32, f32[144,144]{1,0:T(8,128)S(1)} %convert_element_type.9), kind=kLoop, calls=%fused_computation.2 | loop fusion | flops 1228800 | bytes 623040 | tf_op jit(solution)/shard_map/concatenate | solution.py:277
  24.8 6.5 %lookup.1 = (f32[2304,128]{1,0:T(8,128)S(1)}, f32[2304,128]{1,0:T(8,128)S(1)}) custom-call(f32[160,768]{1,0:T(8,128)S(1)} %select_maximum_fusion.inputs_ref), custom_call_target="tpu_custom_call" | custom-call | flops 3000000000 | bytes 4000000 | tf_op jit(solution)/shard_map/lookup/pallas_call | solution.py:278
  31.3 1.0 %copy-done.16 = f32[2304,128]{1,0:T(8,128)} copy-done((f32[2304,128]{1,0:T(8,128)}, f32[2304,128]{1,0:T(8,128)S(1)}, u32[]{:S(2)}) %copy-start.16) | copy-done | bytes 1179672
  32.3 1.0 %copy-done.18 = f32[2304,128]{1,0:T(8,128)} copy-done((f32[2304,128]{1,0:T(8,128)}, f32[2304,128]{1,0:T(8,128)S(1)}, u32[]{:S(2)}) %copy-start.18) | copy-done | bytes 1179672
  33.5 2.2 %copy-done = bf16[1024,2048]{1,0:T(8,128)(2,1)S(1)} copy-done((bf16[1024,2048]{1,0:T(8,128)(2,1)S(1)}, bf16[1024,2048]{1,0:T(8,128)(2,1)}, u32[]{:S(2)}) %copy-start) | copy-done | bytes 4194328
  35.7 1.0 %copy-done.3 = bf16[512,512]{1,0:T(8,128)(2,1)S(1)} copy-done((bf16[512,512]{1,0:T(8,128)(2,1)S(1)}, bf16[512,512]{1,0:T(8,128)(2,1)}, u32[]{:S(2)}) %copy-start.3) | copy-done | bytes 524312
  36.7 1.0 %copy-done.4 = bf16[512,512]{1,0:T(8,128)(2,1)S(1)} copy-done((bf16[512,512]{1,0:T(8,128)(2,1)S(1)}, bf16[512,512]{1,0:T(8,128)(2,1)}, u32[]{:S(2)}) %copy-start.4) | copy-done | bytes 524312
  37.7 1.3 %copy-done.17 = f32[2304,128]{1,0:T(8,128)S(1)} copy-done((f32[2304,128]{1,0:T(8,128)S(1)}, f32[2304,128]{1,0:T(8,128)}, u32[]{:S(2)}) %copy-start.17) | copy-done | bytes 1179672
  39.0 1.3 %copy-done.19 = f32[2304,128]{1,0:T(8,128)S(1)} copy-done((f32[2304,128]{1,0:T(8,128)S(1)}, f32[2304,128]{1,0:T(8,128)}, u32[]{:S(2)}) %copy-start.19) | copy-done | bytes 1179672
  40.3 7.1 %main.1 = (bf16[36,2,512]{2,1,0:T(2,128)(2,1)S(1)}, bf16[36,2,512]{2,1,0:T(2,128)(2,1)S(1)}, bf16[36,2,512]{2,1,0:T(2,128)(2,1)S(1)}, bf16[36,2,512]{2,1,0:T(2,1...) custom-call(bf16[51,2,512]{2,1,0:T(2,128)(2,1)S(1)} %copy-done.6, ...), custom_call_target="tpu_custom_call" | custom-call | flops 5000000000 | bytes 5000000 | tf_op jit(solution)/shard_map/main/pallas_call | solution.py:390
  47.7 3.7 %collective-permute-start.4 = (bf16[36,2,512]{2,1,0:T(2,128)(2,1)S(1)}, bf16[36,2,512]{2,1,0:T(2,128)(2,1)S(1)}, u32[]{:S(2)}, u32[]{:S(2)}) collective-permute-start(bf16[36,2,512]{2,1,0:T(2,128)(2,1)S(1)} %get-tuple-element.39), channel_id=1, source_target_pairs={{0,32},{1,33},{2,34},{3,35},{4,36},{5,37},{6,38},{7,39},{8,40},{9,... | collective-permute-start | bytes 221192 | tf_op jit(solution)/shard_map/ppermute | solution.py:412
  51.4 0.7 %collective-permute-start.5 = (bf16[36,2,512]{2,1,0:T(2,128)(2,1)S(1)}, bf16[36,2,512]{2,1,0:T(2,128)(2,1)S(1)}, u32[]{:S(2)}, u32[]{:S(2)}) collective-permute-start(bf16[36,2,512]{2,1,0:T(2,128)(2,1)S(1)} %get-tuple-element.40), channel_id=1, source_target_pairs={{0,33},{1,34},{2,35},{3,36},{4,37},{5,38},{6,39},{7,40},{8,41},{9,... | collective-permute-start | bytes 221192 | tf_op jit(solution)/shard_map/ppermute | solution.py:412
  52.1 2.1 %encoder_back.1 = (bf16[18,2,512]{2,1,0:T(2,128)(2,1)S(1)}, bf16[18,2,512]{2,1,0:T(2,128)(2,1)S(1)}, bf16[18,2,512]{2,1,0:T(2,128)(2,1)S(1)}, bf16[18,2,512]{2,1,0:T(2,128)(2,1)S(1)}) custom-call(bf16[144,512]{1,0:T(8,128)(2,1)S(1)} %get-tuple-element.41.grad, bf16[144,512]{1,0:T(8,128)(2,1)S(1)} %get-tuple-element.42.tokens, ...), custom_call_target="tpu_custom_call" | custom-call | flops 3000000000 | bytes 3000000 | tf_op jit(solution)/shard_map/encoder_back/pallas_call | solution.py:390
  54.2 0.7 collective-permute-done.3.j2
  54.9 4.8 %collective-permute-done.5.j0 = bf16[36,2,512]{2,1,0:T(2,128)(2,1)S(1)} collective-permute-done((bf16[36,2,512]{2,1,0:T(2,128)(2,1)S(1)}, bf16[36,2,512]{2,1,0:T(2,128)(2,1)S(1)}, u32[]{:S(2)}, u32[]{:S(2)}) %collective-permute-start.5) | collective-permute-done | bytes 73760 | tf_op jit(solution)/shard_map/ppermute | solution.py:412
  59.7 1.0 %collective-permute-start.7 = (bf16[18,2,512]{2,1,0:T(2,128)(2,1)S(1)}, bf16[18,2,512]{2,1,0:T(2,128)(2,1)S(1)}, u32[]{:S(2)}, u32[]{:S(2)}) collective-permute-start(bf16[18,2,512]{2,1,0:T(2,128)(2,1)S(1)} %get-tuple-element.55), channel_id=1, source_target_pairs={{0,32},{1,33},{2,34},{3,35},{4,36},{5,37},{6,38},{7,39},{8,40},{9,... | collective-permute-start | bytes 110600 | tf_op jit(solution)/shard_map/ppermute | solution.py:412
  60.7 2.2 %coarse_back.1 = (bf16[18,2,1024]{2,1,0:T(2,128)(2,1)}, bf16[6,12,2,512]{3,2,1,0:T(2,128)(2,1)}) custom-call(bf16[36,2,512]{2,1,0:T(2,128)(2,1)S(1)} %collective-permute-done.5.j0, bf16[36,2,512]{2,1,0:T(2,128)(2,1)S(1)} %collective-permute-done.4.j1, bf16[36,2,512]{2,1,0:T(2,128)(2,1)S(1)} %collective-permute-done.3.j2, ...), custom_call_target="tpu_custom_call" | custom-call | flops 1000000 | bytes 1000 | tf_op jit(solution)/shard_map/coarse_back/pallas_call | solution.py:390
  62.9 4.7 %collective-permute-done.6 = bf16[18,2,512]{2,1,0:T(2,128)(2,1)S(1)} collective-permute-done((bf16[18,2,512]{2,1,0:T(2,128)(2,1)S(1)}, bf16[18,2,512]{2,1,0:T(2,128)(2,1)S(1)}, u32[]{:S(2)}, u32[]{:S(2)}) %collective-permute-start.6) | collective-permute-done | bytes 36896 | tf_op jit(solution)/shard_map/ppermute | solution.py:412
  67.6 0.4 collective-permute-done.8
  68.0 0.9 %maximum_bitcast_fusion = bf16[2,6,12,512]{3,0,2,1:T(2,128)(2,1)} fusion(bf16[3,6,2,512]{3,2,1,0:T(2,128)(2,1)S(1)} %bitcast.22, bf16[3,6,2,512]{3,2,1,0:T(2,128)(2,1)S(1)} %bitcast.36, bf16[3,6,2,512]{3,2,1,0:T(2,128)(2,1)S(1)} %bitcast.35, bf16[3,6,2,512]{3,2,1,0:T(2,128)(2,1)S(1)} %bitcast.34), kind=kLoop, calls=%fused_computation.7 | loop fusion | flops 221184 | bytes 294912 | tf_op jit(solution)/shard_map/transpose | solution.py:514
  (42 shorter events, 0.8 us)
Async XLA Ops:
  14.1 19.3 %collective-permute-start = (bf16[51,2,512]{2,1,0:T(2,128)(2,1)}, bf16[51,2,512]{2,1,0:T(2,128)(2,1)S(1)}, u32[]{:S(2)}, u32[]{:S(2)}) collective-permute-start(bf16[51,2,512]{2,1,0:T(2,128)(2,1)} %get-tuple-element.32), channel_id=1, source_target_pairs={{0,31},{1,0},{2,1},{3,2},{4,3},{5,4},{6,5},{7,6},{8,7},{9,8},{10,9... | collective-permute-start | bytes 313352 | tf_op jit(solution)/shard_map/ppermute | solution.py:412
  21.9 11.4 %collective-permute-start.1 = (bf16[51,2,512]{2,1,0:T(2,128)(2,1)}, bf16[51,2,512]{2,1,0:T(2,128)(2,1)S(1)}, u32[]{:S(2)}, u32[]{:S(2)}) collective-permute-start(bf16[51,2,512]{2,1,0:T(2,128)(2,1)} %get-tuple-element.33), channel_id=1, source_target_pairs={{0,224},{1,225},{2,226},{3,227},{4,228},{5,229},{6,230},{7,231},{8... | collective-permute-start | bytes 313352 | tf_op jit(solution)/shard_map/ppermute | solution.py:412
  22.6 10.7 %collective-permute-start.2 = (bf16[51,2,512]{2,1,0:T(2,128)(2,1)}, bf16[51,2,512]{2,1,0:T(2,128)(2,1)}, u32[]{:S(2)}, u32[]{:S(2)}) collective-permute-start(bf16[51,2,512]{2,1,0:T(2,128)(2,1)} %get-tuple-element.34), channel_id=1, source_target_pairs={{0,255},{1,224},{2,225},{3,226},{4,227},{5,228},{6,229},{7,230},{8... | collective-permute-start | bytes 313352 | tf_op jit(solution)/shard_map/ppermute | solution.py:412
  24.6 8.7 %copy-start.1 = (bf16[512,1536]{1,0:T(8,128)(2,1)S(1)}, bf16[512,1536]{1,0:T(8,128)(2,1)}, u32[]{:S(2)}) copy-start(bf16[512,1536]{1,0:T(8,128)(2,1)} %d_weight.1) | copy-start | bytes 4718596
  24.7 8.7 %copy-start.2 = (bf16[512,1536]{1,0:T(8,128)(2,1)S(1)}, bf16[512,1536]{1,0:T(8,128)(2,1)}, u32[]{:S(2)}) copy-start(bf16[512,1536]{1,0:T(8,128)(2,1)} %weight.1) | copy-start | bytes 4718596
  24.7 8.7 %copy-start.6 = (bf16[51,2,512]{2,1,0:T(2,128)(2,1)S(1)}, bf16[51,2,512]{2,1,0:T(2,128)(2,1)}, u32[]{:S(2)}) copy-start(bf16[51,2,512]{2,1,0:T(2,128)(2,1)} %get-tuple-element.31.b0) | copy-start | bytes 313348
  24.7 8.7 %copy-start.7 = (f32[1536]{0:T(1024)S(1)}, f32[1536]{0:T(1024)}, u32[]{:S(2)}) copy-start(f32[1536]{0:T(1024)} %e_bias.1) | copy-start | bytes 18436
  24.7 8.7 %copy-start.8 = (f32[1536]{0:T(1024)S(1)}, f32[1536]{0:T(1024)}, u32[]{:S(2)}) copy-start(f32[1536]{0:T(1024)} %d_bias.1) | copy-start | bytes 18436
  24.7 8.7 %copy-start.9 = (f32[2048]{0:T(1024)S(1)}, f32[2048]{0:T(1024)}, u32[]{:S(2)}) copy-start(f32[2048]{0:T(1024)} %param.41) | copy-start | bytes 24580
  24.7 8.7 %copy-start.10 = (f32[512]{0:T(512)S(1)}, f32[512]{0:T(512)}, u32[]{:S(2)}) copy-start(f32[512]{0:T(512)} %param.27) | copy-start | bytes 6148
  24.7 8.7 %copy-start.11 = (f32[512]{0:T(512)S(1)}, f32[512]{0:T(512)}, u32[]{:S(2)}) copy-start(f32[512]{0:T(512)} %param.31) | copy-start | bytes 6148
  24.7 8.7 %copy-start.12 = (f32[512]{0:T(512)S(1)}, f32[512]{0:T(512)}, u32[]{:S(2)}) copy-start(f32[512]{0:T(512)} %param.33) | copy-start | bytes 6148
  24.8 8.7 %copy-start.13 = (f32[512]{0:T(512)S(1)}, f32[512]{0:T(512)}, u32[]{:S(2)}) copy-start(f32[512]{0:T(512)} %param.34) | copy-start | bytes 6148
  24.8 8.7 %copy-start.14 = (f32[512]{0:T(512)S(1)}, f32[512]{0:T(512)}, u32[]{:S(2)}) copy-start(f32[512]{0:T(512)} %param.38) | copy-start | bytes 6148
  24.8 8.7 %copy-start.15 = (f32[512]{0:T(512)S(1)}, f32[512]{0:T(512)}, u32[]{:S(2)}) copy-start(f32[512]{0:T(512)} %param.26) | copy-start | bytes 6148
  33.5 2.2 %copy-start = (bf16[1024,2048]{1,0:T(8,128)(2,1)S(1)}, bf16[1024,2048]{1,0:T(8,128)(2,1)}, u32[]{:S(2)}) copy-start(bf16[1024,2048]{1,0:T(8,128)(2,1)} %split.3) | copy-start | bytes 12582916
  37.7 1.3 %copy-start.17 = (f32[2304,128]{1,0:T(8,128)S(1)}, f32[2304,128]{1,0:T(8,128)}, u32[]{:S(2)}) copy-start(f32[2304,128]{1,0:T(8,128)} %copy-done.16) | copy-start | bytes 3538948
  40.3 11.8 %copy-start.5 = (bf16[512,512]{1,0:T(8,128)(2,1)S(1)}, bf16[512,512]{1,0:T(8,128)(2,1)}, u32[]{:S(2)}) copy-start(bf16[512,512]{1,0:T(8,128)(2,1)} %out_weight.1) | copy-start | bytes 1572868
  47.4 7.6 %collective-permute-start.3 = (bf16[36,2,512]{2,1,0:T(2,128)(2,1)S(1)}, bf16[36,2,512]{2,1,0:T(2,128)(2,1)S(1)}, u32[]{:S(2)}, u32[]{:S(2)}) collective-permute-start(bf16[36,2,512]{2,1,0:T(2,128)(2,1)S(1)} %get-tuple-element.38), channel_id=1, source_target_pairs={{0,1},{1,2},{2,3},{3,4},{4,5},{5,6},{6,7},{7,8},{8,9},{9,10},{10,1... | collective-permute-start | bytes 221192 | tf_op jit(solution)/shard_map/ppermute | solution.py:412
  47.7 7.2 %collective-permute-start.4 = (bf16[36,2,512]{2,1,0:T(2,128)(2,1)S(1)}, bf16[36,2,512]{2,1,0:T(2,128)(2,1)S(1)}, u32[]{:S(2)}, u32[]{:S(2)}) collective-permute-start(bf16[36,2,512]{2,1,0:T(2,128)(2,1)S(1)} %get-tuple-element.39), channel_id=1, source_target_pairs={{0,32},{1,33},{2,34},{3,35},{4,36},{5,37},{6,38},{7,39},{8,40},{9,... | collective-permute-start | bytes 221192 | tf_op jit(solution)/shard_map/ppermute | solution.py:412
  51.4 8.3 %collective-permute-start.5 = (bf16[36,2,512]{2,1,0:T(2,128)(2,1)S(1)}, bf16[36,2,512]{2,1,0:T(2,128)(2,1)S(1)}, u32[]{:S(2)}, u32[]{:S(2)}) collective-permute-start(bf16[36,2,512]{2,1,0:T(2,128)(2,1)S(1)} %get-tuple-element.40), channel_id=1, source_target_pairs={{0,33},{1,34},{2,35},{3,36},{4,37},{5,38},{6,39},{7,40},{8,41},{9,... | collective-permute-start | bytes 221192 | tf_op jit(solution)/shard_map/ppermute | solution.py:412
  59.7 7.9 %collective-permute-start.6 = (bf16[18,2,512]{2,1,0:T(2,128)(2,1)S(1)}, bf16[18,2,512]{2,1,0:T(2,128)(2,1)S(1)}, u32[]{:S(2)}, u32[]{:S(2)}) collective-permute-start(bf16[18,2,512]{2,1,0:T(2,128)(2,1)S(1)} %get-tuple-element.54), channel_id=1, source_target_pairs={{0,33},{1,34},{2,35},{3,36},{4,37},{5,38},{6,39},{7,40},{8,41},{9,... | collective-permute-start | bytes 110600 | tf_op jit(solution)/shard_map/ppermute | solution.py:412
  59.7 7.9 %collective-permute-start.7 = (bf16[18,2,512]{2,1,0:T(2,128)(2,1)S(1)}, bf16[18,2,512]{2,1,0:T(2,128)(2,1)S(1)}, u32[]{:S(2)}, u32[]{:S(2)}) collective-permute-start(bf16[18,2,512]{2,1,0:T(2,128)(2,1)S(1)} %get-tuple-element.55), channel_id=1, source_target_pairs={{0,32},{1,33},{2,34},{3,35},{4,36},{5,37},{6,38},{7,39},{8,40},{9,... | collective-permute-start | bytes 110600 | tf_op jit(solution)/shard_map/ppermute | solution.py:412
  60.7 7.3 %collective-permute-start.8 = (bf16[18,2,512]{2,1,0:T(2,128)(2,1)S(1)}, bf16[18,2,512]{2,1,0:T(2,128)(2,1)S(1)}, u32[]{:S(2)}, u32[]{:S(2)}) collective-permute-start(bf16[18,2,512]{2,1,0:T(2,128)(2,1)S(1)} %get-tuple-element.56), channel_id=1, source_target_pairs={{0,1},{1,2},{2,3},{3,4},{4,5},{5,6},{6,7},{7,8},{8,9},{9,10},{10,1... | collective-permute-start | bytes 110600 | tf_op jit(solution)/shard_map/ppermute | solution.py:412
  (5 other events, 5.4 us)

commit v2 on v1

--- a/solution.py
+++ b/solution.py
@@ -79,7 +79,7 @@
     return total
 
 
-def mask_bias(refs, is_last):
+def mask_bias(refs, lats):
     token = lax.broadcasted_iota(jnp.int32, (1, WIDE), 1)
     quadrant, r, c, level = token_place(token)
     lane = HN * (1 - quadrant % 2) + c
@@ -87,7 +87,7 @@
     rows = jnp.concatenate([ref[CLASS_AT + r, :, :128].astype(f32) for ref in refs for r in range(HL)], axis=0)
     spread = dot(rows.astype(bf16), hot.astype(f32).astype(bf16))
     mine = lax.broadcasted_iota(jnp.int32, (4 * HL * LEVELS, WIDE), 0) == (quadrant * HL + r) * LEVELS + level
-    seam = (quadrant // 2).astype(f32) * is_last.astype(f32)
+    seam = jnp.where(lax.axis_index("lat") == lats - 1, (quadrant // 2).astype(f32), 0.0)
     label = 2.0 * jnp.sum(jnp.where(mine, spread, 0.0), axis=0, keepdims=True) + seam
     label = jnp.where(token < SPAN, label, 9.0)
     eye = lax.broadcasted_iota(jnp.int32, (SPAN, WIDE), 0) == lax.broadcasted_iota(jnp.int32, (SPAN, WIDE), 1)
@@ -162,37 +162,39 @@
 TILES = CLASS_AT + HL
 
 
-def pack_kernel(tokens, cotangent, coarse, classes, o0, o1, o2, o3, kinds, tiles, sems, first_sem):
-    outs = (o0, o1, o2, o3)
-    fetch = pltpu.make_async_copy(classes, kinds, first_sem)
-    fetch.start()
-    copies = []
-
-    def send(src, dst):
-        copy = pltpu.make_async_copy(src, dst, sems.at[len(copies)])
+def pack_kernel(
+    tokens_hbm, cotangent_hbm, coarse_hbm, classes_hbm, o0, o1, o2, o3,
+    tokens, cotangent, coarse, classes, buffers, in_sems, out_sems,
+):
+    arrivals = [
+        pltpu.make_async_copy(src, dst, in_sems.at[n])
+        for n, (src, dst) in enumerate(
+            ((tokens_hbm, tokens), (cotangent_hbm, cotangent), (coarse_hbm, coarse), (classes_hbm, classes))
+        )
+    ]
+    for copy in arrivals:
         copy.start()
-        copies.append(copy)
-
+    buffers[:, pl.ds(CLASS_AT, HL)] = jnp.zeros((4, HL, LEVELS, D), bf16)
+    for copy in arrivals:
+        copy.wait()
+    departures = []
     for q in (3, 2, 1, 0):
         qr, qc = divmod(q, 2)
         lat, lon = HL * (1 - qr), HN * (1 - qc)
-        low_lat = (coarse.shape[0] - COARSE_ROWS) * (1 - qr)
+        low_lat, low_lon = (coarse.shape[0] - COARSE_ROWS) * (1 - qr), COARSE_COLS * (1 - qc)
         for r in range(HL):
-            send(tokens.at[lat + r, pl.ds(lon, HN)], outs[q].at[pl.ds(r * HN, HN)])
-            send(cotangent.at[lat + r, pl.ds(lon, HN)], outs[q].at[pl.ds(COTANGENT_AT + r * HN, HN)])
+            buffers[q, pl.ds(r * HN, HN)] = tokens[lat + r, pl.ds(lon, HN)]
+            buffers[q, pl.ds(COTANGENT_AT + r * HN, HN)] = cotangent[lat + r, pl.ds(lon, HN)]
+            buffers[q, CLASS_AT + r, :, pl.ds(0, WIN_LON)] = classes[lat + r].astype(f32).astype(bf16)
         for r in range(COARSE_ROWS):
             for half in range(2):
-                send(
-                    coarse.at[low_lat + r, pl.ds(COARSE_COLS * (1 - qc), COARSE_COLS), :, pl.ds(D * half, D)],
-                    outs[q].at[pl.ds(COARSE_AT + POINTS * half + r * COARSE_COLS, COARSE_COLS)],
-                )
-    tiles[...] = jnp.zeros_like(tiles)
-    fetch.wait()
-    for r in range(WIN_LAT):
-        tiles[r, :, pl.ds(0, WIN_LON)] = kinds[r].astype(f32).astype(bf16)
-    for q in (3, 2, 1, 0):
-        send(tiles.at[pl.ds(HL * (1 - q // 2), HL)], outs[q].at[pl.ds(CLASS_AT, HL)])
-    for copy in copies:
+                buffers[q, pl.ds(COARSE_AT + POINTS * half + r * COARSE_COLS, COARSE_COLS)] = coarse[
+                    low_lat + r, pl.ds(low_lon, COARSE_COLS), :, pl.ds(D * half, D)
+                ]
+        copy = pltpu.make_async_copy(buffers.at[q], (o0, o1, o2, o3)[q], out_sems.at[q])
+        copy.start()
+        departures.append(copy)
+    for copy in departures:
         copy.wait()
 
 
@@ -253,10 +255,10 @@
                     half * HEADS : (half + 1) * HEADS, n * 128 : (n + 1) * 128
                 ]
 
-    @pl.loop(0, SPAN // 8)
+    @pl.loop(0, SPAN // 16)
     def _(step):
-        for n in range(4):
-            two_rows(8 * step + 2 * n)
+        for n in range(8):
+            two_rows(16 * step + 2 * n)
 
     for g in range(SPAN // rest):
         result = look(packed_low[pl.ds(g, 1), :], packed_high[pl.ds(g, 1), :])
@@ -291,46 +293,56 @@
     )(inputs)
 
 
-def main_kernel(
-    b0, b1, b2, b3, bias_main, bias_rest, is_last,
-    e_gain, e_offset, e_bias, e_out_bias, d_gain, d_offset, d_bias, d_out_bias, split_bias,
-    e_weight, e_out_weight, d_weight, d_out_weight, split,
-    o0, o1, o2, o3, joined_grad, tokens, e_qkv, e_probs,
-    scratch, coarse, fine, d_qkv, d_probs, dqkv,
-):
-    def bias_rows(h):
-        rows = pl.ds(h * SPAN, SPAN)
-        return jnp.concatenate([bias_main[rows, :], bias_rest[rows, :]], axis=1)
-
-    parts = (b0, b1, b2, b3)
-    gather_quadrants(parts, 0, scratch)
-    x = scratch[...]
-    tokens[...] = x.astype(bf16)
-    blank = mask_bias(parts, is_last[0])
-    encoded = block_forward(
-        x, blank, lambda h: bias_rows(h), e_gain[...], e_offset[...], e_weight,
-        e_bias[...].reshape(1, -1), e_out_weight[...], e_out_bias[...], e_qkv, e_probs,
-    ).astype(bf16)
-
-    for q, ref in enumerate(parts):
-        qr, qc = divmod(q, 2)
-        for r in range(COARSE_ROWS):
-            for c in range(COARSE_COLS):
-                at = (qr * COARSE_ROWS + r) * 2 * COARSE_COLS + qc * COARSE_COLS + c
-                for half in range(2):
-                    coarse[pl.ds(2 * at, 2), pl.ds(D * half, D)] = ref[
-                        COARSE_AT + POINTS * half + r * COARSE_COLS + c
-                    ].astype(f32)
-    lowres = coarse[...].astype(bf16)
-    fine[...] = dot(lowres, split[...]) + split_bias[...]
+def coarse_points(q):
+    qr, qc = divmod(q, 2)
+    return [
+        (qr * COARSE_ROWS + r) * 2 * COARSE_COLS + qc * COARSE_COLS + c
+        for r in range(COARSE_ROWS)
+        for c in range(COARSE_COLS)
+    ]
+
+
+def coarse_places():
+    places = []
     for q in range(4):
         qr, qc = divmod(q, 2)
         for r in range(HL):
             for c in range(HN):
                 row, column = qr * HL + r + HL % 2, qc * HN + c + HN % 2
                 at = (row // 2) * 2 * COARSE_COLS + column // 2
-                kind = (row % 2) * 2 + column % 2
-                scratch[pl.ds(2 * (q * PAIRS + r * HN + c), 2), :] = fine[pl.ds(2 * at, 2), pl.ds(kind * D, D)]
+                places.append((q * PAIRS + r * HN + c, at, (row % 2) * 2 + column % 2))
+    return places
+
+
+def main_kernel(
+    lats, b0, b1, b2, b3, bias_main, bias_rest,
+    e_gain, e_offset, e_bias, e_out_bias, d_gain, d_offset, d_bias, d_out_bias, split_bias,
+    e_weight, e_out_weight, d_weight, d_out_weight, split,
+    o0, o1, o2, o3,
+    scratch, coarse, fine, tokens, e_qkv, e_probs, d_qkv, d_probs, dqkv,
+):
+    def bias_rows(h):
+        rows = pl.ds(h * SPAN, SPAN)
+        return jnp.concatenate([bias_main[rows, :], bias_rest[rows, :]], axis=1)
+
+    parts = (b0, b1, b2, b3)
+    gather_quadrants(parts, 0, scratch)
+    x = scratch[...]
+    tokens[...] = x.astype(bf16)
+    blank = mask_bias(parts, lats)
+    encoded = block_forward(
+        x, blank, lambda h: bias_rows(h), e_gain[...], e_offset[...], e_weight,
+        e_bias[...].reshape(1, -1), e_out_weight[...], e_out_bias[...], e_qkv, e_probs,
+    ).astype(bf16)
+
+    for q, ref in enumerate(parts):
+        for n, at in enumerate(coarse_points(q)):
+            for half in range(2):
+                coarse[pl.ds(2 * at, 2), pl.ds(D * half, D)] = ref[COARSE_AT + POINTS * half + n].astype(f32)
+    lowres = coarse[...].astype(bf16)
+    fine[...] = dot(lowres, split[...]) + split_bias[...]
+    for t, at, kind in coarse_places():
+        scratch[pl.ds(2 * t, 2), :] = fine[pl.ds(2 * at, 2), pl.ds(kind * D, D)]
     x = (encoded.astype(f32) + scratch[...]).astype(bf16).astype(f32)
     decoded = block_forward(
         x, blank, lambda h: bias_rows(HEADS + h), d_gain[...], d_offset[...], d_weight,
@@ -342,40 +354,46 @@
     gather_quadrants(parts, COTANGENT_AT, scratch)
     grad = scratch[...].astype(bf16)
     dx = block_backward(grad, x, d_gain[...], d_weight[...], d_out_weight[...], d_qkv, d_probs, dqkv)
+    grad = dx.astype(bf16)
+
     scratch[...] = dx
-    joined_grad[...] = dx.astype(bf16)
+    fine[...] = jnp.zeros_like(fine)
+    for t, at, kind in coarse_places():
+        fine[pl.ds(2 * at, 2), pl.ds(kind * D, D)] = scratch[pl.ds(2 * t, 2), :]
+    coarse[...] = dot_nt(fine[...].astype(bf16), split[...])
+    for q, ref in enumerate(outs):
+        for n, at in enumerate(coarse_points(q)):
+            for half in range(2):
+                ref[COARSE_AT + POINTS * half + n] = coarse[pl.ds(2 * at, 2), pl.ds(D * half, D)].astype(bf16)
+
+    scratch[...] = block_backward(
+        grad, tokens[...].astype(f32), e_gain[...], e_weight[...], e_out_weight[...], e_qkv, e_probs, dqkv
+    )
     scatter_quadrants(scratch, outs, PAIRS)
 
 
-def encoder_back_kernel(grad, tokens, qkv, probs, gain, weight, out_weight, t0, t1, t2, t3, scratch, dqkv):
-    x = tokens[...].astype(f32)
-    scratch[...] = block_backward(grad[...], x, gain[...], weight[...], out_weight[...], qkv, probs, dqkv)
-    scatter_quadrants(scratch, (t0, t1, t2, t3), 0)
-
-
-def coarse_kernel(j0, j1, j2, j3, split, out, decoded, fine, result, sems):
+def home_kernel(h0, h1, h2, h3, decoded, tokens_gradient, coarse_gradient, sems):
     copies = []
-    for q, ref in enumerate((j0, j1, j2, j3)):
-        for r in range(HL):
-            copy = pltpu.make_async_copy(
-                ref.at[pl.ds(r * HN, HN)],
-                decoded.at[q // 2 * HL + r, pl.ds(q % 2 * HN, HN)],
-                sems.at[len(copies)],
-            )
-            copy.start()
-            copies.append(copy)
-    columns = WIN_LON // 2
-    for q, ref in enumerate((j0, j1, j2, j3)):
-        qr, qc = divmod(q, 2)
-        for r in range(HL):
-            for c in range(HN):
-                row, column = qr * HL + r, qc * HN + c
-                at = (row // 2) * columns + column // 2
-                kind = (row % 2) * 2 + column % 2
-                fine[pl.ds(2 * at, 2), pl.ds(kind * D, D)] = ref[PAIRS + r * HN + c].astype(f32)
-    result[...] = dot_nt(fine[...].astype(bf16), split[...])
-    for t in range(out.shape[0]):
-        out[t] = result[pl.ds(2 * t, 2), :].astype(bf16)
+    for q, ref in enumerate((h0, h1, h2, h3)):
+        for n, out in enumerate((decoded, tokens_gradient)):
+            for r in range(HL):
+                copy = pltpu.make_async_copy(
+                    ref.at[pl.ds(PAIRS * n + r * HN, HN)],
+                    out.at[q // 2 * HL + r, pl.ds(q % 2 * HN, HN)],
+                    sems.at[len(copies)],
+                )
+                copy.start()
+                copies.append(copy)
+    for qc, (upper, lower) in enumerate(((h0, h2), (h1, h3))):
+        for half in range(2):
+            for c in range(COARSE_COLS):
+                at = COARSE_AT + POINTS * half + c
+                lanes = pl.ds(D * half, D)
+                column = qc * COARSE_COLS + c
+                coarse_gradient[0, column, :, lanes] = upper[at]
+                both = upper[at + COARSE_COLS].astype(f32) + lower[at].astype(f32)
+                coarse_gradient[1, column, :, lanes] = both.astype(bf16)
+                coarse_gradient[2, column, :, lanes] = lower[at + COARSE_COLS]
     for copy in copies:
         copy.wait()
 
@@ -437,10 +455,13 @@
         ],
         [s((TILES, LEVELS, D), bf16)] * 4,
         [
+            pltpu.VMEM((WIN_LAT, WIN_LON, LEVELS, D), bf16),
+            pltpu.VMEM((WIN_LAT, WIN_LON, LEVELS, D), bf16),
+            pltpu.VMEM((WIN_LAT // 2, WIN_LON // 2, LEVELS, 2 * D), bf16),
             pltpu.VMEM((WIN_LAT, LEVELS, WIN_LON), jnp.int32),
-            pltpu.VMEM((WIN_LAT, LEVELS, D), bf16),
-            pltpu.SemaphoreType.DMA((4 * (2 * HL + 2 * COARSE_ROWS + 1),)),
-            pltpu.SemaphoreType.DMA(()),
+            pltpu.VMEM((4, TILES, LEVELS, D), bf16),
+            pltpu.SemaphoreType.DMA((4,)),
+            pltpu.SemaphoreType.DMA((4,)),
         ],
         100_000_000,
         [ANY] * 4,
@@ -449,71 +470,45 @@
     )
     parts = exchange(packed, -1, lats, lons)
     biases = lookup(relative_index, encoder_table, decoder_table)
-    is_last = (lax.axis_index("lat") == lats - 1).astype(jnp.int32).reshape(1)
-    half = s((2 * PAIRS, LEVELS, D), bf16)
-    quarter = s((PAIRS, LEVELS, D), bf16)
     points = 4 * LEVELS * POINTS
     outs = call(
-        main_kernel,
+        functools.partial(main_kernel, lats),
         "main",
         [
-            *parts, *biases, is_last,
+            *parts, *biases,
             row(encoder_gain), row(encoder_offset), encoder_projection_bias, row(encoder_output_bias),
             row(decoder_gain), row(decoder_offset), decoder_projection_bias, row(decoder_output_bias),
             row(split_bias),
             encoder_projection, encoder_output_weight, decoder_projection, decoder_output_weight, split_weight,
         ],
-        [half] * 4
-        + [s((SPAN, D), bf16), s((SPAN, D), bf16), s((SPAN, 3 * D), bf16), s((HEADS * SPAN, WIDE), bf16)],
+        [s((CLASS_AT, LEVELS, D), bf16)] * 4,
         [
             pltpu.VMEM((SPAN, D), f32),
             pltpu.VMEM((points, 2 * D), f32),
             pltpu.VMEM((points, 4 * D), f32),
+            pltpu.VMEM((SPAN, D), bf16),
+            pltpu.VMEM((SPAN, 3 * D), bf16),
+            pltpu.VMEM((HEADS * SPAN, WIDE), bf16),
             pltpu.VMEM((SPAN, 3 * D), bf16),
             pltpu.VMEM((HEADS * SPAN, WIDE), bf16),
             pltpu.VMEM((SPAN, 3 * D), bf16),
         ],
-        5_000_000_000,
-        [VM] * 6 + [pl.BlockSpec(memory_space=pltpu.SMEM)] + [VM] * 14,
-    )
-    home = exchange(outs[:4], 1, lats, lons)
-    joined_grad, kept_tokens, qkv, probs = outs[4:]
-    token_grads = call(
-        encoder_back_kernel,
-        "encoder_back",
-        [joined_grad, kept_tokens, qkv, probs, row(encoder_gain), encoder_projection, encoder_output_weight],
-        [quarter] * 4,
-        [pltpu.VMEM((SPAN, D), f32), pltpu.VMEM((SPAN, 3 * D), bf16)],
-        3_000_000_000,
-    )
-    home, token_grads = lax.optimization_barrier((home, token_grads))
-    home_tokens = exchange(token_grads, 1, lats, lons)
-    low_tokens = SPAN // 4
-    coarse_gradient, decoded = call(
-        coarse_kernel,
-        "coarse_back",
-        [home[3 - q] for q in range(4)] + [split_weight],
-        [s((low_tokens // LEVELS, LEVELS, 2 * D), bf16), s((WIN_LAT, WIN_LON, LEVELS, D), bf16)],
-        [
-            pltpu.VMEM((low_tokens, 4 * D), f32),
-            pltpu.VMEM((low_tokens, 2 * D), f32),
-            pltpu.SemaphoreType.DMA((4 * HL,)),
-        ],
+        8_000_000_000,
+    )
+    home = exchange(outs, 1, lats, lons)
+    grid = s((WIN_LAT, WIN_LON, LEVELS, D), bf16)
+    low = s((WIN_LAT // 2, WIN_LON // 2, LEVELS, 2 * D), bf16)
+    results = call(
+        home_kernel,
+        "home",
+        [home[3 - q] for q in range(4)],
+        [grid, grid, low],
+        [pltpu.SemaphoreType.DMA((4 * 2 * HL,))],
         1_000_000,
         None,
-        [VM, ANY],
-    )
-    coarse_gradient = jnp.transpose(
-        coarse_gradient.reshape(WIN_LAT // 2, WIN_LON // 2, LEVELS, 2 * D), (2, 0, 1, 3)
-    )
-
-    def assemble(parts):
-        parts = [p.reshape(HL, HN, LEVELS, D) for p in parts]
-        upper = jnp.concatenate([parts[3], parts[2]], axis=1)
-        lower = jnp.concatenate([parts[1], parts[0]], axis=1)
-        return jnp.transpose(jnp.concatenate([upper, lower], axis=0), (2, 0, 1, 3))
-
-    return jnp.transpose(decoded, (2, 0, 1, 3)), assemble(home_tokens), coarse_gradient
+        [ANY, ANY, VM],
+    )
+    return tuple(jnp.transpose(r, (2, 0, 1, 3)) for r in results)
 
 
 def solution(mesh):

time: 70 us -> 42.1 us (0.60); the launches traced: 68.8 us -> 41.9 us
  Pallas kernels: 31.3 us -> 17.8 us
  local copies, waits for them, and re-layouts: 8.94 us -> 0.09 us
  waiting for transfers between devices: 10.5 us -> 7.87 us
  starting transfers between devices: 14.6 us -> 13.6 us
  other arithmetic: 2.59 us -> 1.71 us
    pallas_call x4 -> x3, Pallas kernels: 24.8 us -> 12.8 us  [call(): pl.pallas_call(kernel, out_shape=outs, in_specs=in_specs or [VM] * len(in...]
    unnamed x40 -> x30, local copies, waits for them, and re-layouts: 8.94 us -> 0.09 us
    ppermute x9 -> x6, waiting for transfers between devices: 10.5 us -> 7.87 us  [exchange(): lax.ppermute(pieces[q], ('lat', 'lon'), shift_pairs(qr * steps, qc * step...]
    pallas_call x1, Pallas kernels: 6.46 us -> 4.96 us  [lookup(): pl.pallas_call(lookup_kernel, out_shape=[jax.ShapeDtypeStruct((2 * HEADS...]
    ppermute x9 -> x6, starting transfers between devices: 14.6 us -> 13.6 us  [exchange(): lax.ppermute(pieces[q], ('lat', 'lon'), shift_pairs(qr * steps, qc * step...]
    transpose x1 -> x0, other arithmetic: 0.87 us -> none  [assemble(): return jnp.transpose(jnp.concatenate([upper, lower], axis=0), (2, 0, 1, 3))]
  transfers between devices with their start and end apart: 9 -> 6, of which waited for: 4 -> 4; matrix products, arithmetic and copies ran while one was open for 2% -> 4% of each run, Pallas kernels for 16% -> 12%
where the time goes in v2:
time: 42.1 us; the launch traced here: 41.9 us
  Pallas kernels  17.8 us (42%)
  starting transfers between devices  13.6 us (32%)
  waiting for transfers between devices  7.87 us (19%)
  other arithmetic  1.71 us (4%)
  between operations  0.89 us (2%)
    ppermute x6, starting transfers between devices, exchange(): lax.ppermute(pieces[q], ('lat', 'lon'), shift_pairs(qr * steps, qc * step...  13.6 us
    pallas_call x3, Pallas kernels, call(): pl.pallas_call(kernel, out_shape=outs, in_specs=in_specs or [VM] * len(in...  12.8 us
    ppermute x6, waiting for transfers between devices, exchange(): lax.ppermute(pieces[q], ('lat', 'lon'), shift_pairs(qr * steps, qc * step...  7.87 us
    pallas_call x1, Pallas kernels, lookup(): pl.pallas_call(lookup_kernel, out_shape=[jax.ShapeDtypeStruct((2 * HEADS...  4.96 us
    convert_element_type x1, other arithmetic, lookup(): relative_index.astype(f32)  0.92 us
  transfers between devices with their start and end apart: 6, of which 4 were waited for; matrix products, arithmetic and copies ran while one was open for 4% of the time, Pallas kernels for 12%

profile of v2, /device:TPU:24, one launch (start us, length us, event | category | flops | bytes accessed | tf_op | source)
XLA Modules:
  0.0 41.9 jit_solution(996211656660110429)
XLA Ops:
  0.6 1.9 %pack.1 = (bf16[51,2,512]{2,1,0:T(2,128)(2,1)}, bf16[51,2,512]{2,1,0:T(2,128)(2,1)}, bf16[51,2,512]{2,1,0:T(2,128)(2,1)}, bf16[51,2,512]{2,1,0:T(2,128)(2,1)}) custom-call(bf16[6,12,2,512]{3,2,1,0:T(2,128)(2,1)} %bitcast.21, bf16[6,12,2,512]{3,2,1,0:T(2,128)(2,1)} %bitcast.22, bf16[3,6,2,1024]{3,2,1,0:T(2,128)(2,1)} %bitcast.23, s32[6,2,12]{2,1,0:T(2,128)} %bitcast.24), custom_call_target="tpu_custom_call" | custom-call | flops 100000000 | bytes 100000 | tf_op jit(solution)/shard_map/pack/pallas_call | solution.py:408
  2.5 7.8 %collective-permute-start = (bf16[51,2,512]{2,1,0:T(2,128)(2,1)}, bf16[51,2,512]{2,1,0:T(2,128)(2,1)S(1)}, u32[]{:S(2)}, u32[]{:S(2)}) collective-permute-start(bf16[51,2,512]{2,1,0:T(2,128)(2,1)} %get-tuple-element.17), channel_id=1, source_target_pairs={{0,31},{1,0},{2,1},{3,2},{4,3},{5,4},{6,5},{7,6},{8,7},{9,8},{10,9... | collective-permute-start | bytes 313352 | tf_op jit(solution)/shard_map/ppermute | solution.py:430
  10.3 0.7 %collective-permute-start.1 = (bf16[51,2,512]{2,1,0:T(2,128)(2,1)}, bf16[51,2,512]{2,1,0:T(2,128)(2,1)S(1)}, u32[]{:S(2)}, u32[]{:S(2)}) collective-permute-start(bf16[51,2,512]{2,1,0:T(2,128)(2,1)} %get-tuple-element.18), channel_id=1, source_target_pairs={{0,224},{1,225},{2,226},{3,227},{4,228},{5,229},{6,230},{7,231},{8... | collective-permute-start | bytes 313352 | tf_op jit(solution)/shard_map/ppermute | solution.py:430
  11.1 0.3 collective-permute-start.2
  11.4 0.9 %convert_element_type.8 = f32[144,144]{1,0:T(8,128)S(1)} convert(s32[144,144]{1,0:T(8,128)} %param.25) | non-fusion elementwise | flops 20736 | bytes 165888 | tf_op jit(solution)/shard_map/convert_element_type | solution.py:279
  12.3 0.8 %select_maximum_fusion.inputs_ref = f32[160,768]{1,0:T(8,128)S(1)} fusion(f32[8,759]{1,0:T(8,128)} %param.39, f32[8,759]{1,0:T(8,128)} %param.32, f32[144,144]{1,0:T(8,128)S(1)} %convert_element_type.8), kind=kLoop, calls=%fused_computation.2 | loop fusion | flops 1228800 | bytes 623040 | tf_op jit(solution)/shard_map/concatenate | solution.py:279
  13.1 0.0 copy-start.2
  13.1 0.0 copy-start.3
  13.1 0.0 copy-start.6
  13.2 0.0 copy-start.7
  13.2 0.0 copy-start.10
  13.2 0.0 copy-start.11
  13.2 0.0 copy-start.13
  13.2 0.0 copy-start.14
  13.3 5.0 %lookup.1 = (f32[2304,128]{1,0:T(8,128)S(1)}, f32[2304,128]{1,0:T(8,128)S(1)}) custom-call(f32[160,768]{1,0:T(8,128)S(1)} %select_maximum_fusion.inputs_ref), custom_call_target="tpu_custom_call" | custom-call | flops 3000000000 | bytes 4000000 | tf_op jit(solution)/shard_map/lookup/pallas_call | solution.py:280
  18.2 0.0 collective-permute-done.1.b2
  18.3 0.2 collective-permute-done.2.b3
  18.6 9.4 %main.1 = (bf16[48,2,512]{2,1,0:T(2,128)(2,1)S(1)}, bf16[48,2,512]{2,1,0:T(2,128)(2,1)S(1)}, bf16[48,2,512]{2,1,0:T(2,128)(2,1)S(1)}, bf16[48,2,512]{2,1,0:T(2,128)(2,1)S(1)}) custom-call(bf16[51,2,512]{2,1,0:T(2,128)(2,1)S(1)} %copy-done.5, bf16[51,2,512]{2,1,0:T(2,128)(2,1)S(1)} %collective-permute-done.b1, ...), custom_call_target="tpu_custom_call" | custom-call | flops 8000000000 | bytes 8000000 | tf_op jit(solution)/shard_map/main/pallas_call | solution.py:408
  28.0 3.5 %collective-permute-start.3 = (bf16[48,2,512]{2,1,0:T(2,128)(2,1)S(1)}, bf16[48,2,512]{2,1,0:T(2,128)(2,1)S(1)}, u32[]{:S(2)}, u32[]{:S(2)}) collective-permute-start(bf16[48,2,512]{2,1,0:T(2,128)(2,1)S(1)} %get-tuple-element.22), channel_id=1, source_target_pairs={{0,33},{1,34},{2,35},{3,36},{4,37},{5,38},{6,39},{7,40},{8,41},{9,... | collective-permute-start | bytes 294920 | tf_op jit(solution)/shard_map/ppermute | solution.py:430
  31.5 1.3 %collective-permute-start.4 = (bf16[48,2,512]{2,1,0:T(2,128)(2,1)S(1)}, bf16[48,2,512]{2,1,0:T(2,128)(2,1)S(1)}, u32[]{:S(2)}, u32[]{:S(2)}) collective-permute-start(bf16[48,2,512]{2,1,0:T(2,128)(2,1)S(1)} %get-tuple-element.23), channel_id=1, source_target_pairs={{0,32},{1,33},{2,34},{3,35},{4,36},{5,37},{6,38},{7,39},{8,40},{9,... | collective-permute-start | bytes 294920 | tf_op jit(solution)/shard_map/ppermute | solution.py:430
  32.8 4.0 %collective-permute-done.3.h0 = bf16[48,2,512]{2,1,0:T(2,128)(2,1)S(1)} collective-permute-done((bf16[48,2,512]{2,1,0:T(2,128)(2,1)S(1)}, bf16[48,2,512]{2,1,0:T(2,128)(2,1)S(1)}, u32[]{:S(2)}, u32[]{:S(2)}) %collective-permute-start.3) | collective-permute-done | bytes 98336 | tf_op jit(solution)/shard_map/ppermute | solution.py:430
  36.7 0.4 collective-permute-done.4.h1
  37.1 3.3 %collective-permute-done.5.h2 = bf16[48,2,512]{2,1,0:T(2,128)(2,1)S(1)} collective-permute-done((bf16[48,2,512]{2,1,0:T(2,128)(2,1)S(1)}, bf16[48,2,512]{2,1,0:T(2,128)(2,1)S(1)}, u32[]{:S(2)}, u32[]{:S(2)}) %collective-permute-start.5) | collective-permute-done | bytes 98336 | tf_op jit(solution)/shard_map/ppermute | solution.py:430
  40.4 1.5 %home.1 = (bf16[6,12,2,512]{3,2,1,0:T(2,128)(2,1)}, bf16[6,12,2,512]{3,2,1,0:T(2,128)(2,1)}, bf16[3,6,2,1024]{3,2,1,0:T(2,128)(2,1)}) custom-call(bf16[48,2,512]{2,1,0:T(2,128)(2,1)S(1)} %collective-permute-done.3.h0, bf16[48,2,512]{2,1,0:T(2,128)(2,1)S(1)} %collective-permute-done.4.h1, bf16[48,2,512]{2,1,0:T(2,128)(2,1)S(1)} %collective-permute-done.5.h2, ...), custom_call_target="tpu_custom_call" | custom-call | flops 1000000 | bytes 1000 | tf_op jit(solution)/shard_map/home/pallas_call | solution.py:408
  (24 shorter events, 0.1 us)
Async XLA Ops:
  2.5 15.7 %collective-permute-start = (bf16[51,2,512]{2,1,0:T(2,128)(2,1)}, bf16[51,2,512]{2,1,0:T(2,128)(2,1)S(1)}, u32[]{:S(2)}, u32[]{:S(2)}) collective-permute-start(bf16[51,2,512]{2,1,0:T(2,128)(2,1)} %get-tuple-element.17), channel_id=1, source_target_pairs={{0,31},{1,0},{2,1},{3,2},{4,3},{5,4},{6,5},{7,6},{8,7},{9,8},{10,9... | collective-permute-start | bytes 313352 | tf_op jit(solution)/shard_map/ppermute | solution.py:430
  10.3 8.0 %collective-permute-start.1 = (bf16[51,2,512]{2,1,0:T(2,128)(2,1)}, bf16[51,2,512]{2,1,0:T(2,128)(2,1)S(1)}, u32[]{:S(2)}, u32[]{:S(2)}) collective-permute-start(bf16[51,2,512]{2,1,0:T(2,128)(2,1)} %get-tuple-element.18), channel_id=1, source_target_pairs={{0,224},{1,225},{2,226},{3,227},{4,228},{5,229},{6,230},{7,231},{8... | collective-permute-start | bytes 313352 | tf_op jit(solution)/shard_map/ppermute | solution.py:430
  11.1 7.4 %collective-permute-start.2 = (bf16[51,2,512]{2,1,0:T(2,128)(2,1)}, bf16[51,2,512]{2,1,0:T(2,128)(2,1)S(1)}, u32[]{:S(2)}, u32[]{:S(2)}) collective-permute-start(bf16[51,2,512]{2,1,0:T(2,128)(2,1)} %get-tuple-element.19), channel_id=1, source_target_pairs={{0,255},{1,224},{2,225},{3,226},{4,227},{5,228},{6,229},{7,230},{8... | collective-permute-start | bytes 313352 | tf_op jit(solution)/shard_map/ppermute | solution.py:430
  13.1 5.4 %copy-start = (bf16[1024,2048]{1,0:T(8,128)(2,1)S(1)}, bf16[1024,2048]{1,0:T(8,128)(2,1)}, u32[]{:S(2)}) copy-start(bf16[1024,2048]{1,0:T(8,128)(2,1)} %split.1) | copy-start | bytes 12582916
  13.1 5.4 %copy-start.1 = (bf16[512,1536]{1,0:T(8,128)(2,1)S(1)}, bf16[512,1536]{1,0:T(8,128)(2,1)}, u32[]{:S(2)}) copy-start(bf16[512,1536]{1,0:T(8,128)(2,1)} %e_weight.1) | copy-start | bytes 4718596
  13.1 5.4 %copy-start.2 = (bf16[512,1536]{1,0:T(8,128)(2,1)S(1)}, bf16[512,1536]{1,0:T(8,128)(2,1)}, u32[]{:S(2)}) copy-start(bf16[512,1536]{1,0:T(8,128)(2,1)} %d_weight.1) | copy-start | bytes 4718596
  13.1 5.4 %copy-start.3 = (bf16[512,512]{1,0:T(8,128)(2,1)S(1)}, bf16[512,512]{1,0:T(8,128)(2,1)}, u32[]{:S(2)}) copy-start(bf16[512,512]{1,0:T(8,128)(2,1)} %e_out_weight.1) | copy-start | bytes 1572868
  13.1 5.4 %copy-start.4 = (bf16[512,512]{1,0:T(8,128)(2,1)S(1)}, bf16[512,512]{1,0:T(8,128)(2,1)}, u32[]{:S(2)}) copy-start(bf16[512,512]{1,0:T(8,128)(2,1)} %d_out_weight.1) | copy-start | bytes 1572868
  13.1 5.3 %copy-start.5 = (bf16[51,2,512]{2,1,0:T(2,128)(2,1)S(1)}, bf16[51,2,512]{2,1,0:T(2,128)(2,1)}, u32[]{:S(2)}) copy-start(bf16[51,2,512]{2,1,0:T(2,128)(2,1)} %get-tuple-element.16.b0) | copy-start | bytes 313348
  13.1 5.3 %copy-start.6 = (f32[1536]{0:T(1024)S(1)}, f32[1536]{0:T(1024)}, u32[]{:S(2)}) copy-start(f32[1536]{0:T(1024)} %e_bias.1) | copy-start | bytes 18436
  13.2 5.3 %copy-start.7 = (f32[1536]{0:T(1024)S(1)}, f32[1536]{0:T(1024)}, u32[]{:S(2)}) copy-start(f32[1536]{0:T(1024)} %d_bias.1) | copy-start | bytes 18436
  13.2 5.3 %copy-start.8 = (f32[2048]{0:T(1024)S(1)}, f32[2048]{0:T(1024)}, u32[]{:S(2)}) copy-start(f32[2048]{0:T(1024)} %param.41) | copy-start | bytes 24580
  13.2 5.3 %copy-start.9 = (f32[512]{0:T(512)S(1)}, f32[512]{0:T(512)}, u32[]{:S(2)}) copy-start(f32[512]{0:T(512)} %param.26) | copy-start | bytes 6148
  13.2 5.3 %copy-start.10 = (f32[512]{0:T(512)S(1)}, f32[512]{0:T(512)}, u32[]{:S(2)}) copy-start(f32[512]{0:T(512)} %param.27) | copy-start | bytes 6148
  13.2 5.3 %copy-start.11 = (f32[512]{0:T(512)S(1)}, f32[512]{0:T(512)}, u32[]{:S(2)}) copy-start(f32[512]{0:T(512)} %param.31) | copy-start | bytes 6148
  13.2 5.3 %copy-start.12 = (f32[512]{0:T(512)S(1)}, f32[512]{0:T(512)}, u32[]{:S(2)}) copy-start(f32[512]{0:T(512)} %param.33) | copy-start | bytes 6148
  13.2 5.3 %copy-start.13 = (f32[512]{0:T(512)S(1)}, f32[512]{0:T(512)}, u32[]{:S(2)}) copy-start(f32[512]{0:T(512)} %param.34) | copy-start | bytes 6148
  13.2 5.3 %copy-start.14 = (f32[512]{0:T(512)S(1)}, f32[512]{0:T(512)}, u32[]{:S(2)}) copy-start(f32[512]{0:T(512)} %param.38) | copy-start | bytes 6148
  28.0 8.7 %collective-permute-start.3 = (bf16[48,2,512]{2,1,0:T(2,128)(2,1)S(1)}, bf16[48,2,512]{2,1,0:T(2,128)(2,1)S(1)}, u32[]{:S(2)}, u32[]{:S(2)}) collective-permute-start(bf16[48,2,512]{2,1,0:T(2,128)(2,1)S(1)} %get-tuple-element.22), channel_id=1, source_target_pairs={{0,33},{1,34},{2,35},{3,36},{4,37},{5,38},{6,39},{7,40},{8,41},{9,... | collective-permute-start | bytes 294920 | tf_op jit(solution)/shard_map/ppermute | solution.py:430
  31.5 5.7 %collective-permute-start.4 = (bf16[48,2,512]{2,1,0:T(2,128)(2,1)S(1)}, bf16[48,2,512]{2,1,0:T(2,128)(2,1)S(1)}, u32[]{:S(2)}, u32[]{:S(2)}) collective-permute-start(bf16[48,2,512]{2,1,0:T(2,128)(2,1)S(1)} %get-tuple-element.23), channel_id=1, source_target_pairs={{0,32},{1,33},{2,34},{3,35},{4,36},{5,37},{6,38},{7,39},{8,40},{9,... | collective-permute-start | bytes 294920 | tf_op jit(solution)/shard_map/ppermute | solution.py:430
  32.7 7.7 %collective-permute-start.5 = (bf16[48,2,512]{2,1,0:T(2,128)(2,1)S(1)}, bf16[48,2,512]{2,1,0:T(2,128)(2,1)S(1)}, u32[]{:S(2)}, u32[]{:S(2)}) collective-permute-start(bf16[48,2,512]{2,1,0:T(2,128)(2,1)S(1)} %get-tuple-element.24), channel_id=1, source_target_pairs={{0,1},{1,2},{2,3},{3,4},{4,5},{5,6},{6,7},{7,8},{8,9},{9,10},{10,1... | collective-permute-start | bytes 294920 | tf_op jit(solution)/shard_map/ppermute | solution.py:430

commit v3 on v2

--- a/solution.py
+++ b/solution.py
@@ -38,16 +38,36 @@
     return lax.dot_general(a, b, TN, preferred_element_type=f32)
 
 
-def gather_quadrants(refs, base, scratch):
+def column_parity():
+    return lax.axis_index("lon") % 2
+
+
+def swapped(m, parity):
+    return m + parity * (1 - 2 * m)
+
+
+def gather_quadrants(refs, base, scratch, parity):
     for q, ref in enumerate(refs):
+        m, qc = divmod(q, 2)
+        half = swapped(m, parity)
         for t in range(PAIRS):
-            scratch[pl.ds(2 * (q * PAIRS + t), 2), :] = ref[base + t].astype(f32)
-
-
-def scatter_quadrants(scratch, refs, base):
+            scratch[half, pl.ds(2 * (qc * PAIRS + t), 2), :] = ref[base + t].astype(f32)
+
+
+def scatter_quadrants(scratch, refs, base, parity):
     for q, ref in enumerate(refs):
+        m, qc = divmod(q, 2)
+        half = swapped(m, parity)
         for t in range(PAIRS):
-            ref[base + t] = scratch[pl.ds(2 * (q * PAIRS + t), 2), :].astype(bf16)
+            ref[base + t] = scratch[half, pl.ds(2 * (qc * PAIRS + t), 2), :].astype(bf16)
+
+
+def whole(scratch):
+    return scratch[...].reshape(-1, scratch.shape[-1])
+
+
+def fill(scratch, value):
+    scratch[...] = value.reshape(scratch.shape)
 
 
 def token_place(t):
@@ -79,15 +99,17 @@
     return total
 
 
-def mask_bias(refs, lats):
+def mask_bias(refs, lats, parity):
     token = lax.broadcasted_iota(jnp.int32, (1, WIDE), 1)
     quadrant, r, c, level = token_place(token)
     lane = HN * (1 - quadrant % 2) + c
     hot = lax.broadcasted_iota(jnp.int32, (128, WIDE), 0) == lane
     rows = jnp.concatenate([ref[CLASS_AT + r, :, :128].astype(f32) for ref in refs for r in range(HL)], axis=0)
     spread = dot(rows.astype(bf16), hot.astype(f32).astype(bf16))
-    mine = lax.broadcasted_iota(jnp.int32, (4 * HL * LEVELS, WIDE), 0) == (quadrant * HL + r) * LEVELS + level
-    seam = jnp.where(lax.axis_index("lat") == lats - 1, (quadrant // 2).astype(f32), 0.0)
+    piece = swapped(quadrant // 2, parity) * 2 + quadrant % 2
+    mine = lax.broadcasted_iota(jnp.int32, (4 * HL * LEVELS, WIDE), 0) == (piece * HL + r) * LEVELS + level
+    last = lax.axis_index("lat") == jnp.where(parity == 0, lats - 1, 0)
+    seam = jnp.where(last, (quadrant // 2).astype(f32), 0.0)
     label = 2.0 * jnp.sum(jnp.where(mine, spread, 0.0), axis=0, keepdims=True) + seam
     label = jnp.where(token < SPAN, label, 9.0)
     eye = lax.broadcasted_iota(jnp.int32, (SPAN, WIDE), 0) == lax.broadcasted_iota(jnp.int32, (SPAN, WIDE), 1)
@@ -178,10 +200,12 @@
     for copy in arrivals:
         copy.wait()
     departures = []
+    parity = column_parity()
     for q in (3, 2, 1, 0):
-        qr, qc = divmod(q, 2)
-        lat, lon = HL * (1 - qr), HN * (1 - qc)
-        low_lat, low_lon = (coarse.shape[0] - COARSE_ROWS) * (1 - qr), COARSE_COLS * (1 - qc)
+        m, qc = divmod(q, 2)
+        later = swapped(swapped(1 - m, qc), parity)
+        lat, lon = HL * later, HN * (1 - qc)
+        low_lat, low_lon = (coarse.shape[0] - COARSE_ROWS) * later, COARSE_COLS * (1 - qc)
         for r in range(HL):
             buffers[q, pl.ds(r * HN, HN)] = tokens[lat + r, pl.ds(lon, HN)]
             buffers[q, pl.ds(COTANGENT_AT + r * HN, HN)] = cotangent[lat + r, pl.ds(lon, HN)]
@@ -255,10 +279,10 @@
                     half * HEADS : (half + 1) * HEADS, n * 128 : (n + 1) * 128
                 ]
 
-    @pl.loop(0, SPAN // 16)
+    @pl.loop(0, SPAN // 48)
     def _(step):
-        for n in range(8):
-            two_rows(16 * step + 2 * n)
+        for n in range(24):
+            two_rows(48 * step + 2 * n)
 
     for g in range(SPAN // rest):
         result = look(packed_low[pl.ds(g, 1), :], packed_high[pl.ds(g, 1), :])
@@ -293,13 +317,8 @@
     )(inputs)
 
 
-def coarse_points(q):
-    qr, qc = divmod(q, 2)
-    return [
-        (qr * COARSE_ROWS + r) * 2 * COARSE_COLS + qc * COARSE_COLS + c
-        for r in range(COARSE_ROWS)
-        for c in range(COARSE_COLS)
-    ]
+def coarse_points(qc):
+    return [r * 2 * COARSE_COLS + qc * COARSE_COLS + c for r in range(COARSE_ROWS) for c in range(COARSE_COLS)]
 
 
 def coarse_places():
@@ -325,75 +344,83 @@
         rows = pl.ds(h * SPAN, SPAN)
         return jnp.concatenate([bias_main[rows, :], bias_rest[rows, :]], axis=1)
 
+    parity = column_parity()
     parts = (b0, b1, b2, b3)
-    gather_quadrants(parts, 0, scratch)
-    x = scratch[...]
+    gather_quadrants(parts, 0, scratch, parity)
+    x = whole(scratch)
     tokens[...] = x.astype(bf16)
-    blank = mask_bias(parts, lats)
+    blank = mask_bias(parts, lats, parity)
     encoded = block_forward(
         x, blank, lambda h: bias_rows(h), e_gain[...], e_offset[...], e_weight,
         e_bias[...].reshape(1, -1), e_out_weight[...], e_out_bias[...], e_qkv, e_probs,
     ).astype(bf16)
 
     for q, ref in enumerate(parts):
-        for n, at in enumerate(coarse_points(q)):
+        part = swapped(q // 2, parity)
+        for n, at in enumerate(coarse_points(q % 2)):
             for half in range(2):
-                coarse[pl.ds(2 * at, 2), pl.ds(D * half, D)] = ref[COARSE_AT + POINTS * half + n].astype(f32)
-    lowres = coarse[...].astype(bf16)
+                coarse[part, pl.ds(2 * at, 2), pl.ds(D * half, D)] = ref[COARSE_AT + POINTS * half + n].astype(f32)
+    lowres = whole(coarse).astype(bf16)
     fine[...] = dot(lowres, split[...]) + split_bias[...]
     for t, at, kind in coarse_places():
-        scratch[pl.ds(2 * t, 2), :] = fine[pl.ds(2 * at, 2), pl.ds(kind * D, D)]
-    x = (encoded.astype(f32) + scratch[...]).astype(bf16).astype(f32)
+        scratch[t // (2 * PAIRS), pl.ds(2 * (t % (2 * PAIRS)), 2), :] = fine[pl.ds(2 * at, 2), pl.ds(kind * D, D)]
+    x = (encoded.astype(f32) + whole(scratch)).astype(bf16).astype(f32)
     decoded = block_forward(
         x, blank, lambda h: bias_rows(HEADS + h), d_gain[...], d_offset[...], d_weight,
         d_bias[...].reshape(1, -1), d_out_weight[...], d_out_bias[...], d_qkv, d_probs,
     )
     outs = (o0, o1, o2, o3)
-    scratch[...] = decoded
-    scatter_quadrants(scratch, outs, 0)
-    gather_quadrants(parts, COTANGENT_AT, scratch)
-    grad = scratch[...].astype(bf16)
+    fill(scratch, decoded)
+    scatter_quadrants(scratch, outs, 0, parity)
+    gather_quadrants(parts, COTANGENT_AT, scratch, parity)
+    grad = whole(scratch).astype(bf16)
     dx = block_backward(grad, x, d_gain[...], d_weight[...], d_out_weight[...], d_qkv, d_probs, dqkv)
     grad = dx.astype(bf16)
 
-    scratch[...] = dx
+    fill(scratch, dx)
     fine[...] = jnp.zeros_like(fine)
     for t, at, kind in coarse_places():
-        fine[pl.ds(2 * at, 2), pl.ds(kind * D, D)] = scratch[pl.ds(2 * t, 2), :]
-    coarse[...] = dot_nt(fine[...].astype(bf16), split[...])
+        fine[pl.ds(2 * at, 2), pl.ds(kind * D, D)] = scratch[t // (2 * PAIRS), pl.ds(2 * (t % (2 * PAIRS)), 2), :]
+    fill(coarse, dot_nt(fine[...].astype(bf16), split[...]))
     for q, ref in enumerate(outs):
-        for n, at in enumerate(coarse_points(q)):
+        part = swapped(q // 2, parity)
+        for n, at in enumerate(coarse_points(q % 2)):
             for half in range(2):
-                ref[COARSE_AT + POINTS * half + n] = coarse[pl.ds(2 * at, 2), pl.ds(D * half, D)].astype(bf16)
-
-    scratch[...] = block_backward(
+                ref[COARSE_AT + POINTS * half + n] = coarse[part, pl.ds(2 * at, 2), pl.ds(D * half, D)].astype(bf16)
+
+    dx = block_backward(
         grad, tokens[...].astype(f32), e_gain[...], e_weight[...], e_out_weight[...], e_qkv, e_probs, dqkv
     )
-    scatter_quadrants(scratch, outs, PAIRS)
+    fill(scratch, dx)
+    scatter_quadrants(scratch, outs, PAIRS, parity)
 
 
 def home_kernel(h0, h1, h2, h3, decoded, tokens_gradient, coarse_gradient, sems):
+    parity = column_parity()
+    refs = (h0, h1, h2, h3)
     copies = []
-    for q, ref in enumerate((h0, h1, h2, h3)):
+    for q, ref in enumerate(refs):
+        m, qc = divmod(q, 2)
+        later = swapped(swapped(1 - m, qc), parity)
         for n, out in enumerate((decoded, tokens_gradient)):
             for r in range(HL):
                 copy = pltpu.make_async_copy(
                     ref.at[pl.ds(PAIRS * n + r * HN, HN)],
-                    out.at[q // 2 * HL + r, pl.ds(q % 2 * HN, HN)],
+                    out.at[HL * later + r, pl.ds(HN * (1 - qc), HN)],
                     sems.at[len(copies)],
                 )
                 copy.start()
                 copies.append(copy)
-    for qc, (upper, lower) in enumerate(((h0, h2), (h1, h3))):
+    for qc in range(2):
+        begins = swapped(qc, parity) == 0
+        own, other = refs[qc], refs[2 + qc]
         for half in range(2):
             for c in range(COARSE_COLS):
                 at = COARSE_AT + POINTS * half + c
-                lanes = pl.ds(D * half, D)
-                column = qc * COARSE_COLS + c
-                coarse_gradient[0, column, :, lanes] = upper[at]
-                both = upper[at + COARSE_COLS].astype(f32) + lower[at].astype(f32)
-                coarse_gradient[1, column, :, lanes] = both.astype(bf16)
-                coarse_gradient[2, column, :, lanes] = lower[at + COARSE_COLS]
+                a0, a1, b0, b1 = (r[at + k].astype(f32) for r in (own, other) for k in (0, COARSE_COLS))
+                rows = (jnp.where(begins, b0, a0), jnp.where(begins, b1 + a0, a1 + b0), jnp.where(begins, a1, b1))
+                for n, row in enumerate(rows):
+                    coarse_gradient[n, (1 - qc) * COARSE_COLS + c, :, pl.ds(D * half, D)] = row.astype(bf16)
     for copy in copies:
         copy.wait()
 
@@ -417,17 +444,19 @@
     )(*inputs)
 
 
-def shift_pairs(lat, lon, lats, lons):
-    return [
-        (i * lons + j, ((i + lat) % lats) * lons + (j + lon) % lons) for i in range(lats) for j in range(lons)
-    ]
-
-
-def exchange(pieces, steps, lats, lons):
+def exchange(pieces, lats, lons, back):
     out = [pieces[0]]
     for q in range(1, 4):
-        qr, qc = divmod(q, 2)
-        out.append(lax.ppermute(pieces[q], ("lat", "lon"), shift_pairs(qr * steps, qc * steps, lats, lons)))
+        m, qc = divmod(q, 2)
+        pairs = []
+        for i in range(lats):
+            for j in range(lons):
+                to = (j - qc) % lons
+                step = m * (1 if to % 2 else -1)
+                pairs.append((i * lons + j, (i + step) % lats * lons + to))
+        if back:
+            pairs = [(target, source) for source, target in pairs]
+        out.append(lax.ppermute(pieces[q], ("lat", "lon"), pairs))
     return out
 
 
@@ -468,7 +497,7 @@
         [ANY] * 4,
         60,
     )
-    parts = exchange(packed, -1, lats, lons)
+    parts = exchange(packed, lats, lons, False)
     biases = lookup(relative_index, encoder_table, decoder_table)
     points = 4 * LEVELS * POINTS
     outs = call(
@@ -483,8 +512,8 @@
         ],
         [s((CLASS_AT, LEVELS, D), bf16)] * 4,
         [
-            pltpu.VMEM((SPAN, D), f32),
-            pltpu.VMEM((points, 2 * D), f32),
+            pltpu.VMEM((2, SPAN // 2, D), f32),
+            pltpu.VMEM((2, points // 2, 2 * D), f32),
             pltpu.VMEM((points, 4 * D), f32),
             pltpu.VMEM((SPAN, D), bf16),
             pltpu.VMEM((SPAN, 3 * D), bf16),
@@ -495,13 +524,13 @@
         ],
         8_000_000_000,
     )
-    home = exchange(outs, 1, lats, lons)
+    home = exchange(outs, lats, lons, True)
     grid = s((WIN_LAT, WIN_LON, LEVELS, D), bf16)
     low = s((WIN_LAT // 2, WIN_LON // 2, LEVELS, 2 * D), bf16)
     results = call(
         home_kernel,
         "home",
-        [home[3 - q] for q in range(4)],
+        home,
         [grid, grid, low],
         [pltpu.SemaphoreType.DMA((4 * 2 * HL,))],
         1_000_000,

time: 42.1 us -> 42.8 us (1.017)
  waiting for transfers between devices: 7.87 us -> 10.4 us
  starting transfers between devices: 13.6 us -> 12.1 us
  Pallas kernels: 17.8 us -> 17 us
    ppermute x6, waiting for transfers between devices: 7.87 us -> 10.4 us  [exchange(): out.append(lax.ppermute(pieces[q], ('lat', 'lon'), pairs))]
    ppermute x6, starting transfers between devices: 13.6 us -> 12.1 us  [exchange(): out.append(lax.ppermute(pieces[q], ('lat', 'lon'), pairs))]
    pallas_call x1, Pallas kernels: 4.96 us -> 3.95 us  [lookup(): pl.pallas_call(lookup_kernel, out_shape=[jax.ShapeDtypeStruct((2 * HEADS...]
  transfers between devices with their start and end apart: 6 -> 6, of which waited for: 4 -> 4; matrix products, arithmetic and copies ran while one was open for 4% -> 4% of each run, Pallas kernels for 12% -> 9%
where the time goes in v3:
time: 42.8 us; the launch traced here: 42.3 us
  Pallas kernels  17 us (40%)
  starting transfers between devices  12.1 us (28%)
  waiting for transfers between devices  10.4 us (24%)
  other arithmetic  1.71 us (4%)
  between operations  1.06 us (2%)
    pallas_call x3, Pallas kernels, call(): pl.pallas_call(kernel, out_shape=outs, in_specs=in_specs or [VM] * len(in...  13 us
    ppermute x6, starting transfers between devices, exchange(): out.append(lax.ppermute(pieces[q], ('lat', 'lon'), pairs))  12.1 us
    ppermute x6, waiting for transfers between devices, exchange(): out.append(lax.ppermute(pieces[q], ('lat', 'lon'), pairs))  10.4 us
    pallas_call x1, Pallas kernels, lookup(): pl.pallas_call(lookup_kernel, out_shape=[jax.ShapeDtypeStruct((2 * HEADS...  3.95 us
    convert_element_type x1, other arithmetic, lookup(): relative_index.astype(f32)  0.92 us
  transfers between devices with their start and end apart: 6, of which 4 were waited for; matrix products, arithmetic and copies ran while one was open for 4% of the time, Pallas kernels for 9%

profile of v3, /device:TPU:24, one launch (start us, length us, event | category | flops | bytes accessed | tf_op | source)
XLA Modules:
  0.0 42.3 jit_solution(9491871135060707246)
XLA Ops:
  0.6 1.9 %pack.1 = (bf16[51,2,512]{2,1,0:T(2,128)(2,1)}, bf16[51,2,512]{2,1,0:T(2,128)(2,1)}, bf16[51,2,512]{2,1,0:T(2,128)(2,1)}, bf16[51,2,512]{2,1,0:T(2,128)(2,1)}) custom-call(bf16[6,12,2,512]{3,2,1,0:T(2,128)(2,1)} %bitcast.21, bf16[6,12,2,512]{3,2,1,0:T(2,128)(2,1)} %bitcast.22, bf16[3,6,2,1024]{3,2,1,0:T(2,128)(2,1)} %bitcast.23, s32[6,2,12]{2,1,0:T(2,128)} %bitcast.24), custom_call_target="tpu_custom_call" | custom-call | flops 100000000 | bytes 100000 | tf_op jit(solution)/shard_map/pack/pallas_call | solution.py:435
  2.5 7.8 %collective-permute-start = (bf16[51,2,512]{2,1,0:T(2,128)(2,1)}, bf16[51,2,512]{2,1,0:T(2,128)(2,1)S(1)}, u32[]{:S(2)}, u32[]{:S(2)}) collective-permute-start(bf16[51,2,512]{2,1,0:T(2,128)(2,1)} %get-tuple-element.17), channel_id=1, source_target_pairs={{0,31},{1,0},{2,1},{3,2},{4,3},{5,4},{6,5},{7,6},{8,7},{9,8},{10,9... | collective-permute-start | bytes 313352 | tf_op jit(solution)/shard_map/ppermute | solution.py:459
  10.3 0.7 %collective-permute-start.1 = (bf16[51,2,512]{2,1,0:T(2,128)(2,1)}, bf16[51,2,512]{2,1,0:T(2,128)(2,1)S(1)}, u32[]{:S(2)}, u32[]{:S(2)}) collective-permute-start(bf16[51,2,512]{2,1,0:T(2,128)(2,1)} %get-tuple-element.18), channel_id=1, source_target_pairs={{0,224},{1,33},{2,226},{3,35},{4,228},{5,37},{6,230},{7,39},{8,232... | collective-permute-start | bytes 313352 | tf_op jit(solution)/shard_map/ppermute | solution.py:459
  11.1 0.6 %collective-permute-start.2 = (bf16[51,2,512]{2,1,0:T(2,128)(2,1)}, bf16[51,2,512]{2,1,0:T(2,128)(2,1)S(1)}, u32[]{:S(2)}, u32[]{:S(2)}) collective-permute-start(bf16[51,2,512]{2,1,0:T(2,128)(2,1)} %get-tuple-element.19), channel_id=1, source_target_pairs={{0,63},{1,224},{2,33},{3,226},{4,35},{5,228},{6,37},{7,230},{8,39}... | collective-permute-start | bytes 313352 | tf_op jit(solution)/shard_map/ppermute | solution.py:459
  11.7 0.9 %convert_element_type.8 = f32[144,144]{1,0:T(8,128)S(1)} convert(s32[144,144]{1,0:T(8,128)} %param.25) | non-fusion elementwise | flops 20736 | bytes 165888 | tf_op jit(solution)/shard_map/convert_element_type | solution.py:303
  12.6 0.8 %select_maximum_fusion.inputs_ref = f32[160,768]{1,0:T(8,128)S(1)} fusion(f32[8,759]{1,0:T(8,128)} %param.39, f32[8,759]{1,0:T(8,128)} %param.32, f32[144,144]{1,0:T(8,128)S(1)} %convert_element_type.8), kind=kLoop, calls=%fused_computation.2 | loop fusion | flops 1228800 | bytes 623040 | tf_op jit(solution)/shard_map/concatenate | solution.py:303
  13.4 0.0 copy-start
  13.4 0.0 copy-start.1
  13.4 0.0 copy-start.2
  13.5 0.0 copy-start.4
  13.5 0.0 copy-start.5
  13.5 0.0 copy-start.8
  13.5 0.0 copy-start.9
  13.6 0.0 copy-start.12
  13.6 0.0 copy-start.13
  13.6 3.9 %lookup.1 = (f32[2304,128]{1,0:T(8,128)S(1)}, f32[2304,128]{1,0:T(8,128)S(1)}) custom-call(f32[160,768]{1,0:T(8,128)S(1)} %select_maximum_fusion.inputs_ref), custom_call_target="tpu_custom_call" | custom-call | flops 3000000000 | bytes 4000000 | tf_op jit(solution)/shard_map/lookup/pallas_call | solution.py:304
  17.6 0.7 %collective-permute-done.1.b2 = bf16[51,2,512]{2,1,0:T(2,128)(2,1)S(1)} collective-permute-done((bf16[51,2,512]{2,1,0:T(2,128)(2,1)}, bf16[51,2,512]{2,1,0:T(2,128)(2,1)S(1)}, u32[]{:S(2)}, u32[]{:S(2)}) %collective-permute-start.1) | collective-permute-done | bytes 104480 | tf_op jit(solution)/shard_map/ppermute | solution.py:459
  18.3 0.2 collective-permute-done.2.b3
  18.6 9.6 %main.1 = (bf16[48,2,512]{2,1,0:T(2,128)(2,1)S(1)}, bf16[48,2,512]{2,1,0:T(2,128)(2,1)S(1)}, bf16[48,2,512]{2,1,0:T(2,128)(2,1)S(1)}, bf16[48,2,512]{2,1,0:T(2,128)(2,1)S(1)}) custom-call(bf16[51,2,512]{2,1,0:T(2,128)(2,1)S(1)} %copy-done.5, bf16[51,2,512]{2,1,0:T(2,128)(2,1)S(1)} %collective-permute-done.b1, ...), custom_call_target="tpu_custom_call" | custom-call | flops 8000000000 | bytes 8000000 | tf_op jit(solution)/shard_map/main/pallas_call | solution.py:435
  28.2 0.1 collective-permute-start.3
  28.3 2.8 %collective-permute-start.4 = (bf16[48,2,512]{2,1,0:T(2,128)(2,1)S(1)}, bf16[48,2,512]{2,1,0:T(2,128)(2,1)S(1)}, u32[]{:S(2)}, u32[]{:S(2)}) collective-permute-start(bf16[48,2,512]{2,1,0:T(2,128)(2,1)S(1)} %get-tuple-element.24), channel_id=1, source_target_pairs={{224,0},{33,1},{226,2},{35,3},{228,4},{37,5},{230,6},{39,7},{232,8... | collective-permute-start | bytes 294920 | tf_op jit(solution)/shard_map/ppermute | solution.py:459
  31.1 5.0 %collective-permute-done.3.h1 = bf16[48,2,512]{2,1,0:T(2,128)(2,1)S(1)} collective-permute-done((bf16[48,2,512]{2,1,0:T(2,128)(2,1)S(1)}, bf16[48,2,512]{2,1,0:T(2,128)(2,1)S(1)}, u32[]{:S(2)}, u32[]{:S(2)}) %collective-permute-start.3) | collective-permute-done | bytes 98336 | tf_op jit(solution)/shard_map/ppermute | solution.py:459
  36.1 4.5 %collective-permute-done.5.h3 = bf16[48,2,512]{2,1,0:T(2,128)(2,1)S(1)} collective-permute-done((bf16[48,2,512]{2,1,0:T(2,128)(2,1)S(1)}, bf16[48,2,512]{2,1,0:T(2,128)(2,1)S(1)}, u32[]{:S(2)}, u32[]{:S(2)}) %collective-permute-start.5) | collective-permute-done | bytes 98336 | tf_op jit(solution)/shard_map/ppermute | solution.py:459
  40.6 1.5 %home.1 = (bf16[6,12,2,512]{3,2,1,0:T(2,128)(2,1)}, bf16[6,12,2,512]{3,2,1,0:T(2,128)(2,1)}, bf16[3,6,2,1024]{3,2,1,0:T(2,128)(2,1)}) custom-call(bf16[48,2,512]{2,1,0:T(2,128)(2,1)S(1)} %get-tuple-element.22.h0, bf16[48,2,512]{2,1,0:T(2,128)(2,1)S(1)} %collective-permute-done.3.h1, bf16[48,2,512]{2,1,0:T(2,128)(2,1)S(1)} %collective-permute-done.4.h2, ...), custom_call_target="tpu_custom_call" | custom-call | flops 1000000 | bytes 1000 | tf_op jit(solution)/shard_map/home/pallas_call | solution.py:435
  (24 shorter events, 0.1 us)
Async XLA Ops:
  2.5 15.1 %collective-permute-start = (bf16[51,2,512]{2,1,0:T(2,128)(2,1)}, bf16[51,2,512]{2,1,0:T(2,128)(2,1)S(1)}, u32[]{:S(2)}, u32[]{:S(2)}) collective-permute-start(bf16[51,2,512]{2,1,0:T(2,128)(2,1)} %get-tuple-element.17), channel_id=1, source_target_pairs={{0,31},{1,0},{2,1},{3,2},{4,3},{5,4},{6,5},{7,6},{8,7},{9,8},{10,9... | collective-permute-start | bytes 313352 | tf_op jit(solution)/shard_map/ppermute | solution.py:459
  10.3 8.0 %collective-permute-start.1 = (bf16[51,2,512]{2,1,0:T(2,128)(2,1)}, bf16[51,2,512]{2,1,0:T(2,128)(2,1)S(1)}, u32[]{:S(2)}, u32[]{:S(2)}) collective-permute-start(bf16[51,2,512]{2,1,0:T(2,128)(2,1)} %get-tuple-element.18), channel_id=1, source_target_pairs={{0,224},{1,33},{2,226},{3,35},{4,228},{5,37},{6,230},{7,39},{8,232... | collective-permute-start | bytes 313352 | tf_op jit(solution)/shard_map/ppermute | solution.py:459
  11.1 7.4 %collective-permute-start.2 = (bf16[51,2,512]{2,1,0:T(2,128)(2,1)}, bf16[51,2,512]{2,1,0:T(2,128)(2,1)S(1)}, u32[]{:S(2)}, u32[]{:S(2)}) collective-permute-start(bf16[51,2,512]{2,1,0:T(2,128)(2,1)} %get-tuple-element.19), channel_id=1, source_target_pairs={{0,63},{1,224},{2,33},{3,226},{4,35},{5,228},{6,37},{7,230},{8,39}... | collective-permute-start | bytes 313352 | tf_op jit(solution)/shard_map/ppermute | solution.py:459
  13.4 5.0 %copy-start = (bf16[1024,2048]{1,0:T(8,128)(2,1)S(1)}, bf16[1024,2048]{1,0:T(8,128)(2,1)}, u32[]{:S(2)}) copy-start(bf16[1024,2048]{1,0:T(8,128)(2,1)} %split.1) | copy-start | bytes 12582916
  13.4 5.0 %copy-start.1 = (bf16[512,1536]{1,0:T(8,128)(2,1)S(1)}, bf16[512,1536]{1,0:T(8,128)(2,1)}, u32[]{:S(2)}) copy-start(bf16[512,1536]{1,0:T(8,128)(2,1)} %e_weight.1) | copy-start | bytes 4718596
  13.4 5.0 %copy-start.2 = (bf16[512,1536]{1,0:T(8,128)(2,1)S(1)}, bf16[512,1536]{1,0:T(8,128)(2,1)}, u32[]{:S(2)}) copy-start(bf16[512,1536]{1,0:T(8,128)(2,1)} %d_weight.1) | copy-start | bytes 4718596
  13.4 5.0 %copy-start.3 = (bf16[512,512]{1,0:T(8,128)(2,1)S(1)}, bf16[512,512]{1,0:T(8,128)(2,1)}, u32[]{:S(2)}) copy-start(bf16[512,512]{1,0:T(8,128)(2,1)} %e_out_weight.1) | copy-start | bytes 1572868
  13.5 5.0 %copy-start.4 = (bf16[512,512]{1,0:T(8,128)(2,1)S(1)}, bf16[512,512]{1,0:T(8,128)(2,1)}, u32[]{:S(2)}) copy-start(bf16[512,512]{1,0:T(8,128)(2,1)} %d_out_weight.1) | copy-start | bytes 1572868
  13.5 5.0 %copy-start.5 = (bf16[51,2,512]{2,1,0:T(2,128)(2,1)S(1)}, bf16[51,2,512]{2,1,0:T(2,128)(2,1)}, u32[]{:S(2)}) copy-start(bf16[51,2,512]{2,1,0:T(2,128)(2,1)} %get-tuple-element.16.b0) | copy-start | bytes 313348
  13.5 5.0 %copy-start.6 = (f32[1536]{0:T(1024)S(1)}, f32[1536]{0:T(1024)}, u32[]{:S(2)}) copy-start(f32[1536]{0:T(1024)} %e_bias.1) | copy-start | bytes 18436
  13.5 5.0 %copy-start.7 = (f32[1536]{0:T(1024)S(1)}, f32[1536]{0:T(1024)}, u32[]{:S(2)}) copy-start(f32[1536]{0:T(1024)} %d_bias.1) | copy-start | bytes 18436
  13.5 5.0 %copy-start.8 = (f32[2048]{0:T(1024)S(1)}, f32[2048]{0:T(1024)}, u32[]{:S(2)}) copy-start(f32[2048]{0:T(1024)} %param.41) | copy-start | bytes 24580
  13.5 5.0 %copy-start.9 = (f32[512]{0:T(512)S(1)}, f32[512]{0:T(512)}, u32[]{:S(2)}) copy-start(f32[512]{0:T(512)} %param.26) | copy-start | bytes 6148
  13.5 5.0 %copy-start.10 = (f32[512]{0:T(512)S(1)}, f32[512]{0:T(512)}, u32[]{:S(2)}) copy-start(f32[512]{0:T(512)} %param.27) | copy-start | bytes 6148
  13.5 5.0 %copy-start.11 = (f32[512]{0:T(512)S(1)}, f32[512]{0:T(512)}, u32[]{:S(2)}) copy-start(f32[512]{0:T(512)} %param.31) | copy-start | bytes 6148
  13.6 5.0 %copy-start.12 = (f32[512]{0:T(512)S(1)}, f32[512]{0:T(512)}, u32[]{:S(2)}) copy-start(f32[512]{0:T(512)} %param.33) | copy-start | bytes 6148
  13.6 5.0 %copy-start.13 = (f32[512]{0:T(512)S(1)}, f32[512]{0:T(512)}, u32[]{:S(2)}) copy-start(f32[512]{0:T(512)} %param.34) | copy-start | bytes 6148
  13.6 5.0 %copy-start.14 = (f32[512]{0:T(512)S(1)}, f32[512]{0:T(512)}, u32[]{:S(2)}) copy-start(f32[512]{0:T(512)} %param.38) | copy-start | bytes 6148
  28.2 7.8 %collective-permute-start.3 = (bf16[48,2,512]{2,1,0:T(2,128)(2,1)S(1)}, bf16[48,2,512]{2,1,0:T(2,128)(2,1)S(1)}, u32[]{:S(2)}, u32[]{:S(2)}) collective-permute-start(bf16[48,2,512]{2,1,0:T(2,128)(2,1)S(1)} %get-tuple-element.23), channel_id=1, source_target_pairs={{31,0},{0,1},{1,2},{2,3},{3,4},{4,5},{5,6},{6,7},{7,8},{8,9},{9,10... | collective-permute-start | bytes 294920 | tf_op jit(solution)/shard_map/ppermute | solution.py:459
  28.3 7.7 %collective-permute-start.4 = (bf16[48,2,512]{2,1,0:T(2,128)(2,1)S(1)}, bf16[48,2,512]{2,1,0:T(2,128)(2,1)S(1)}, u32[]{:S(2)}, u32[]{:S(2)}) collective-permute-start(bf16[48,2,512]{2,1,0:T(2,128)(2,1)S(1)} %get-tuple-element.24), channel_id=1, source_target_pairs={{224,0},{33,1},{226,2},{35,3},{228,4},{37,5},{230,6},{39,7},{232,8... | collective-permute-start | bytes 294920 | tf_op jit(solution)/shard_map/ppermute | solution.py:459
  31.1 9.5 %collective-permute-start.5 = (bf16[48,2,512]{2,1,0:T(2,128)(2,1)S(1)}, bf16[48,2,512]{2,1,0:T(2,128)(2,1)S(1)}, u32[]{:S(2)}, u32[]{:S(2)}) collective-permute-start(bf16[48,2,512]{2,1,0:T(2,128)(2,1)S(1)} %get-tuple-element.25), channel_id=1, source_target_pairs={{63,0},{224,1},{33,2},{226,3},{35,4},{228,5},{37,6},{230,7},{39,8}... | collective-permute-start | bytes 294920 | tf_op jit(solution)/shard_map/ppermute | solution.py:459

commit v4 on v3

--- a/solution.py
+++ b/solution.py
@@ -46,6 +46,20 @@
     return m + parity * (1 - 2 * m)
 
 
+def turned(window_row, lats):
+    return (window_row % lats + lats) % lats // (lats // 2)
+
+
+def own_turned(lats):
+    return turned(lax.axis_index("lat") - column_parity(), lats)
+
+
+def piece_cut(m, n, lats):
+    target = swapped(n, column_parity())
+    window_row = lax.axis_index("lat") - (1 - target if m else target)
+    return swapped(1 - m, target), swapped(1 - n, turned(window_row, lats))
+
+
 def gather_quadrants(refs, base, scratch, parity):
     for q, ref in enumerate(refs):
         m, qc = divmod(q, 2)
@@ -102,7 +116,7 @@
 def mask_bias(refs, lats, parity):
     token = lax.broadcasted_iota(jnp.int32, (1, WIDE), 1)
     quadrant, r, c, level = token_place(token)
-    lane = HN * (1 - quadrant % 2) + c
+    lane = HN * swapped(1 - quadrant % 2, own_turned(lats)) + c
     hot = lax.broadcasted_iota(jnp.int32, (128, WIDE), 0) == lane
     rows = jnp.concatenate([ref[CLASS_AT + r, :, :128].astype(f32) for ref in refs for r in range(HL)], axis=0)
     spread = dot(rows.astype(bf16), hot.astype(f32).astype(bf16))
@@ -185,7 +199,7 @@
 
 
 def pack_kernel(
-    tokens_hbm, cotangent_hbm, coarse_hbm, classes_hbm, o0, o1, o2, o3,
+    lats, tokens_hbm, cotangent_hbm, coarse_hbm, classes_hbm, o0, o1, o2, o3,
     tokens, cotangent, coarse, classes, buffers, in_sems, out_sems,
 ):
     arrivals = [
@@ -200,12 +214,10 @@
     for copy in arrivals:
         copy.wait()
     departures = []
-    parity = column_parity()
-    for q in (3, 2, 1, 0):
-        m, qc = divmod(q, 2)
-        later = swapped(swapped(1 - m, qc), parity)
-        lat, lon = HL * later, HN * (1 - qc)
-        low_lat, low_lon = (coarse.shape[0] - COARSE_ROWS) * later, COARSE_COLS * (1 - qc)
+    for q in (2, 1, 3, 0):
+        later, right = piece_cut(*divmod(q, 2), lats)
+        lat, lon = HL * later, HN * right
+        low_lat, low_lon = (coarse.shape[0] - COARSE_ROWS) * later, COARSE_COLS * right
         for r in range(HL):
             buffers[q, pl.ds(r * HN, HN)] = tokens[lat + r, pl.ds(lon, HN)]
             buffers[q, pl.ds(COTANGENT_AT + r * HN, HN)] = cotangent[lat + r, pl.ds(lon, HN)]
@@ -222,10 +234,11 @@
         copy.wait()
 
 
-def lookup_kernel(inputs_ref, out_ref, rest_ref, low, high, packed_low, packed_high, parts):
+def lookup_kernel(lats, inputs_ref, out_ref, rest_ref, low, high, packed_low, packed_high, parts):
     token = lax.broadcasted_iota(jnp.int32, (SPAN, 1), 0)
     quadrant, r, c, level = token_place(token)
-    old = level * (WIN_LAT * WIN_LON) + (quadrant // 2 * HL + r) * WIN_LON + quadrant % 2 * HN + c
+    right = swapped(quadrant % 2, own_turned(lats))
+    old = level * (WIN_LAT * WIN_LON) + (quadrant // 2 * HL + r) * WIN_LON + right * HN + c
     order = (lax.broadcasted_iota(jnp.int32, (SPAN, SPAN), 1) == old).astype(f32).astype(bf16)
     index = inputs_ref[:SPAN, :SPAN].astype(jnp.int32)
     rest = SPAN - 128
@@ -294,7 +307,7 @@
                 )
 
 
-def lookup(relative_index, encoder_table, decoder_table):
+def lookup(lats, relative_index, encoder_table, decoder_table):
     blocks = -(-encoder_table.shape[1] // WIDE)
 
     def widen(rows):
@@ -302,7 +315,7 @@
 
     inputs = jnp.concatenate([widen(relative_index.astype(f32)), widen(encoder_table), widen(decoder_table)], axis=0)
     return pl.pallas_call(
-        lookup_kernel,
+        functools.partial(lookup_kernel, lats),
         out_shape=[jax.ShapeDtypeStruct((2 * HEADS * SPAN, 128), f32)] * 2,
         scratch_shapes=[
             pltpu.VMEM((SPAN, 128), f32),
@@ -334,7 +347,7 @@
 
 
 def main_kernel(
-    lats, b0, b1, b2, b3, bias_main, bias_rest,
+    lats, b0, b2, b1, b3, bias_main, bias_rest,
     e_gain, e_offset, e_bias, e_out_bias, d_gain, d_offset, d_bias, d_out_bias, split_bias,
     e_weight, e_out_weight, d_weight, d_out_weight, split,
     o0, o1, o2, o3,
@@ -395,32 +408,26 @@
     scatter_quadrants(scratch, outs, PAIRS, parity)
 
 
-def home_kernel(h0, h1, h2, h3, decoded, tokens_gradient, coarse_gradient, sems):
-    parity = column_parity()
-    refs = (h0, h1, h2, h3)
+def home_kernel(lats, h0, h2, h1, h3, decoded, tokens_gradient, coarse_gradient, total, sems):
     copies = []
-    for q, ref in enumerate(refs):
-        m, qc = divmod(q, 2)
-        later = swapped(swapped(1 - m, qc), parity)
+    total[...] = jnp.zeros_like(total)
+    for q, ref in enumerate((h0, h1, h2, h3)):
+        later, right = piece_cut(*divmod(q, 2), lats)
         for n, out in enumerate((decoded, tokens_gradient)):
             for r in range(HL):
                 copy = pltpu.make_async_copy(
                     ref.at[pl.ds(PAIRS * n + r * HN, HN)],
-                    out.at[HL * later + r, pl.ds(HN * (1 - qc), HN)],
+                    out.at[HL * later + r, pl.ds(HN * right, HN)],
                     sems.at[len(copies)],
                 )
                 copy.start()
                 copies.append(copy)
-    for qc in range(2):
-        begins = swapped(qc, parity) == 0
-        own, other = refs[qc], refs[2 + qc]
         for half in range(2):
-            for c in range(COARSE_COLS):
-                at = COARSE_AT + POINTS * half + c
-                a0, a1, b0, b1 = (r[at + k].astype(f32) for r in (own, other) for k in (0, COARSE_COLS))
-                rows = (jnp.where(begins, b0, a0), jnp.where(begins, b1 + a0, a1 + b0), jnp.where(begins, a1, b1))
-                for n, row in enumerate(rows):
-                    coarse_gradient[n, (1 - qc) * COARSE_COLS + c, :, pl.ds(D * half, D)] = row.astype(bf16)
+            for r in range(COARSE_ROWS):
+                for c in range(COARSE_COLS):
+                    part = ref[COARSE_AT + POINTS * half + r * COARSE_COLS + c].astype(f32)
+                    total[later + r, COARSE_COLS * right + c, :, pl.ds(D * half, D)] += part
+    coarse_gradient[...] = total[...].astype(bf16)
     for copy in copies:
         copy.wait()
 
@@ -445,18 +452,19 @@
 
 
 def exchange(pieces, lats, lons, back):
-    out = [pieces[0]]
-    for q in range(1, 4):
-        m, qc = divmod(q, 2)
+    out = list(pieces)
+    for q in (2, 1, 3):
+        m, n = divmod(q, 2)
         pairs = []
         for i in range(lats):
             for j in range(lons):
-                to = (j - qc) % lons
-                step = m * (1 if to % 2 else -1)
-                pairs.append((i * lons + j, (i + step) % lats * lons + to))
+                target = (j + n) % 2
+                turn = turned(i - (1 - target if m else target), lats)
+                to = (i + m * (2 * target - 1)) % lats, (j + n * (2 * turn - 1)) % lons
+                pairs.append((i * lons + j, to[0] * lons + to[1]))
         if back:
             pairs = [(target, source) for source, target in pairs]
-        out.append(lax.ppermute(pieces[q], ("lat", "lon"), pairs))
+        out[q] = lax.ppermute(pieces[q], ("lat", "lon"), pairs)
     return out
 
 
@@ -474,7 +482,7 @@
 
     s = jax.ShapeDtypeStruct
     packed = call(
-        pack_kernel,
+        functools.partial(pack_kernel, lats),
         "pack",
         [
             jnp.transpose(tokens, (1, 2, 0, 3)),
@@ -498,13 +506,13 @@
         60,
     )
     parts = exchange(packed, lats, lons, False)
-    biases = lookup(relative_index, encoder_table, decoder_table)
+    biases = lookup(lats, relative_index, encoder_table, decoder_table)
     points = 4 * LEVELS * POINTS
     outs = call(
         functools.partial(main_kernel, lats),
         "main",
         [
-            *parts, *biases,
+            parts[0], parts[2], parts[1], parts[3], *biases,
             row(encoder_gain), row(encoder_offset), encoder_projection_bias, row(encoder_output_bias),
             row(decoder_gain), row(decoder_offset), decoder_projection_bias, row(decoder_output_bias),
             row(split_bias),
@@ -528,11 +536,14 @@
     grid = s((WIN_LAT, WIN_LON, LEVELS, D), bf16)
     low = s((WIN_LAT // 2, WIN_LON // 2, LEVELS, 2 * D), bf16)
     results = call(
-        home_kernel,
+        functools.partial(home_kernel, lats),
         "home",
-        home,
+        [home[0], home[2], home[1], home[3]],
         [grid, grid, low],
-        [pltpu.SemaphoreType.DMA((4 * 2 * HL,))],
+        [
+            pltpu.VMEM((WIN_LAT // 2, WIN_LON // 2, LEVELS, 2 * D), f32),
+            pltpu.SemaphoreType.DMA((4 * 2 * HL,)),
+        ],
         1_000_000,
         None,
         [ANY, ANY, VM],

time: 42.8 us -> 41.9 us (0.979)
  waiting for transfers between devices: 10.4 us -> 8.83 us
  starting transfers between devices: 12.1 us -> 13 us
    ppermute x6, waiting for transfers between devices: 10.4 us -> 8.83 us  [exchange(): out[q] = lax.ppermute(pieces[q], ('lat', 'lon'), pairs)]
    ppermute x6, starting transfers between devices: 12.1 us -> 13 us  [exchange(): out[q] = lax.ppermute(pieces[q], ('lat', 'lon'), pairs)]
where the time goes in v4:
time: 41.9 us; the launch traced here: 41.7 us
  Pallas kernels  17 us (41%)
  starting transfers between devices  13 us (31%)
  waiting for transfers between devices  8.83 us (21%)
  other arithmetic  1.71 us (4%)
  between operations  1.06 us (3%)
    pallas_call x3, Pallas kernels, call(): pl.pallas_call(kernel, out_shape=outs, in_specs=in_specs or [VM] * len(in...  13 us
    ppermute x6, starting transfers between devices, exchange(): out[q] = lax.ppermute(pieces[q], ('lat', 'lon'), pairs)  13 us
    ppermute x6, waiting for transfers between devices, exchange(): out[q] = lax.ppermute(pieces[q], ('lat', 'lon'), pairs)  8.83 us
    pallas_call x1, Pallas kernels, lookup(): pl.pallas_call(functools.partial(lookup_kernel, lats), out_shape=[jax.Sha...  3.96 us
    convert_element_type x1, other arithmetic, lookup(): relative_index.astype(f32)  0.92 us
  transfers between devices with their start and end apart: 6, of which 4 were waited for; matrix products, arithmetic and copies ran while one was open for 4% of the time, Pallas kernels for 9%

profile of v4, /device:TPU:24, one launch (start us, length us, event | category | flops | bytes accessed | tf_op | source)
XLA Modules:
  0.0 41.7 jit_solution(2428686716756367343)
XLA Ops:
  0.6 1.9 %pack.1 = (bf16[51,2,512]{2,1,0:T(2,128)(2,1)}, bf16[51,2,512]{2,1,0:T(2,128)(2,1)}, bf16[51,2,512]{2,1,0:T(2,128)(2,1)}, bf16[51,2,512]{2,1,0:T(2,128)(2,1)}) custom-call(bf16[6,12,2,512]{3,2,1,0:T(2,128)(2,1)} %bitcast.21, bf16[6,12,2,512]{3,2,1,0:T(2,128)(2,1)} %bitcast.22, bf16[3,6,2,1024]{3,2,1,0:T(2,128)(2,1)} %bitcast.23, s32[6,2,12]{2,1,0:T(2,128)} %bitcast.24), custom_call_target="tpu_custom_call" | custom-call | flops 100000000 | bytes 100000 | tf_op jit(solution)/shard_map/pack/pallas_call | solution.py:442
  2.5 0.8 %collective-permute-start = (bf16[51,2,512]{2,1,0:T(2,128)(2,1)}, bf16[51,2,512]{2,1,0:T(2,128)(2,1)S(1)}, u32[]{:S(2)}, u32[]{:S(2)}) collective-permute-start(bf16[51,2,512]{2,1,0:T(2,128)(2,1)} %get-tuple-element.17), channel_id=1, source_target_pairs={{0,224},{1,33},{2,226},{3,35},{4,228},{5,37},{6,230},{7,39},{8,232... | collective-permute-start | bytes 313352 | tf_op jit(solution)/shard_map/ppermute | solution.py:467
  3.3 7.6 %collective-permute-start.1 = (bf16[51,2,512]{2,1,0:T(2,128)(2,1)}, bf16[51,2,512]{2,1,0:T(2,128)(2,1)S(1)}, u32[]{:S(2)}, u32[]{:S(2)}) collective-permute-start(bf16[51,2,512]{2,1,0:T(2,128)(2,1)} %get-tuple-element.18), channel_id=1, source_target_pairs={{0,1},{1,0},{2,3},{3,2},{4,5},{5,4},{6,7},{7,6},{8,9},{9,8},{10,11... | collective-permute-start | bytes 313352 | tf_op jit(solution)/shard_map/ppermute | solution.py:467
  10.9 0.3 collective-permute-start.2
  11.2 0.9 %convert_element_type.8 = f32[144,144]{1,0:T(8,128)S(1)} convert(s32[144,144]{1,0:T(8,128)} %param.25) | non-fusion elementwise | flops 20736 | bytes 165888 | tf_op jit(solution)/shard_map/convert_element_type | solution.py:316
  12.1 0.8 %select_maximum_fusion.inputs_ref = f32[160,768]{1,0:T(8,128)S(1)} fusion(f32[8,759]{1,0:T(8,128)} %param.39, f32[8,759]{1,0:T(8,128)} %param.32, f32[144,144]{1,0:T(8,128)S(1)} %convert_element_type.8), kind=kLoop, calls=%fused_computation.2 | loop fusion | flops 1228800 | bytes 623040 | tf_op jit(solution)/shard_map/concatenate | solution.py:316
  12.9 0.0 copy-start
  12.9 0.0 copy-start.1
  13.0 0.0 copy-start.2
  13.0 0.0 copy-start.5
  13.0 0.0 copy-start.6
  13.0 0.0 copy-start.9
  13.1 0.0 copy-start.10
  13.1 0.0 copy-start.13
  13.1 0.0 copy-start.14
  13.1 4.0 %lookup.1 = (f32[2304,128]{1,0:T(8,128)S(1)}, f32[2304,128]{1,0:T(8,128)S(1)}) custom-call(f32[160,768]{1,0:T(8,128)S(1)} %select_maximum_fusion.inputs_ref), custom_call_target="tpu_custom_call" | custom-call | flops 3000000000 | bytes 4000000 | tf_op jit(solution)/shard_map/lookup/pallas_call | solution.py:317
  17.1 0.2 collective-permute-done.2.b3
  17.5 9.6 %main.1 = (bf16[48,2,512]{2,1,0:T(2,128)(2,1)S(1)}, bf16[48,2,512]{2,1,0:T(2,128)(2,1)S(1)}, bf16[48,2,512]{2,1,0:T(2,128)(2,1)S(1)}, bf16[48,2,512]{2,1,0:T(2,128)(2,1)S(1)}) custom-call(bf16[51,2,512]{2,1,0:T(2,128)(2,1)S(1)} %copy-done.5, bf16[51,2,512]{2,1,0:T(2,128)(2,1)S(1)} %collective-permute-done.b2, ...), custom_call_target="tpu_custom_call" | custom-call | flops 8000000000 | bytes 8000000 | tf_op jit(solution)/shard_map/main/pallas_call | solution.py:442
  27.1 3.4 %collective-permute-start.3 = (bf16[48,2,512]{2,1,0:T(2,128)(2,1)S(1)}, bf16[48,2,512]{2,1,0:T(2,128)(2,1)S(1)}, u32[]{:S(2)}, u32[]{:S(2)}) collective-permute-start(bf16[48,2,512]{2,1,0:T(2,128)(2,1)S(1)} %get-tuple-element.23), channel_id=1, source_target_pairs={{224,0},{33,1},{226,2},{35,3},{228,4},{37,5},{230,6},{39,7},{232,8... | collective-permute-start | bytes 294920 | tf_op jit(solution)/shard_map/ppermute | solution.py:467
  30.6 0.9 %collective-permute-start.5 = (bf16[48,2,512]{2,1,0:T(2,128)(2,1)S(1)}, bf16[48,2,512]{2,1,0:T(2,128)(2,1)S(1)}, u32[]{:S(2)}, u32[]{:S(2)}) collective-permute-start(bf16[48,2,512]{2,1,0:T(2,128)(2,1)S(1)} %get-tuple-element.25), channel_id=1, source_target_pairs={{63,0},{226,1},{33,2},{228,3},{35,4},{230,5},{37,6},{232,7},{39,8}... | collective-permute-start | bytes 294920 | tf_op jit(solution)/shard_map/ppermute | solution.py:467
  31.4 1.3 %collective-permute-done.3.h2 = bf16[48,2,512]{2,1,0:T(2,128)(2,1)S(1)} collective-permute-done((bf16[48,2,512]{2,1,0:T(2,128)(2,1)S(1)}, bf16[48,2,512]{2,1,0:T(2,128)(2,1)S(1)}, u32[]{:S(2)}, u32[]{:S(2)}) %collective-permute-start.3) | collective-permute-done | bytes 98336 | tf_op jit(solution)/shard_map/ppermute | solution.py:467
  32.8 5.4 %collective-permute-done.4.h1 = bf16[48,2,512]{2,1,0:T(2,128)(2,1)S(1)} collective-permute-done((bf16[48,2,512]{2,1,0:T(2,128)(2,1)S(1)}, bf16[48,2,512]{2,1,0:T(2,128)(2,1)S(1)}, u32[]{:S(2)}, u32[]{:S(2)}) %collective-permute-start.4) | collective-permute-done | bytes 98336 | tf_op jit(solution)/shard_map/ppermute | solution.py:467
  38.2 1.8 %collective-permute-done.5.h3 = bf16[48,2,512]{2,1,0:T(2,128)(2,1)S(1)} collective-permute-done((bf16[48,2,512]{2,1,0:T(2,128)(2,1)S(1)}, bf16[48,2,512]{2,1,0:T(2,128)(2,1)S(1)}, u32[]{:S(2)}, u32[]{:S(2)}) %collective-permute-start.5) | collective-permute-done | bytes 98336 | tf_op jit(solution)/shard_map/ppermute | solution.py:467
  40.0 1.6 %home.1 = (bf16[6,12,2,512]{3,2,1,0:T(2,128)(2,1)}, bf16[6,12,2,512]{3,2,1,0:T(2,128)(2,1)}, bf16[3,6,2,1024]{3,2,1,0:T(2,128)(2,1)}) custom-call(bf16[48,2,512]{2,1,0:T(2,128)(2,1)S(1)} %get-tuple-element.22.h0, bf16[48,2,512]{2,1,0:T(2,128)(2,1)S(1)} %collective-permute-done.3.h2, bf16[48,2,512]{2,1,0:T(2,128)(2,1)S(1)} %collective-permute-done.4.h1, ...), custom_call_target="tpu_custom_call" | custom-call | flops 1000000 | bytes 1000 | tf_op jit(solution)/shard_map/home/pallas_call | solution.py:442
  (24 shorter events, 0.1 us)
Async XLA Ops:
  2.5 14.6 %collective-permute-start = (bf16[51,2,512]{2,1,0:T(2,128)(2,1)}, bf16[51,2,512]{2,1,0:T(2,128)(2,1)S(1)}, u32[]{:S(2)}, u32[]{:S(2)}) collective-permute-start(bf16[51,2,512]{2,1,0:T(2,128)(2,1)} %get-tuple-element.17), channel_id=1, source_target_pairs={{0,224},{1,33},{2,226},{3,35},{4,228},{5,37},{6,230},{7,39},{8,232... | collective-permute-start | bytes 313352 | tf_op jit(solution)/shard_map/ppermute | solution.py:467
  3.3 13.8 %collective-permute-start.1 = (bf16[51,2,512]{2,1,0:T(2,128)(2,1)}, bf16[51,2,512]{2,1,0:T(2,128)(2,1)S(1)}, u32[]{:S(2)}, u32[]{:S(2)}) collective-permute-start(bf16[51,2,512]{2,1,0:T(2,128)(2,1)} %get-tuple-element.18), channel_id=1, source_target_pairs={{0,1},{1,0},{2,3},{3,2},{4,5},{5,4},{6,7},{7,6},{8,9},{9,8},{10,11... | collective-permute-start | bytes 313352 | tf_op jit(solution)/shard_map/ppermute | solution.py:467
  10.9 6.4 %collective-permute-start.2 = (bf16[51,2,512]{2,1,0:T(2,128)(2,1)}, bf16[51,2,512]{2,1,0:T(2,128)(2,1)S(1)}, u32[]{:S(2)}, u32[]{:S(2)}) collective-permute-start(bf16[51,2,512]{2,1,0:T(2,128)(2,1)} %get-tuple-element.19), channel_id=1, source_target_pairs={{0,63},{1,226},{2,33},{3,228},{4,35},{5,230},{6,37},{7,232},{8,39}... | collective-permute-start | bytes 313352 | tf_op jit(solution)/shard_map/ppermute | solution.py:467
  12.9 4.4 %copy-start = (bf16[1024,2048]{1,0:T(8,128)(2,1)S(1)}, bf16[1024,2048]{1,0:T(8,128)(2,1)}, u32[]{:S(2)}) copy-start(bf16[1024,2048]{1,0:T(8,128)(2,1)} %split.1) | copy-start | bytes 12582916
  12.9 4.4 %copy-start.1 = (bf16[512,1536]{1,0:T(8,128)(2,1)S(1)}, bf16[512,1536]{1,0:T(8,128)(2,1)}, u32[]{:S(2)}) copy-start(bf16[512,1536]{1,0:T(8,128)(2,1)} %e_weight.1) | copy-start | bytes 4718596
  13.0 4.4 %copy-start.2 = (bf16[512,1536]{1,0:T(8,128)(2,1)S(1)}, bf16[512,1536]{1,0:T(8,128)(2,1)}, u32[]{:S(2)}) copy-start(bf16[512,1536]{1,0:T(8,128)(2,1)} %d_weight.1) | copy-start | bytes 4718596
  13.0 4.4 %copy-start.3 = (bf16[512,512]{1,0:T(8,128)(2,1)S(1)}, bf16[512,512]{1,0:T(8,128)(2,1)}, u32[]{:S(2)}) copy-start(bf16[512,512]{1,0:T(8,128)(2,1)} %e_out_weight.1) | copy-start | bytes 1572868
  13.0 4.4 %copy-start.4 = (bf16[512,512]{1,0:T(8,128)(2,1)S(1)}, bf16[512,512]{1,0:T(8,128)(2,1)}, u32[]{:S(2)}) copy-start(bf16[512,512]{1,0:T(8,128)(2,1)} %d_out_weight.1) | copy-start | bytes 1572868
  13.0 4.4 %copy-start.5 = (bf16[51,2,512]{2,1,0:T(2,128)(2,1)S(1)}, bf16[51,2,512]{2,1,0:T(2,128)(2,1)}, u32[]{:S(2)}) copy-start(bf16[51,2,512]{2,1,0:T(2,128)(2,1)} %get-tuple-element.16.b0) | copy-start | bytes 313348
  13.0 4.4 %copy-start.6 = (f32[1536]{0:T(1024)S(1)}, f32[1536]{0:T(1024)}, u32[]{:S(2)}) copy-start(f32[1536]{0:T(1024)} %e_bias.1) | copy-start | bytes 18436
  13.0 4.4 %copy-start.7 = (f32[1536]{0:T(1024)S(1)}, f32[1536]{0:T(1024)}, u32[]{:S(2)}) copy-start(f32[1536]{0:T(1024)} %d_bias.1) | copy-start | bytes 18436
  13.0 4.4 %copy-start.8 = (f32[2048]{0:T(1024)S(1)}, f32[2048]{0:T(1024)}, u32[]{:S(2)}) copy-start(f32[2048]{0:T(1024)} %param.41) | copy-start | bytes 24580
  13.0 4.4 %copy-start.9 = (f32[512]{0:T(512)S(1)}, f32[512]{0:T(512)}, u32[]{:S(2)}) copy-start(f32[512]{0:T(512)} %param.26) | copy-start | bytes 6148
  13.1 4.4 %copy-start.10 = (f32[512]{0:T(512)S(1)}, f32[512]{0:T(512)}, u32[]{:S(2)}) copy-start(f32[512]{0:T(512)} %param.27) | copy-start | bytes 6148
  13.1 4.4 %copy-start.11 = (f32[512]{0:T(512)S(1)}, f32[512]{0:T(512)}, u32[]{:S(2)}) copy-start(f32[512]{0:T(512)} %param.31) | copy-start | bytes 6148
  13.1 4.4 %copy-start.12 = (f32[512]{0:T(512)S(1)}, f32[512]{0:T(512)}, u32[]{:S(2)}) copy-start(f32[512]{0:T(512)} %param.33) | copy-start | bytes 6148
  13.1 4.4 %copy-start.13 = (f32[512]{0:T(512)S(1)}, f32[512]{0:T(512)}, u32[]{:S(2)}) copy-start(f32[512]{0:T(512)} %param.34) | copy-start | bytes 6148
  13.1 4.4 %copy-start.14 = (f32[512]{0:T(512)S(1)}, f32[512]{0:T(512)}, u32[]{:S(2)}) copy-start(f32[512]{0:T(512)} %param.38) | copy-start | bytes 6148
  27.1 5.7 %collective-permute-start.3 = (bf16[48,2,512]{2,1,0:T(2,128)(2,1)S(1)}, bf16[48,2,512]{2,1,0:T(2,128)(2,1)S(1)}, u32[]{:S(2)}, u32[]{:S(2)}) collective-permute-start(bf16[48,2,512]{2,1,0:T(2,128)(2,1)S(1)} %get-tuple-element.23), channel_id=1, source_target_pairs={{224,0},{33,1},{226,2},{35,3},{228,4},{37,5},{230,6},{39,7},{232,8... | collective-permute-start | bytes 294920 | tf_op jit(solution)/shard_map/ppermute | solution.py:467
  30.5 7.7 %collective-permute-start.4 = (bf16[48,2,512]{2,1,0:T(2,128)(2,1)S(1)}, bf16[48,2,512]{2,1,0:T(2,128)(2,1)S(1)}, u32[]{:S(2)}, u32[]{:S(2)}) collective-permute-start(bf16[48,2,512]{2,1,0:T(2,128)(2,1)S(1)} %get-tuple-element.24), channel_id=1, source_target_pairs={{1,0},{0,1},{3,2},{2,3},{5,4},{4,5},{7,6},{6,7},{9,8},{8,9},{11,10... | collective-permute-start | bytes 294920 | tf_op jit(solution)/shard_map/ppermute | solution.py:467
  30.6 9.5 %collective-permute-start.5 = (bf16[48,2,512]{2,1,0:T(2,128)(2,1)S(1)}, bf16[48,2,512]{2,1,0:T(2,128)(2,1)S(1)}, u32[]{:S(2)}, u32[]{:S(2)}) collective-permute-start(bf16[48,2,512]{2,1,0:T(2,128)(2,1)S(1)} %get-tuple-element.25), channel_id=1, source_target_pairs={{63,0},{226,1},{33,2},{228,3},{35,4},{230,5},{37,6},{232,7},{39,8}... | collective-permute-start | bytes 294920 | tf_op jit(solution)/shard_map/ppermute | solution.py:467

commit v5 on v4

--- a/solution.py
+++ b/solution.py
@@ -15,6 +15,8 @@
 D = 512
 HEAD = D // HEADS
 WIDE = 256
+FIRST = 128
+REST = SPAN - FIRST
 HL, HN = WIN_LAT // 2, WIN_LON // 2
 PAIRS = HL * HN
 GROUP = 4
@@ -96,43 +98,49 @@
     return centred * rstd, rstd
 
 
-def head_masks(dtype):
-    lane = lax.broadcasted_iota(jnp.int32, (1, GROUP * HEAD), 1) // HEAD
-    return [(lane == h).astype(dtype) for h in range(GROUP)]
-
-
-def stack_heads(x):
-    return jnp.concatenate([x * m for m in head_masks(x.dtype)], axis=0)
-
-
-def merge_heads(y):
-    masks = head_masks(f32)
-    total = y[:SPAN] * masks[0]
-    for h in range(1, GROUP):
-        total = total + y[h * SPAN : (h + 1) * SPAN] * masks[h]
+def head_of(lanes):
+    return lax.broadcasted_iota(jnp.int32, (1, lanes), 1) // HEAD
+
+
+def stack(x):
+    lanes = x.shape[1]
+    return jnp.concatenate([x * (head_of(lanes) == h).astype(x.dtype) for h in range(lanes // HEAD)], axis=0)
+
+
+def unstack(y):
+    lanes = y.shape[1]
+    rows = y.shape[0] // (lanes // HEAD)
+    total = y[:rows]
+    for h in range(1, lanes // HEAD):
+        total = jnp.where(head_of(lanes) == h, y[h * rows : (h + 1) * rows], total)
     return total
 
 
+def main_lanes(g):
+    return pl.ds(g * GROUP * HEAD, GROUP * HEAD)
+
+
+def columns_of(g):
+    return slice(g * GROUP * FIRST, (g + 1) * GROUP * FIRST)
+
+
 def mask_bias(refs, lats, parity):
-    token = lax.broadcasted_iota(jnp.int32, (1, WIDE), 1)
+    lane = lax.broadcasted_iota(jnp.int32, (1, WIDE + FIRST), 1)
+    token = jnp.where(lane < WIDE, lane, FIRST + lane % REST)
     quadrant, r, c, level = token_place(token)
-    lane = HN * swapped(1 - quadrant % 2, own_turned(lats)) + c
-    hot = lax.broadcasted_iota(jnp.int32, (128, WIDE), 0) == lane
+    place = HN * swapped(1 - quadrant % 2, own_turned(lats)) + c
+    hot = lax.broadcasted_iota(jnp.int32, (128, WIDE + FIRST), 0) == place
     rows = jnp.concatenate([ref[CLASS_AT + r, :, :128].astype(f32) for ref in refs for r in range(HL)], axis=0)
     spread = dot(rows.astype(bf16), hot.astype(f32).astype(bf16))
     piece = swapped(quadrant // 2, parity) * 2 + quadrant % 2
-    mine = lax.broadcasted_iota(jnp.int32, (4 * HL * LEVELS, WIDE), 0) == (piece * HL + r) * LEVELS + level
+    row = lax.broadcasted_iota(jnp.int32, (4 * HL * LEVELS, WIDE + FIRST), 0)
+    mine = row == (piece * HL + r) * LEVELS + level
     last = lax.axis_index("lat") == jnp.where(parity == 0, lats - 1, 0)
     seam = jnp.where(last, (quadrant // 2).astype(f32), 0.0)
     label = 2.0 * jnp.sum(jnp.where(mine, spread, 0.0), axis=0, keepdims=True) + seam
-    label = jnp.where(token < SPAN, label, 9.0)
     eye = lax.broadcasted_iota(jnp.int32, (SPAN, WIDE), 0) == lax.broadcasted_iota(jnp.int32, (SPAN, WIDE), 1)
-    column = jnp.sum(jnp.where(eye, label, 0.0), axis=1, keepdims=True)
-    return jnp.where(column == label, 0.0, BLANK)
-
-
-def pad_keys(x):
-    return jnp.concatenate([x, jnp.zeros((WIDE - SPAN, x.shape[1]), x.dtype)], axis=0)
+    column = jnp.sum(jnp.where(eye, label[:, :WIDE], 0.0), axis=1, keepdims=True)
+    return [jnp.where(column == queries, 0.0, BLANK) for queries in (label[:, :FIRST], label[:, WIDE:])]
 
 
 def block_forward(x, blank, bias_of, gain, offset, weight, bias, out_weight, out_bias, qkv_ref, probs_ref):
@@ -141,43 +149,51 @@
     queries = (dot(normed, weight[:, :D]) + bias[:, :D]).astype(bf16) * jnp.array(HEAD**-0.5, bf16)
     qkv_ref[:, :D] = queries
     qkv_ref[:, D:] = (dot(normed, weight[:, D:]) + bias[:, D:]).astype(bf16)
-    mixed = []
+    keys, values = qkv_ref[:, D : 2 * D], qkv_ref[:, 2 * D :]
+
+    def soften(s, tile):
+        s = s + bias_of(tile) + blank[tile // HEADS]
+        e = jnp.exp(s - jnp.max(s, axis=0, keepdims=True))
+        p = e * (1.0 / jnp.sum(e, axis=0, keepdims=True))
+        probs_ref[:, pl.ds(tile * FIRST, FIRST)] = p.astype(bf16)
+
     for g in range(HEADS // GROUP):
-        lanes = pl.ds(g * GROUP * HEAD, GROUP * HEAD)
-        q4 = stack_heads(qkv_ref[:, pl.ds(g * 256, 256)])
-        k4 = pad_keys(qkv_ref[:, pl.ds(D + g * 256, 256)])
-        v4 = pad_keys(qkv_ref[:, pl.ds(2 * D + g * 256, 256)])
-        scores = dot_nt(q4, k4)
+        scores = dot_nt(keys[:, g * 256 : (g + 1) * 256], stack(qkv_ref[:FIRST, main_lanes(g)]))
         for h in range(GROUP):
-            s = scores[h * SPAN : (h + 1) * SPAN] + bias_of(g * GROUP + h) + blank
-            e = jnp.exp(s - jnp.max(s, axis=-1, keepdims=True))
-            p = e * (1.0 / jnp.sum(e, axis=-1, keepdims=True))
-            probs_ref[pl.ds((g * GROUP + h) * SPAN, SPAN), :] = p.astype(bf16)
-        p4 = probs_ref[pl.ds(g * GROUP * SPAN, GROUP * SPAN), :]
-        mixed.append(merge_heads(dot(p4, v4)))
-    heads_out = jnp.concatenate(mixed, axis=1).astype(bf16)
+            soften(scores[:, h * FIRST : (h + 1) * FIRST], g * GROUP + h)
+    soften(dot_nt(keys, stack(qkv_ref[FIRST:, :D])), HEADS)
+    first = [
+        unstack(dot_tn(probs_ref[:, columns_of(g)], values[:, g * 256 : (g + 1) * 256])) for g in range(HEADS // GROUP)
+    ]
+    rest = unstack(dot_tn(probs_ref[:, HEADS * FIRST :], values))
+    heads_out = jnp.concatenate([jnp.concatenate(first, axis=1).astype(bf16), rest.astype(bf16)], axis=0)
     return x + dot(heads_out, out_weight) + out_bias
 
 
 def block_backward(grad, x, gain, weight, out_weight, qkv_ref, probs_ref, dqkv_ref):
     dheads = dot_nt(grad, out_weight).astype(bf16)
+    keys, values = qkv_ref[:, D : 2 * D], qkv_ref[:, 2 * D :]
+
+    def harden(dprobs, columns):
+        pf = probs_ref[:, columns].astype(f32)
+        weighted = pf * dprobs
+        return (weighted - pf * jnp.sum(weighted, axis=0, keepdims=True)).astype(bf16)
+
+    last = slice(HEADS * FIRST, HEADS * FIRST + HEADS * REST)
+    q_rest, do_rest = stack(qkv_ref[FIRST:, :D]), stack(dheads[FIRST:])
+    ds_rest = harden(dot_nt(values, do_rest), last)
+    dqkv_ref[FIRST:, :D] = (unstack(dot_tn(ds_rest, keys)) * HEAD**-0.5).astype(bf16)
+    dk_rest, dv_rest = dot(ds_rest, q_rest), dot(probs_ref[:, last], do_rest)
     for g in range(HEADS // GROUP):
-        q4 = stack_heads(qkv_ref[:, pl.ds(g * 256, 256)])
-        k4 = pad_keys(qkv_ref[:, pl.ds(D + g * 256, 256)])
-        v4 = pad_keys(qkv_ref[:, pl.ds(2 * D + g * 256, 256)])
-        do4 = stack_heads(dheads[:, g * 256 : (g + 1) * 256])
-        p4 = probs_ref[pl.ds(g * GROUP * SPAN, GROUP * SPAN), :]
-        dprobs = dot_nt(do4, v4)
-        pf = p4.astype(f32)
-        weighted = pf * dprobs
-        ds = (weighted - pf * jnp.sum(weighted, axis=-1, keepdims=True)).astype(bf16)
-        dq = merge_heads(dot(ds, k4)) * HEAD**-0.5
-        dk = dot_tn(ds[:, :SPAN], q4)
-        dv = dot_tn(p4[:, :SPAN], do4)
-        dqkv_ref[:, pl.ds(g * 256, 256)] = dq.astype(bf16)
-        dqkv_ref[:, pl.ds(D + g * 256, 256)] = dk.astype(bf16)
+        lanes = slice(g * 256, (g + 1) * 256)
+        q4, do4 = stack(qkv_ref[:FIRST, main_lanes(g)]), stack(dheads[:FIRST, lanes])
+        ds = harden(dot_nt(values[:, lanes], do4), columns_of(g))
+        dq = unstack(dot_tn(ds, keys[:, lanes])) * HEAD**-0.5
+        dqkv_ref[:FIRST, lanes] = dq.astype(bf16)
+        dqkv_ref[:, pl.ds(D + g * 256, 256)] = (dot(ds, q4) + dk_rest[:, lanes]).astype(bf16)
+        dv = dot(probs_ref[:, columns_of(g)], do4) + dv_rest[:, lanes]
         dqkv_ref[:, pl.ds(2 * D + g * 256, 256)] = dv.astype(bf16)
-    dnormed = dot_nt(dqkv_ref[...], weight).astype(bf16).astype(f32)
+    dnormed = dot_nt(dqkv_ref[...], weight)
     xhat, rstd = normalise(x)
     dxhat = dnormed * gain
     dx = rstd * (
@@ -185,7 +201,7 @@
         - jnp.mean(dxhat, axis=-1, keepdims=True)
         - xhat * jnp.mean(dxhat * xhat, axis=-1, keepdims=True)
     )
-    return grad.astype(f32) + dx.astype(bf16).astype(f32)
+    return grad.astype(f32) + dx
 
 
 COARSE_ROWS, COARSE_COLS = HL // 2 + 1, HN // 2
@@ -234,7 +250,7 @@
         copy.wait()
 
 
-def lookup_kernel(lats, inputs_ref, out_ref, rest_ref, low, high, packed_low, packed_high, parts):
+def lookup_kernel(lats, inputs_ref, out_ref, rest_ref, low, high, packed_low, packed_high, parts, spots):
     token = lax.broadcasted_iota(jnp.int32, (SPAN, 1), 0)
     quadrant, r, c, level = token_place(token)
     right = swapped(quadrant % 2, own_turned(lats))
@@ -250,7 +266,7 @@
         == lax.broadcasted_iota(jnp.int32, (SPAN, WIDE), 0) % rest
     )
     for part, full, packed in ((index % WIDE, low, packed_low), (index // WIDE, high, packed_high)):
-        moved = dot_nt(dot(order, part.astype(f32).astype(bf16)).astype(bf16), order)
+        moved = dot_nt(dot_nt(order, part.astype(f32).astype(bf16)).astype(bf16), order)
         full[...] = moved[:, :128]
         tail = jnp.where(own, dot(moved[:, 128:].astype(bf16), spread), 0.0)
         for g in range(SPAN // rest):
@@ -297,14 +313,27 @@
         for n in range(24):
             two_rows(48 * step + 2 * n)
 
+    block = lax.broadcasted_iota(jnp.int32, (HEADS, 128), 1) // rest
+    head = lax.broadcasted_iota(jnp.int32, (HEADS, 128), 0)
     for g in range(SPAN // rest):
         result = look(packed_low[pl.ds(g, 1), :], packed_high[pl.ds(g, 1), :])
-        for n in range(rest):
-            first = n * rest // 128 * 128
+        for first in range(0, WIDE, 128):
             for half in range(2):
-                rest_ref[pl.ds(half * HEADS * SPAN + rest * g + n, HEADS, stride=SPAN), :] = pltpu.roll(
-                    result[half * HEADS : (half + 1) * HEADS, first : first + 128], (first - n * rest) % 128, axis=1
-                )
+                rows = result[half * HEADS : (half + 1) * HEADS, first : first + 128]
+                rows = pltpu.roll(rows, 0, axis=1, stride=rest, stride_axis=0)
+                for n in range(128 // rest):
+                    at = half * HEADS * SPAN + rest * g + first // rest + n
+                    spots[pl.ds(at, HEADS, stride=SPAN), :] = jnp.where(block == (head + n) % HEADS, rows, 0.0)
+    lane = lax.broadcasted_iota(jnp.int32, (8, 128), 1)
+    turn = (lane + rest * lax.broadcasted_iota(jnp.int32, (8, 128), 0)) % 128
+    for half in range(2):
+        for k in range(0, SPAN, 8):
+            total = spots[pl.ds(half * HEADS * SPAN + k, 8), :]
+            for h in range(1, HEADS):
+                total = total + spots[pl.ds((half * HEADS + h) * SPAN + k, 8), :]
+            rest_ref[pl.ds(half * SPAN + k, 8), :] = jnp.take_along_axis(
+                total, turn, axis=1, mode="promise_in_bounds"
+            )
 
 
 def lookup(lats, relative_index, encoder_table, decoder_table):
@@ -316,13 +345,17 @@
     inputs = jnp.concatenate([widen(relative_index.astype(f32)), widen(encoder_table), widen(decoder_table)], axis=0)
     return pl.pallas_call(
         functools.partial(lookup_kernel, lats),
-        out_shape=[jax.ShapeDtypeStruct((2 * HEADS * SPAN, 128), f32)] * 2,
+        out_shape=[
+            jax.ShapeDtypeStruct((2 * HEADS * SPAN, FIRST), f32),
+            jax.ShapeDtypeStruct((2 * SPAN, HEADS * REST), f32),
+        ],
         scratch_shapes=[
             pltpu.VMEM((SPAN, 128), f32),
             pltpu.VMEM((SPAN, 128), f32),
             pltpu.VMEM((16, WIDE), f32),
             pltpu.VMEM((16, WIDE), f32),
             pltpu.VMEM((blocks * 3 * 2 * HEADS, WIDE), bf16),
+            pltpu.VMEM((2 * HEADS * SPAN, 128), f32),
         ],
         compiler_params=pltpu.CompilerParams(vmem_limit_bytes=32 * 2**20),
         cost_estimate=pl.CostEstimate(flops=3_000_000_000, bytes_accessed=4_000_000, transcendentals=0),
@@ -353,9 +386,13 @@
     o0, o1, o2, o3,
     scratch, coarse, fine, tokens, e_qkv, e_probs, d_qkv, d_probs, dqkv,
 ):
-    def bias_rows(h):
-        rows = pl.ds(h * SPAN, SPAN)
-        return jnp.concatenate([bias_main[rows, :], bias_rest[rows, :]], axis=1)
+    def bias_tiles(block):
+        def tile(h):
+            if h == HEADS:
+                return bias_rest[pl.ds(block * SPAN, SPAN), :]
+            return bias_main[pl.ds((block * HEADS + h) * SPAN, SPAN), :]
+
+        return tile
 
     parity = column_parity()
     parts = (b0, b1, b2, b3)
@@ -364,7 +401,7 @@
     tokens[...] = x.astype(bf16)
     blank = mask_bias(parts, lats, parity)
     encoded = block_forward(
-        x, blank, lambda h: bias_rows(h), e_gain[...], e_offset[...], e_weight,
+        x, blank, bias_tiles(0), e_gain[...], e_offset[...], e_weight,
         e_bias[...].reshape(1, -1), e_out_weight[...], e_out_bias[...], e_qkv, e_probs,
     ).astype(bf16)
 
@@ -379,7 +416,7 @@
         scratch[t // (2 * PAIRS), pl.ds(2 * (t % (2 * PAIRS)), 2), :] = fine[pl.ds(2 * at, 2), pl.ds(kind * D, D)]
     x = (encoded.astype(f32) + whole(scratch)).astype(bf16).astype(f32)
     decoded = block_forward(
-        x, blank, lambda h: bias_rows(HEADS + h), d_gain[...], d_offset[...], d_weight,
+        x, blank, bias_tiles(1), d_gain[...], d_offset[...], d_weight,
         d_bias[...].reshape(1, -1), d_out_weight[...], d_out_bias[...], d_qkv, d_probs,
     )
     outs = (o0, o1, o2, o3)
@@ -525,9 +562,9 @@
             pltpu.VMEM((points, 4 * D), f32),
             pltpu.VMEM((SPAN, D), bf16),
             pltpu.VMEM((SPAN, 3 * D), bf16),
-            pltpu.VMEM((HEADS * SPAN, WIDE), bf16),
+            pltpu.VMEM((SPAN, HEADS * SPAN), bf16),
             pltpu.VMEM((SPAN, 3 * D), bf16),
-            pltpu.VMEM((HEADS * SPAN, WIDE), bf16),
+            pltpu.VMEM((SPAN, HEADS * SPAN), bf16),
             pltpu.VMEM((SPAN, 3 * D), bf16),
         ],
         8_000_000_000,

time: 41.9 us -> 41.6 us (level)
  transfers between devices with their start and end apart: 6 -> 6, of which waited for: 4 -> 4; matrix products, arithmetic and copies ran while one was open for 4% -> 4% of each run, Pallas kernels for 9% -> 10%
where the time goes in v5:
time: 41.6 us; the launch traced here: 41.4 us
  Pallas kernels  16.9 us (41%)
  starting transfers between devices  13.1 us (31%)
  waiting for transfers between devices  8.61 us (21%)
  other arithmetic  1.71 us (4%)
  between operations  0.88 us (2%)
    ppermute x6, starting transfers between devices, exchange(): out[q] = lax.ppermute(pieces[q], ('lat', 'lon'), pairs)  13.1 us
    pallas_call x3, Pallas kernels, call(): pl.pallas_call(kernel, out_shape=outs, in_specs=in_specs or [VM] * len(in...  12.8 us
    ppermute x6, waiting for transfers between devices, exchange(): out[q] = lax.ppermute(pieces[q], ('lat', 'lon'), pairs)  8.61 us
    pallas_call x1, Pallas kernels, lookup(): pl.pallas_call(functools.partial(lookup_kernel, lats), out_shape=[jax.Sha...  4.09 us
    convert_element_type x1, other arithmetic, lookup(): relative_index.astype(f32)  0.92 us
  transfers between devices with their start and end apart: 6, of which 4 were waited for; matrix products, arithmetic and copies ran while one was open for 4% of the time, Pallas kernels for 10%

profile of v5, /device:TPU:24, one launch (start us, length us, event | category | flops | bytes accessed | tf_op | source)
XLA Modules:
  0.0 41.4 jit_solution(2815620840691458783)
XLA Ops:
  0.6 1.9 %pack.1 = (bf16[51,2,512]{2,1,0:T(2,128)(2,1)}, bf16[51,2,512]{2,1,0:T(2,128)(2,1)}, bf16[51,2,512]{2,1,0:T(2,128)(2,1)}, bf16[51,2,512]{2,1,0:T(2,128)(2,1)}) custom-call(bf16[6,12,2,512]{3,2,1,0:T(2,128)(2,1)} %bitcast.21, bf16[6,12,2,512]{3,2,1,0:T(2,128)(2,1)} %bitcast.22, bf16[3,6,2,1024]{3,2,1,0:T(2,128)(2,1)} %bitcast.23, s32[6,2,12]{2,1,0:T(2,128)} %bitcast.24), custom_call_target="tpu_custom_call" | custom-call | flops 100000000 | bytes 100000 | tf_op jit(solution)/shard_map/pack/pallas_call | solution.py:479
  2.5 0.8 %collective-permute-start = (bf16[51,2,512]{2,1,0:T(2,128)(2,1)}, bf16[51,2,512]{2,1,0:T(2,128)(2,1)S(1)}, u32[]{:S(2)}, u32[]{:S(2)}) collective-permute-start(bf16[51,2,512]{2,1,0:T(2,128)(2,1)} %get-tuple-element.17), channel_id=1, source_target_pairs={{0,224},{1,33},{2,226},{3,35},{4,228},{5,37},{6,230},{7,39},{8,232... | collective-permute-start | bytes 313352 | tf_op jit(solution)/shard_map/ppermute | solution.py:504
  3.3 7.6 %collective-permute-start.1 = (bf16[51,2,512]{2,1,0:T(2,128)(2,1)}, bf16[51,2,512]{2,1,0:T(2,128)(2,1)S(1)}, u32[]{:S(2)}, u32[]{:S(2)}) collective-permute-start(bf16[51,2,512]{2,1,0:T(2,128)(2,1)} %get-tuple-element.18), channel_id=1, source_target_pairs={{0,1},{1,0},{2,3},{3,2},{4,5},{5,4},{6,7},{7,6},{8,9},{9,8},{10,11... | collective-permute-start | bytes 313352 | tf_op jit(solution)/shard_map/ppermute | solution.py:504
  10.9 0.3 collective-permute-start.2
  11.2 0.9 %convert_element_type.8 = f32[144,144]{1,0:T(8,128)S(1)} convert(s32[144,144]{1,0:T(8,128)} %param.25) | non-fusion elementwise | flops 20736 | bytes 165888 | tf_op jit(solution)/shard_map/convert_element_type | solution.py:345
  12.1 0.8 %select_maximum_fusion.inputs_ref = f32[160,768]{1,0:T(8,128)S(1)} fusion(f32[8,759]{1,0:T(8,128)} %param.39, f32[8,759]{1,0:T(8,128)} %param.32, f32[144,144]{1,0:T(8,128)S(1)} %convert_element_type.8), kind=kLoop, calls=%fused_computation.2 | loop fusion | flops 1228800 | bytes 623040 | tf_op jit(solution)/shard_map/concatenate | solution.py:345
  12.9 0.0 copy-start
  12.9 0.0 copy-start.1
  13.0 0.0 copy-start.2
  13.0 0.0 copy-start.3
  13.0 0.0 copy-start.6
  13.0 0.0 copy-start.7
  13.1 0.0 copy-start.10
  13.1 0.0 copy-start.11
  13.1 0.0 copy-start.14
  13.1 4.1 %lookup.1 = (f32[2304,128]{1,0:T(8,128)S(1)}, f32[288,128]{1,0:T(8,128)S(1)}) custom-call(f32[160,768]{1,0:T(8,128)S(1)} %select_maximum_fusion.inputs_ref), custom_call_target="tpu_custom_call" | custom-call | flops 3000000000 | bytes 4000000 | tf_op jit(solution)/shard_map/lookup/pallas_call | solution.py:346
  17.2 0.1 collective-permute-done.2.b3
  17.5 9.4 %main.1 = (bf16[48,2,512]{2,1,0:T(2,128)(2,1)S(1)}, bf16[48,2,512]{2,1,0:T(2,128)(2,1)S(1)}, bf16[48,2,512]{2,1,0:T(2,128)(2,1)S(1)}, bf16[48,2,512]{2,1,0:T(2,128)(2,1)S(1)}) custom-call(bf16[51,2,512]{2,1,0:T(2,128)(2,1)S(1)} %copy-done.5, bf16[51,2,512]{2,1,0:T(2,128)(2,1)S(1)} %collective-permute-done.b2, ...), custom_call_target="tpu_custom_call" | custom-call | flops 8000000000 | bytes 8000000 | tf_op jit(solution)/shard_map/main/pallas_call | solution.py:479
  26.9 3.4 %collective-permute-start.3 = (bf16[48,2,512]{2,1,0:T(2,128)(2,1)S(1)}, bf16[48,2,512]{2,1,0:T(2,128)(2,1)S(1)}, u32[]{:S(2)}, u32[]{:S(2)}) collective-permute-start(bf16[48,2,512]{2,1,0:T(2,128)(2,1)S(1)} %get-tuple-element.23), channel_id=1, source_target_pairs={{224,0},{33,1},{226,2},{35,3},{228,4},{37,5},{230,6},{39,7},{232,8... | collective-permute-start | bytes 294920 | tf_op jit(solution)/shard_map/ppermute | solution.py:504
  30.3 1.0 %collective-permute-start.5 = (bf16[48,2,512]{2,1,0:T(2,128)(2,1)S(1)}, bf16[48,2,512]{2,1,0:T(2,128)(2,1)S(1)}, u32[]{:S(2)}, u32[]{:S(2)}) collective-permute-start(bf16[48,2,512]{2,1,0:T(2,128)(2,1)S(1)} %get-tuple-element.25), channel_id=1, source_target_pairs={{63,0},{226,1},{33,2},{228,3},{35,4},{230,5},{37,6},{232,7},{39,8}... | collective-permute-start | bytes 294920 | tf_op jit(solution)/shard_map/ppermute | solution.py:504
  31.3 1.2 %collective-permute-done.3.h2 = bf16[48,2,512]{2,1,0:T(2,128)(2,1)S(1)} collective-permute-done((bf16[48,2,512]{2,1,0:T(2,128)(2,1)S(1)}, bf16[48,2,512]{2,1,0:T(2,128)(2,1)S(1)}, u32[]{:S(2)}, u32[]{:S(2)}) %collective-permute-start.3) | collective-permute-done | bytes 98336 | tf_op jit(solution)/shard_map/ppermute | solution.py:504
  32.6 5.4 %collective-permute-done.4.h1 = bf16[48,2,512]{2,1,0:T(2,128)(2,1)S(1)} collective-permute-done((bf16[48,2,512]{2,1,0:T(2,128)(2,1)S(1)}, bf16[48,2,512]{2,1,0:T(2,128)(2,1)S(1)}, u32[]{:S(2)}, u32[]{:S(2)}) %collective-permute-start.4) | collective-permute-done | bytes 98336 | tf_op jit(solution)/shard_map/ppermute | solution.py:504
  38.0 1.8 %collective-permute-done.5.h3 = bf16[48,2,512]{2,1,0:T(2,128)(2,1)S(1)} collective-permute-done((bf16[48,2,512]{2,1,0:T(2,128)(2,1)S(1)}, bf16[48,2,512]{2,1,0:T(2,128)(2,1)S(1)}, u32[]{:S(2)}, u32[]{:S(2)}) %collective-permute-start.5) | collective-permute-done | bytes 98336 | tf_op jit(solution)/shard_map/ppermute | solution.py:504
  39.8 1.6 %home.1 = (bf16[6,12,2,512]{3,2,1,0:T(2,128)(2,1)}, bf16[6,12,2,512]{3,2,1,0:T(2,128)(2,1)}, bf16[3,6,2,1024]{3,2,1,0:T(2,128)(2,1)}) custom-call(bf16[48,2,512]{2,1,0:T(2,128)(2,1)S(1)} %get-tuple-element.22.h0, bf16[48,2,512]{2,1,0:T(2,128)(2,1)S(1)} %collective-permute-done.3.h2, bf16[48,2,512]{2,1,0:T(2,128)(2,1)S(1)} %collective-permute-done.4.h1, ...), custom_call_target="tpu_custom_call" | custom-call | flops 1000000 | bytes 1000 | tf_op jit(solution)/shard_map/home/pallas_call | solution.py:479
  (24 shorter events, 0.1 us)
Async XLA Ops:
  2.5 14.7 %collective-permute-start = (bf16[51,2,512]{2,1,0:T(2,128)(2,1)}, bf16[51,2,512]{2,1,0:T(2,128)(2,1)S(1)}, u32[]{:S(2)}, u32[]{:S(2)}) collective-permute-start(bf16[51,2,512]{2,1,0:T(2,128)(2,1)} %get-tuple-element.17), channel_id=1, source_target_pairs={{0,224},{1,33},{2,226},{3,35},{4,228},{5,37},{6,230},{7,39},{8,232... | collective-permute-start | bytes 313352 | tf_op jit(solution)/shard_map/ppermute | solution.py:504
  3.3 13.9 %collective-permute-start.1 = (bf16[51,2,512]{2,1,0:T(2,128)(2,1)}, bf16[51,2,512]{2,1,0:T(2,128)(2,1)S(1)}, u32[]{:S(2)}, u32[]{:S(2)}) collective-permute-start(bf16[51,2,512]{2,1,0:T(2,128)(2,1)} %get-tuple-element.18), channel_id=1, source_target_pairs={{0,1},{1,0},{2,3},{3,2},{4,5},{5,4},{6,7},{7,6},{8,9},{9,8},{10,11... | collective-permute-start | bytes 313352 | tf_op jit(solution)/shard_map/ppermute | solution.py:504
  10.9 6.4 %collective-permute-start.2 = (bf16[51,2,512]{2,1,0:T(2,128)(2,1)}, bf16[51,2,512]{2,1,0:T(2,128)(2,1)S(1)}, u32[]{:S(2)}, u32[]{:S(2)}) collective-permute-start(bf16[51,2,512]{2,1,0:T(2,128)(2,1)} %get-tuple-element.19), channel_id=1, source_target_pairs={{0,63},{1,226},{2,33},{3,228},{4,35},{5,230},{6,37},{7,232},{8,39}... | collective-permute-start | bytes 313352 | tf_op jit(solution)/shard_map/ppermute | solution.py:504
  12.9 4.4 %copy-start = (bf16[1024,2048]{1,0:T(8,128)(2,1)S(1)}, bf16[1024,2048]{1,0:T(8,128)(2,1)}, u32[]{:S(2)}) copy-start(bf16[1024,2048]{1,0:T(8,128)(2,1)} %split.1) | copy-start | bytes 12582916
  12.9 4.4 %copy-start.1 = (bf16[512,1536]{1,0:T(8,128)(2,1)S(1)}, bf16[512,1536]{1,0:T(8,128)(2,1)}, u32[]{:S(2)}) copy-start(bf16[512,1536]{1,0:T(8,128)(2,1)} %e_weight.1) | copy-start | bytes 4718596
  13.0 4.4 %copy-start.2 = (bf16[512,1536]{1,0:T(8,128)(2,1)S(1)}, bf16[512,1536]{1,0:T(8,128)(2,1)}, u32[]{:S(2)}) copy-start(bf16[512,1536]{1,0:T(8,128)(2,1)} %d_weight.1) | copy-start | bytes 4718596
  13.0 4.4 %copy-start.3 = (bf16[512,512]{1,0:T(8,128)(2,1)S(1)}, bf16[512,512]{1,0:T(8,128)(2,1)}, u32[]{:S(2)}) copy-start(bf16[512,512]{1,0:T(8,128)(2,1)} %e_out_weight.1) | copy-start | bytes 1572868
  13.0 4.4 %copy-start.4 = (bf16[512,512]{1,0:T(8,128)(2,1)S(1)}, bf16[512,512]{1,0:T(8,128)(2,1)}, u32[]{:S(2)}) copy-start(bf16[512,512]{1,0:T(8,128)(2,1)} %d_out_weight.1) | copy-start | bytes 1572868
  13.0 4.4 %copy-start.5 = (bf16[51,2,512]{2,1,0:T(2,128)(2,1)S(1)}, bf16[51,2,512]{2,1,0:T(2,128)(2,1)}, u32[]{:S(2)}) copy-start(bf16[51,2,512]{2,1,0:T(2,128)(2,1)} %get-tuple-element.16.b0) | copy-start | bytes 313348
  13.0 4.4 %copy-start.6 = (f32[1536]{0:T(1024)S(1)}, f32[1536]{0:T(1024)}, u32[]{:S(2)}) copy-start(f32[1536]{0:T(1024)} %e_bias.1) | copy-start | bytes 18436
  13.0 4.4 %copy-start.7 = (f32[1536]{0:T(1024)S(1)}, f32[1536]{0:T(1024)}, u32[]{:S(2)}) copy-start(f32[1536]{0:T(1024)} %d_bias.1) | copy-start | bytes 18436
  13.0 4.4 %copy-start.8 = (f32[2048]{0:T(1024)S(1)}, f32[2048]{0:T(1024)}, u32[]{:S(2)}) copy-start(f32[2048]{0:T(1024)} %param.41) | copy-start | bytes 24580
  13.0 4.4 %copy-start.9 = (f32[512]{0:T(512)S(1)}, f32[512]{0:T(512)}, u32[]{:S(2)}) copy-start(f32[512]{0:T(512)} %param.26) | copy-start | bytes 6148
  13.1 4.4 %copy-start.10 = (f32[512]{0:T(512)S(1)}, f32[512]{0:T(512)}, u32[]{:S(2)}) copy-start(f32[512]{0:T(512)} %param.27) | copy-start | bytes 6148
  13.1 4.4 %copy-start.11 = (f32[512]{0:T(512)S(1)}, f32[512]{0:T(512)}, u32[]{:S(2)}) copy-start(f32[512]{0:T(512)} %param.31) | copy-start | bytes 6148
  13.1 4.4 %copy-start.12 = (f32[512]{0:T(512)S(1)}, f32[512]{0:T(512)}, u32[]{:S(2)}) copy-start(f32[512]{0:T(512)} %param.33) | copy-start | bytes 6148
  13.1 4.4 %copy-start.13 = (f32[512]{0:T(512)S(1)}, f32[512]{0:T(512)}, u32[]{:S(2)}) copy-start(f32[512]{0:T(512)} %param.34) | copy-start | bytes 6148
  13.1 4.4 %copy-start.14 = (f32[512]{0:T(512)S(1)}, f32[512]{0:T(512)}, u32[]{:S(2)}) copy-start(f32[512]{0:T(512)} %param.38) | copy-start | bytes 6148
  26.9 5.7 %collective-permute-start.3 = (bf16[48,2,512]{2,1,0:T(2,128)(2,1)S(1)}, bf16[48,2,512]{2,1,0:T(2,128)(2,1)S(1)}, u32[]{:S(2)}, u32[]{:S(2)}) collective-permute-start(bf16[48,2,512]{2,1,0:T(2,128)(2,1)S(1)} %get-tuple-element.23), channel_id=1, source_target_pairs={{224,0},{33,1},{226,2},{35,3},{228,4},{37,5},{230,6},{39,7},{232,8... | collective-permute-start | bytes 294920 | tf_op jit(solution)/shard_map/ppermute | solution.py:504
  30.3 7.7 %collective-permute-start.4 = (bf16[48,2,512]{2,1,0:T(2,128)(2,1)S(1)}, bf16[48,2,512]{2,1,0:T(2,128)(2,1)S(1)}, u32[]{:S(2)}, u32[]{:S(2)}) collective-permute-start(bf16[48,2,512]{2,1,0:T(2,128)(2,1)S(1)} %get-tuple-element.24), channel_id=1, source_target_pairs={{1,0},{0,1},{3,2},{2,3},{5,4},{4,5},{7,6},{6,7},{9,8},{8,9},{11,10... | collective-permute-start | bytes 294920 | tf_op jit(solution)/shard_map/ppermute | solution.py:504
  30.3 9.5 %collective-permute-start.5 = (bf16[48,2,512]{2,1,0:T(2,128)(2,1)S(1)}, bf16[48,2,512]{2,1,0:T(2,128)(2,1)S(1)}, u32[]{:S(2)}, u32[]{:S(2)}) collective-permute-start(bf16[48,2,512]{2,1,0:T(2,128)(2,1)S(1)} %get-tuple-element.25), channel_id=1, source_target_pairs={{63,0},{226,1},{33,2},{228,3},{35,4},{230,5},{37,6},{232,7},{39,8}... | collective-permute-start | bytes 294920 | tf_op jit(solution)/shard_map/ppermute | solution.py:504

commit v6 on v5

--- a/solution.py
+++ b/solution.py
@@ -48,18 +48,8 @@
     return m + parity * (1 - 2 * m)
 
 
-def turned(window_row, lats):
-    return (window_row % lats + lats) % lats // (lats // 2)
-
-
-def own_turned(lats):
-    return turned(lax.axis_index("lat") - column_parity(), lats)
-
-
-def piece_cut(m, n, lats):
-    target = swapped(n, column_parity())
-    window_row = lax.axis_index("lat") - (1 - target if m else target)
-    return swapped(1 - m, target), swapped(1 - n, turned(window_row, lats))
+def piece_cut(m, n):
+    return swapped(1 - m, swapped(n, column_parity())), 1 - n
 
 
 def gather_quadrants(refs, base, scratch, parity):
@@ -128,7 +118,7 @@
     lane = lax.broadcasted_iota(jnp.int32, (1, WIDE + FIRST), 1)
     token = jnp.where(lane < WIDE, lane, FIRST + lane % REST)
     quadrant, r, c, level = token_place(token)
-    place = HN * swapped(1 - quadrant % 2, own_turned(lats)) + c
+    place = HN * (1 - quadrant % 2) + c
     hot = lax.broadcasted_iota(jnp.int32, (128, WIDE + FIRST), 0) == place
     rows = jnp.concatenate([ref[CLASS_AT + r, :, :128].astype(f32) for ref in refs for r in range(HL)], axis=0)
     spread = dot(rows.astype(bf16), hot.astype(f32).astype(bf16))
@@ -215,7 +205,7 @@
 
 
 def pack_kernel(
-    lats, tokens_hbm, cotangent_hbm, coarse_hbm, classes_hbm, o0, o1, o2, o3,
+    tokens_hbm, cotangent_hbm, coarse_hbm, classes_hbm, o0, o1, o2, o3,
     tokens, cotangent, coarse, classes, buffers, in_sems, out_sems,
 ):
     arrivals = [
@@ -230,8 +220,8 @@
     for copy in arrivals:
         copy.wait()
     departures = []
-    for q in (2, 1, 3, 0):
-        later, right = piece_cut(*divmod(q, 2), lats)
+    for q in (1, 3, 2, 0):
+        later, right = piece_cut(*divmod(q, 2))
         lat, lon = HL * later, HN * right
         low_lat, low_lon = (coarse.shape[0] - COARSE_ROWS) * later, COARSE_COLS * right
         for r in range(HL):
@@ -250,11 +240,10 @@
         copy.wait()
 
 
-def lookup_kernel(lats, inputs_ref, out_ref, rest_ref, low, high, packed_low, packed_high, parts, spots):
+def lookup_kernel(inputs_ref, out_ref, rest_ref, low, high, packed_low, packed_high, parts, spots):
     token = lax.broadcasted_iota(jnp.int32, (SPAN, 1), 0)
     quadrant, r, c, level = token_place(token)
-    right = swapped(quadrant % 2, own_turned(lats))
-    old = level * (WIN_LAT * WIN_LON) + (quadrant // 2 * HL + r) * WIN_LON + right * HN + c
+    old = level * (WIN_LAT * WIN_LON) + (quadrant // 2 * HL + r) * WIN_LON + quadrant % 2 * HN + c
     order = (lax.broadcasted_iota(jnp.int32, (SPAN, SPAN), 1) == old).astype(f32).astype(bf16)
     index = inputs_ref[:SPAN, :SPAN].astype(jnp.int32)
     rest = SPAN - 128
@@ -336,15 +325,15 @@
             )
 
 
-def lookup(lats, relative_index, encoder_table, decoder_table):
+def lookup(relative_index, encoder_table, decoder_table):
     blocks = -(-encoder_table.shape[1] // WIDE)
 
-    def widen(rows):
-        return jnp.pad(rows, ((0, 0), (0, blocks * WIDE - rows.shape[1])))
-
-    inputs = jnp.concatenate([widen(relative_index.astype(f32)), widen(encoder_table), widen(decoder_table)], axis=0)
+    def placed(rows, at):
+        return jnp.pad(rows, ((at, SPAN + 2 * HEADS - at - rows.shape[0]), (0, blocks * WIDE - rows.shape[1])))
+
+    inputs = placed(relative_index, 0).astype(f32) + placed(encoder_table, SPAN) + placed(decoder_table, SPAN + HEADS)
     return pl.pallas_call(
-        functools.partial(lookup_kernel, lats),
+        lookup_kernel,
         out_shape=[
             jax.ShapeDtypeStruct((2 * HEADS * SPAN, FIRST), f32),
             jax.ShapeDtypeStruct((2 * SPAN, HEADS * REST), f32),
@@ -380,7 +369,7 @@
 
 
 def main_kernel(
-    lats, b0, b2, b1, b3, bias_main, bias_rest,
+    lats, b0, b1, b3, b2, bias_main, bias_rest,
     e_gain, e_offset, e_bias, e_out_bias, d_gain, d_offset, d_bias, d_out_bias, split_bias,
     e_weight, e_out_weight, d_weight, d_out_weight, split,
     o0, o1, o2, o3,
@@ -445,11 +434,11 @@
     scatter_quadrants(scratch, outs, PAIRS, parity)
 
 
-def home_kernel(lats, h0, h2, h1, h3, decoded, tokens_gradient, coarse_gradient, total, sems):
+def home_kernel(h0, h1, h3, h2, decoded, tokens_gradient, coarse_gradient, total, sems):
     copies = []
     total[...] = jnp.zeros_like(total)
     for q, ref in enumerate((h0, h1, h2, h3)):
-        later, right = piece_cut(*divmod(q, 2), lats)
+        later, right = piece_cut(*divmod(q, 2))
         for n, out in enumerate((decoded, tokens_gradient)):
             for r in range(HL):
                 copy = pltpu.make_async_copy(
@@ -490,15 +479,14 @@
 
 def exchange(pieces, lats, lons, back):
     out = list(pieces)
-    for q in (2, 1, 3):
+    for q in (1, 3, 2):
         m, n = divmod(q, 2)
         pairs = []
         for i in range(lats):
             for j in range(lons):
-                target = (j + n) % 2
-                turn = turned(i - (1 - target if m else target), lats)
-                to = (i + m * (2 * target - 1)) % lats, (j + n * (2 * turn - 1)) % lons
-                pairs.append((i * lons + j, to[0] * lons + to[1]))
+                to = (j - n) % lons
+                step = m * (1 if to % 2 else -1)
+                pairs.append((i * lons + j, (i + step) % lats * lons + to))
         if back:
             pairs = [(target, source) for source, target in pairs]
         out[q] = lax.ppermute(pieces[q], ("lat", "lon"), pairs)
@@ -519,7 +507,7 @@
 
     s = jax.ShapeDtypeStruct
     packed = call(
-        functools.partial(pack_kernel, lats),
+        pack_kernel,
         "pack",
         [
             jnp.transpose(tokens, (1, 2, 0, 3)),
@@ -543,13 +531,13 @@
         60,
     )
     parts = exchange(packed, lats, lons, False)
-    biases = lookup(lats, relative_index, encoder_table, decoder_table)
+    biases = lookup(relative_index, encoder_table, decoder_table)
     points = 4 * LEVELS * POINTS
     outs = call(
         functools.partial(main_kernel, lats),
         "main",
         [
-            parts[0], parts[2], parts[1], parts[3], *biases,
+            parts[0], parts[1], parts[3], parts[2], *biases,
             row(encoder_gain), row(encoder_offset), encoder_projection_bias, row(encoder_output_bias),
             row(decoder_gain), row(decoder_offset), decoder_projection_bias, row(decoder_output_bias),
             row(split_bias),
@@ -573,9 +561,9 @@
     grid = s((WIN_LAT, WIN_LON, LEVELS, D), bf16)
     low = s((WIN_LAT // 2, WIN_LON // 2, LEVELS, 2 * D), bf16)
     results = call(
-        functools.partial(home_kernel, lats),
+        home_kernel,
         "home",
-        [home[0], home[2], home[1], home[3]],
+        [home[0], home[1], home[3], home[2]],
         [grid, grid, low],
         [
             pltpu.VMEM((WIN_LAT // 2, WIN_LON // 2, LEVELS, 2 * D), f32),

time: 41.6 us -> 40.3 us (0.969)
  other arithmetic: 1.71 us -> 0.98 us
  starting transfers between devices: 13.1 us -> 12.6 us
    add x0 -> x1, other arithmetic: none -> 0.98 us  [lookup(): placed(relative_index, 0).astype(f32) + placed(encoder_table, SPAN)]
    convert_element_type x1 -> x0, other arithmetic: 0.92 us -> none  [lookup(): relative_index.astype(f32)]
    concatenate x1 -> x0, other arithmetic: 0.79 us -> none  [lookup(): jnp.concatenate([widen(relative_index.astype(f32)), widen(encoder_table),...]
    ppermute x6, starting transfers between devices: 13.1 us -> 12.6 us  [exchange(): out[q] = lax.ppermute(pieces[q], ('lat', 'lon'), pairs)]
  transfers between devices with their start and end apart: 6 -> 6, of which waited for: 4 -> 3; matrix products, arithmetic and copies ran while one was open for 4% -> 2% of each run, Pallas kernels for 10% -> 10%
where the time goes in v6:
time: 40.3 us; the launch traced here: 40.2 us
  Pallas kernels  16.9 us (42%)
  starting transfers between devices  12.6 us (31%)
  waiting for transfers between devices  8.78 us (22%)
  other arithmetic  0.98 us (2%)
  between operations  0.88 us (2%)
    pallas_call x3, Pallas kernels, call(): pl.pallas_call(kernel, out_shape=outs, in_specs=in_specs or [VM] * len(in...  12.8 us
    ppermute x6, starting transfers between devices, exchange(): out[q] = lax.ppermute(pieces[q], ('lat', 'lon'), pairs)  12.6 us
    ppermute x6, waiting for transfers between devices, exchange(): out[q] = lax.ppermute(pieces[q], ('lat', 'lon'), pairs)  8.78 us
    pallas_call x1, Pallas kernels, lookup(): pl.pallas_call(lookup_kernel, out_shape=[jax.ShapeDtypeStruct((2 * HEADS...  4.07 us
    add x1, other arithmetic, lookup(): placed(relative_index, 0).astype(f32) + placed(encoder_table, SPAN)  0.98 us
  transfers between devices with their start and end apart: 6, of which 3 were waited for; matrix products, arithmetic and copies ran while one was open for 2% of the time, Pallas kernels for 10%

profile of v6, /device:TPU:24, one launch (start us, length us, event | category | flops | bytes accessed | tf_op | source)
XLA Modules:
  0.0 40.2 jit_solution(16777816235173213364)
XLA Ops:
  0.6 1.9 %pack.1 = (bf16[51,2,512]{2,1,0:T(2,128)(2,1)}, bf16[51,2,512]{2,1,0:T(2,128)(2,1)}, bf16[51,2,512]{2,1,0:T(2,128)(2,1)}, bf16[51,2,512]{2,1,0:T(2,128)(2,1)}) custom-call(bf16[6,12,2,512]{3,2,1,0:T(2,128)(2,1)} %bitcast.21, bf16[6,12,2,512]{3,2,1,0:T(2,128)(2,1)} %bitcast.22, bf16[3,6,2,1024]{3,2,1,0:T(2,128)(2,1)} %bitcast.23, s32[6,2,12]{2,1,0:T(2,128)} %bitcast.24), custom_call_target="tpu_custom_call" | custom-call | flops 100000000 | bytes 100000 | tf_op jit(solution)/shard_map/pack/pallas_call | solution.py:468
  2.5 7.8 %collective-permute-start = (bf16[51,2,512]{2,1,0:T(2,128)(2,1)}, bf16[51,2,512]{2,1,0:T(2,128)(2,1)S(1)}, u32[]{:S(2)}, u32[]{:S(2)}) collective-permute-start(bf16[51,2,512]{2,1,0:T(2,128)(2,1)} %get-tuple-element.17), channel_id=1, source_target_pairs={{0,31},{1,0},{2,1},{3,2},{4,3},{5,4},{6,5},{7,6},{8,7},{9,8},{10,9... | collective-permute-start | bytes 313352 | tf_op jit(solution)/shard_map/ppermute | solution.py:492
  10.3 0.1 collective-permute-start.1
  10.4 2.1 %collective-permute-start.2 = (bf16[51,2,512]{2,1,0:T(2,128)(2,1)}, bf16[51,2,512]{2,1,0:T(2,128)(2,1)S(1)}, u32[]{:S(2)}, u32[]{:S(2)}) collective-permute-start(bf16[51,2,512]{2,1,0:T(2,128)(2,1)} %get-tuple-element.19), channel_id=1, source_target_pairs={{0,224},{1,33},{2,226},{3,35},{4,228},{5,37},{6,230},{7,39},{8,232... | collective-permute-start | bytes 313352 | tf_op jit(solution)/shard_map/ppermute | solution.py:492
  12.5 1.0 %pad_add_fusion.inputs_ref = f32[160,768]{1,0:T(8,128)S(1)} fusion(f32[8,759]{1,0:T(8,128)} %param.39, f32[8,759]{1,0:T(8,128)} %param.32, s32[144,144]{1,0:T(8,128)} %param.25), kind=kLoop, calls=%fused_computation | loop fusion | flops 368640 | bytes 623040 | tf_op jit(solution)/shard_map/add | solution.py:334
  13.4 0.0 copy-start
  13.5 0.0 copy-start.1
  13.5 0.0 copy-start.2
  13.5 0.0 copy-start.3
  13.5 0.0 copy-start.4
  13.5 0.0 copy-start.7
  13.5 0.0 copy-start.8
  13.6 0.0 copy-start.10
  13.6 0.0 copy-start.11
  13.6 0.0 copy-start.14
  13.6 4.1 %lookup.1 = (f32[2304,128]{1,0:T(8,128)S(1)}, f32[288,128]{1,0:T(8,128)S(1)}) custom-call(f32[160,768]{1,0:T(8,128)S(1)} %pad_add_fusion.inputs_ref), custom_call_target="tpu_custom_call" | custom-call | flops 3000000000 | bytes 4000000 | tf_op jit(solution)/shard_map/lookup/pallas_call | solution.py:335
  17.7 0.2 collective-permute-done.2.b2
  18.0 9.4 %main.1 = (bf16[48,2,512]{2,1,0:T(2,128)(2,1)S(1)}, bf16[48,2,512]{2,1,0:T(2,128)(2,1)S(1)}, bf16[48,2,512]{2,1,0:T(2,128)(2,1)S(1)}, bf16[48,2,512]{2,1,0:T(2,128)(2,1)S(1)}) custom-call(bf16[51,2,512]{2,1,0:T(2,128)(2,1)S(1)} %copy-done.5, bf16[51,2,512]{2,1,0:T(2,128)(2,1)S(1)} %collective-permute-done.b1, ...), custom_call_target="tpu_custom_call" | custom-call | flops 8000000000 | bytes 8000000 | tf_op jit(solution)/shard_map/main/pallas_call | solution.py:468
  27.4 1.8 %collective-permute-start.3 = (bf16[48,2,512]{2,1,0:T(2,128)(2,1)S(1)}, bf16[48,2,512]{2,1,0:T(2,128)(2,1)S(1)}, u32[]{:S(2)}, u32[]{:S(2)}) collective-permute-start(bf16[48,2,512]{2,1,0:T(2,128)(2,1)S(1)} %get-tuple-element.23), channel_id=1, source_target_pairs={{31,0},{0,1},{1,2},{2,3},{3,4},{4,5},{5,6},{6,7},{7,8},{8,9},{9,10... | collective-permute-start | bytes 294920 | tf_op jit(solution)/shard_map/ppermute | solution.py:492
  29.2 0.6 %collective-permute-start.4 = (bf16[48,2,512]{2,1,0:T(2,128)(2,1)S(1)}, bf16[48,2,512]{2,1,0:T(2,128)(2,1)S(1)}, u32[]{:S(2)}, u32[]{:S(2)}) collective-permute-start(bf16[48,2,512]{2,1,0:T(2,128)(2,1)S(1)} %get-tuple-element.24), channel_id=1, source_target_pairs={{63,0},{224,1},{33,2},{226,3},{35,4},{228,5},{37,6},{230,7},{39,8}... | collective-permute-start | bytes 294920 | tf_op jit(solution)/shard_map/ppermute | solution.py:492
  29.8 0.3 collective-permute-start.5
  30.1 5.1 %collective-permute-done.3.h1 = bf16[48,2,512]{2,1,0:T(2,128)(2,1)S(1)} collective-permute-done((bf16[48,2,512]{2,1,0:T(2,128)(2,1)S(1)}, bf16[48,2,512]{2,1,0:T(2,128)(2,1)S(1)}, u32[]{:S(2)}, u32[]{:S(2)}) %collective-permute-start.3) | collective-permute-done | bytes 98336 | tf_op jit(solution)/shard_map/ppermute | solution.py:492
  35.2 3.5 %collective-permute-done.4.h3 = bf16[48,2,512]{2,1,0:T(2,128)(2,1)S(1)} collective-permute-done((bf16[48,2,512]{2,1,0:T(2,128)(2,1)S(1)}, bf16[48,2,512]{2,1,0:T(2,128)(2,1)S(1)}, u32[]{:S(2)}, u32[]{:S(2)}) %collective-permute-start.4) | collective-permute-done | bytes 98336 | tf_op jit(solution)/shard_map/ppermute | solution.py:492
  38.7 1.5 %home.1 = (bf16[6,12,2,512]{3,2,1,0:T(2,128)(2,1)}, bf16[6,12,2,512]{3,2,1,0:T(2,128)(2,1)}, bf16[3,6,2,1024]{3,2,1,0:T(2,128)(2,1)}) custom-call(bf16[48,2,512]{2,1,0:T(2,128)(2,1)S(1)} %get-tuple-element.22.h0, bf16[48,2,512]{2,1,0:T(2,128)(2,1)S(1)} %collective-permute-done.3.h1, bf16[48,2,512]{2,1,0:T(2,128)(2,1)S(1)} %collective-permute-done.4.h3, ...), custom_call_target="tpu_custom_call" | custom-call | flops 1000000 | bytes 1000 | tf_op jit(solution)/shard_map/home/pallas_call | solution.py:468
  (23 shorter events, 0.1 us)
Async XLA Ops:
  2.5 15.2 %collective-permute-start = (bf16[51,2,512]{2,1,0:T(2,128)(2,1)}, bf16[51,2,512]{2,1,0:T(2,128)(2,1)S(1)}, u32[]{:S(2)}, u32[]{:S(2)}) collective-permute-start(bf16[51,2,512]{2,1,0:T(2,128)(2,1)} %get-tuple-element.17), channel_id=1, source_target_pairs={{0,31},{1,0},{2,1},{3,2},{4,3},{5,4},{6,5},{7,6},{8,7},{9,8},{10,9... | collective-permute-start | bytes 313352 | tf_op jit(solution)/shard_map/ppermute | solution.py:492
  10.3 7.4 %collective-permute-start.1 = (bf16[51,2,512]{2,1,0:T(2,128)(2,1)}, bf16[51,2,512]{2,1,0:T(2,128)(2,1)S(1)}, u32[]{:S(2)}, u32[]{:S(2)}) collective-permute-start(bf16[51,2,512]{2,1,0:T(2,128)(2,1)} %get-tuple-element.18), channel_id=1, source_target_pairs={{0,63},{1,224},{2,33},{3,226},{4,35},{5,228},{6,37},{7,230},{8,39}... | collective-permute-start | bytes 313352 | tf_op jit(solution)/shard_map/ppermute | solution.py:492
  10.4 7.5 %collective-permute-start.2 = (bf16[51,2,512]{2,1,0:T(2,128)(2,1)}, bf16[51,2,512]{2,1,0:T(2,128)(2,1)S(1)}, u32[]{:S(2)}, u32[]{:S(2)}) collective-permute-start(bf16[51,2,512]{2,1,0:T(2,128)(2,1)} %get-tuple-element.19), channel_id=1, source_target_pairs={{0,224},{1,33},{2,226},{3,35},{4,228},{5,37},{6,230},{7,39},{8,232... | collective-permute-start | bytes 313352 | tf_op jit(solution)/shard_map/ppermute | solution.py:492
  13.4 4.4 %copy-start = (bf16[1024,2048]{1,0:T(8,128)(2,1)S(1)}, bf16[1024,2048]{1,0:T(8,128)(2,1)}, u32[]{:S(2)}) copy-start(bf16[1024,2048]{1,0:T(8,128)(2,1)} %split.1) | copy-start | bytes 12582916
  13.5 4.4 %copy-start.1 = (bf16[512,1536]{1,0:T(8,128)(2,1)S(1)}, bf16[512,1536]{1,0:T(8,128)(2,1)}, u32[]{:S(2)}) copy-start(bf16[512,1536]{1,0:T(8,128)(2,1)} %e_weight.1) | copy-start | bytes 4718596
  13.5 4.4 %copy-start.2 = (bf16[512,1536]{1,0:T(8,128)(2,1)S(1)}, bf16[512,1536]{1,0:T(8,128)(2,1)}, u32[]{:S(2)}) copy-start(bf16[512,1536]{1,0:T(8,128)(2,1)} %d_weight.1) | copy-start | bytes 4718596
  13.5 4.4 %copy-start.3 = (bf16[512,512]{1,0:T(8,128)(2,1)S(1)}, bf16[512,512]{1,0:T(8,128)(2,1)}, u32[]{:S(2)}) copy-start(bf16[512,512]{1,0:T(8,128)(2,1)} %e_out_weight.1) | copy-start | bytes 1572868
  13.5 4.4 %copy-start.4 = (bf16[512,512]{1,0:T(8,128)(2,1)S(1)}, bf16[512,512]{1,0:T(8,128)(2,1)}, u32[]{:S(2)}) copy-start(bf16[512,512]{1,0:T(8,128)(2,1)} %d_out_weight.1) | copy-start | bytes 1572868
  13.5 4.4 %copy-start.5 = (bf16[51,2,512]{2,1,0:T(2,128)(2,1)S(1)}, bf16[51,2,512]{2,1,0:T(2,128)(2,1)}, u32[]{:S(2)}) copy-start(bf16[51,2,512]{2,1,0:T(2,128)(2,1)} %get-tuple-element.16.b0) | copy-start | bytes 313348
  13.5 4.4 %copy-start.6 = (f32[1536]{0:T(1024)S(1)}, f32[1536]{0:T(1024)}, u32[]{:S(2)}) copy-start(f32[1536]{0:T(1024)} %e_bias.1) | copy-start | bytes 18436
  13.5 4.4 %copy-start.7 = (f32[1536]{0:T(1024)S(1)}, f32[1536]{0:T(1024)}, u32[]{:S(2)}) copy-start(f32[1536]{0:T(1024)} %d_bias.1) | copy-start | bytes 18436
  13.5 4.4 %copy-start.8 = (f32[2048]{0:T(1024)S(1)}, f32[2048]{0:T(1024)}, u32[]{:S(2)}) copy-start(f32[2048]{0:T(1024)} %param.41) | copy-start | bytes 24580
  13.6 4.4 %copy-start.9 = (f32[512]{0:T(512)S(1)}, f32[512]{0:T(512)}, u32[]{:S(2)}) copy-start(f32[512]{0:T(512)} %param.26) | copy-start | bytes 6148
  13.6 4.4 %copy-start.10 = (f32[512]{0:T(512)S(1)}, f32[512]{0:T(512)}, u32[]{:S(2)}) copy-start(f32[512]{0:T(512)} %param.27) | copy-start | bytes 6148
  13.6 4.4 %copy-start.11 = (f32[512]{0:T(512)S(1)}, f32[512]{0:T(512)}, u32[]{:S(2)}) copy-start(f32[512]{0:T(512)} %param.31) | copy-start | bytes 6148
  13.6 4.4 %copy-start.12 = (f32[512]{0:T(512)S(1)}, f32[512]{0:T(512)}, u32[]{:S(2)}) copy-start(f32[512]{0:T(512)} %param.33) | copy-start | bytes 6148
  13.6 4.4 %copy-start.13 = (f32[512]{0:T(512)S(1)}, f32[512]{0:T(512)}, u32[]{:S(2)}) copy-start(f32[512]{0:T(512)} %param.34) | copy-start | bytes 6148
  13.6 4.4 %copy-start.14 = (f32[512]{0:T(512)S(1)}, f32[512]{0:T(512)}, u32[]{:S(2)}) copy-start(f32[512]{0:T(512)} %param.38) | copy-start | bytes 6148
  27.4 7.7 %collective-permute-start.3 = (bf16[48,2,512]{2,1,0:T(2,128)(2,1)S(1)}, bf16[48,2,512]{2,1,0:T(2,128)(2,1)S(1)}, u32[]{:S(2)}, u32[]{:S(2)}) collective-permute-start(bf16[48,2,512]{2,1,0:T(2,128)(2,1)S(1)} %get-tuple-element.23), channel_id=1, source_target_pairs={{31,0},{0,1},{1,2},{2,3},{3,4},{4,5},{5,6},{6,7},{7,8},{8,9},{9,10... | collective-permute-start | bytes 294920 | tf_op jit(solution)/shard_map/ppermute | solution.py:492
  29.2 9.5 %collective-permute-start.4 = (bf16[48,2,512]{2,1,0:T(2,128)(2,1)S(1)}, bf16[48,2,512]{2,1,0:T(2,128)(2,1)S(1)}, u32[]{:S(2)}, u32[]{:S(2)}) collective-permute-start(bf16[48,2,512]{2,1,0:T(2,128)(2,1)S(1)} %get-tuple-element.24), channel_id=1, source_target_pairs={{63,0},{224,1},{33,2},{226,3},{35,4},{228,5},{37,6},{230,7},{39,8}... | collective-permute-start | bytes 294920 | tf_op jit(solution)/shard_map/ppermute | solution.py:492
  29.8 8.9 %collective-permute-start.5 = (bf16[48,2,512]{2,1,0:T(2,128)(2,1)S(1)}, bf16[48,2,512]{2,1,0:T(2,128)(2,1)S(1)}, u32[]{:S(2)}, u32[]{:S(2)}) collective-permute-start(bf16[48,2,512]{2,1,0:T(2,128)(2,1)S(1)} %get-tuple-element.25), channel_id=1, source_target_pairs={{224,0},{33,1},{226,2},{35,3},{228,4},{37,5},{230,6},{39,7},{232,8... | collective-permute-start | bytes 294920 | tf_op jit(solution)/shard_map/ppermute | solution.py:492

commit v7 on v6

--- a/solution.py
+++ b/solution.py
@@ -54,18 +54,16 @@
 
 def gather_quadrants(refs, base, scratch, parity):
     for q, ref in enumerate(refs):
-        m, qc = divmod(q, 2)
-        half = swapped(m, parity)
-        for t in range(PAIRS):
-            scratch[half, pl.ds(2 * (qc * PAIRS + t), 2), :] = ref[base + t].astype(f32)
+        m, n = divmod(q, 2)
+        rows = ref[pl.ds(base, PAIRS)].reshape(2 * PAIRS, D).astype(f32)
+        scratch[swapped(m, parity), pl.ds(2 * PAIRS * n, 2 * PAIRS), :] = rows
 
 
 def scatter_quadrants(scratch, refs, base, parity):
     for q, ref in enumerate(refs):
-        m, qc = divmod(q, 2)
-        half = swapped(m, parity)
-        for t in range(PAIRS):
-            ref[base + t] = scratch[half, pl.ds(2 * (qc * PAIRS + t), 2), :].astype(bf16)
+        m, n = divmod(q, 2)
+        rows = scratch[swapped(m, parity), pl.ds(2 * PAIRS * n, 2 * PAIRS), :]
+        ref[pl.ds(base, PAIRS)] = rows.astype(bf16).reshape(PAIRS, LEVELS, D)
 
 
 def whole(scratch):
@@ -133,12 +131,15 @@
     return [jnp.where(column == queries, 0.0, BLANK) for queries in (label[:, :FIRST], label[:, WIDE:])]
 
 
-def block_forward(x, blank, bias_of, gain, offset, weight, bias, out_weight, out_bias, qkv_ref, probs_ref):
+def project(x, gain, offset, weight, bias, qkv_ref):
     xhat, _ = normalise(x)
     normed = (xhat * gain + offset).astype(bf16)
     queries = (dot(normed, weight[:, :D]) + bias[:, :D]).astype(bf16) * jnp.array(HEAD**-0.5, bf16)
     qkv_ref[:, :D] = queries
     qkv_ref[:, D:] = (dot(normed, weight[:, D:]) + bias[:, D:]).astype(bf16)
+
+
+def attend(x, blank, bias_of, out_weight, out_bias, qkv_ref, probs_ref):
     keys, values = qkv_ref[:, D : 2 * D], qkv_ref[:, 2 * D :]
 
     def soften(s, tile):
@@ -160,8 +161,7 @@
     return x + dot(heads_out, out_weight) + out_bias
 
 
-def block_backward(grad, x, gain, weight, out_weight, qkv_ref, probs_ref, dqkv_ref):
-    dheads = dot_nt(grad, out_weight).astype(bf16)
+def block_backward(grad, dheads, x, gain, weight, qkv_ref, probs_ref, dqkv_ref):
     keys, values = qkv_ref[:, D : 2 * D], qkv_ref[:, 2 * D :]
 
     def harden(dprobs, columns):
@@ -352,20 +352,15 @@
     )(inputs)
 
 
-def coarse_points(qc):
-    return [r * 2 * COARSE_COLS + qc * COARSE_COLS + c for r in range(COARSE_ROWS) for c in range(COARSE_COLS)]
-
-
-def coarse_places():
-    places = []
-    for q in range(4):
-        qr, qc = divmod(q, 2)
-        for r in range(HL):
-            for c in range(HN):
-                row, column = qr * HL + r + HL % 2, qc * HN + c + HN % 2
-                at = (row // 2) * 2 * COARSE_COLS + column // 2
-                places.append((q * PAIRS + r * HN + c, at, (row % 2) * 2 + column % 2))
-    return places
+POINT_ROWS = 4 * LEVELS * POINTS
+
+
+def fine_place(t):
+    quadrant, r, c, level = token_place(t)
+    row, column = quadrant // 2 * HL + r + HL % 2, quadrant % 2 * HN + c + HN % 2
+    point = row // 4 * 2 * POINTS + column // 2 // COARSE_COLS * POINTS
+    point = point + row // 2 % 2 * COARSE_COLS + column // 2 % COARSE_COLS
+    return (row % 2 * 2 + column % 2) * POINT_ROWS + LEVELS * point + level
 
 
 def main_kernel(
@@ -373,7 +368,8 @@
     e_gain, e_offset, e_bias, e_out_bias, d_gain, d_offset, d_bias, d_out_bias, split_bias,
     e_weight, e_out_weight, d_weight, d_out_weight, split,
     o0, o1, o2, o3,
-    scratch, coarse, fine, tokens, e_qkv, e_probs, d_qkv, d_probs, dqkv,
+    in_tokens, in_cotangent, out_decoded, out_tokens, coarse, coarse_grad,
+    e_qkv, e_probs, d_qkv, d_probs, d_dqkv, e_dqkv,
 ):
     def bias_tiles(block):
         def tile(h):
@@ -384,54 +380,52 @@
         return tile
 
     parity = column_parity()
-    parts = (b0, b1, b2, b3)
-    gather_quadrants(parts, 0, scratch, parity)
-    x = whole(scratch)
-    tokens[...] = x.astype(bf16)
+    parts, outs = (b0, b1, b2, b3), (o0, o1, o2, o3)
+    gather_quadrants(parts, 0, in_tokens, parity)
+    tokens = whole(in_tokens)
+    project(tokens, e_gain[...], e_offset[...], e_weight, e_bias[...].reshape(1, -1), e_qkv)
     blank = mask_bias(parts, lats, parity)
-    encoded = block_forward(
-        x, blank, bias_tiles(0), e_gain[...], e_offset[...], e_weight,
-        e_bias[...].reshape(1, -1), e_out_weight[...], e_out_bias[...], e_qkv, e_probs,
-    ).astype(bf16)
 
     for q, ref in enumerate(parts):
-        part = swapped(q // 2, parity)
-        for n, at in enumerate(coarse_points(q % 2)):
-            for half in range(2):
-                coarse[part, pl.ds(2 * at, 2), pl.ds(D * half, D)] = ref[COARSE_AT + POINTS * half + n].astype(f32)
-    lowres = whole(coarse).astype(bf16)
-    fine[...] = dot(lowres, split[...]) + split_bias[...]
-    for t, at, kind in coarse_places():
-        scratch[t // (2 * PAIRS), pl.ds(2 * (t % (2 * PAIRS)), 2), :] = fine[pl.ds(2 * at, 2), pl.ds(kind * D, D)]
-    x = (encoded.astype(f32) + whole(scratch)).astype(bf16).astype(f32)
-    decoded = block_forward(
-        x, blank, bias_tiles(1), d_gain[...], d_offset[...], d_weight,
-        d_bias[...].reshape(1, -1), d_out_weight[...], d_out_bias[...], d_qkv, d_probs,
-    )
-    outs = (o0, o1, o2, o3)
-    fill(scratch, decoded)
-    scatter_quadrants(scratch, outs, 0, parity)
-    gather_quadrants(parts, COTANGENT_AT, scratch, parity)
-    grad = whole(scratch).astype(bf16)
-    dx = block_backward(grad, x, d_gain[...], d_weight[...], d_out_weight[...], d_qkv, d_probs, dqkv)
+        m, n = divmod(q, 2)
+        for half in range(2):
+            rows = ref[pl.ds(COARSE_AT + POINTS * half, POINTS)].reshape(2 * POINTS, D).astype(f32)
+            coarse[swapped(m, parity), pl.ds(2 * POINTS * n, 2 * POINTS), pl.ds(D * half, D)] = rows
+    fine = dot(whole(coarse).astype(bf16), split[...]) + split_bias[...]
+    fine = jnp.concatenate([fine[:, D * k : D * (k + 1)] for k in range(4)], axis=0)
+    shape = (SPAN, 4 * POINT_ROWS)
+    token = lax.broadcasted_iota(jnp.int32, (SPAN, 1), 0)
+    picks = (lax.broadcasted_iota(jnp.int32, shape, 1) == fine_place(token)).astype(f32).astype(bf16)
+    high = fine.astype(bf16)
+    upsampled = dot(picks, high) + dot(picks, (fine - high.astype(f32)).astype(bf16))
+
+    gather_quadrants(parts, COTANGENT_AT, in_cotangent, parity)
+    grad = whole(in_cotangent).astype(bf16)
+    dheads = dot_nt(grad, d_out_weight[...]).astype(bf16)
+
+    encoded = attend(tokens, blank, bias_tiles(0), e_out_weight[...], e_out_bias[...], e_qkv, e_probs).astype(bf16)
+    joined = (encoded.astype(f32) + upsampled).astype(bf16).astype(f32)
+    project(joined, d_gain[...], d_offset[...], d_weight, d_bias[...].reshape(1, -1), d_qkv)
+    decoded = attend(joined, blank, bias_tiles(1), d_out_weight[...], d_out_bias[...], d_qkv, d_probs)
+    dx = block_backward(grad, dheads, joined, d_gain[...], d_weight[...], d_qkv, d_probs, d_dqkv)
+    fill(out_decoded, decoded)
+    scatter_quadrants(out_decoded, outs, 0, parity)
+
     grad = dx.astype(bf16)
-
-    fill(scratch, dx)
-    fine[...] = jnp.zeros_like(fine)
-    for t, at, kind in coarse_places():
-        fine[pl.ds(2 * at, 2), pl.ds(kind * D, D)] = scratch[t // (2 * PAIRS), pl.ds(2 * (t % (2 * PAIRS)), 2), :]
-    fill(coarse, dot_nt(fine[...].astype(bf16), split[...]))
+    dheads = dot_nt(grad, e_out_weight[...]).astype(bf16)
+    token = lax.broadcasted_iota(jnp.int32, (1, SPAN), 1)
+    places = (lax.broadcasted_iota(jnp.int32, shape[::-1], 0) == fine_place(token)).astype(f32).astype(bf16)
+    spread = dot(places, grad).astype(bf16)
+    spread = jnp.concatenate([spread[POINT_ROWS * k : POINT_ROWS * (k + 1)] for k in range(4)], axis=1)
+    fill(coarse_grad, dot_nt(spread, split[...]))
+    dx = block_backward(grad, dheads, tokens, e_gain[...], e_weight[...], e_qkv, e_probs, e_dqkv)
     for q, ref in enumerate(outs):
-        part = swapped(q // 2, parity)
-        for n, at in enumerate(coarse_points(q % 2)):
-            for half in range(2):
-                ref[COARSE_AT + POINTS * half + n] = coarse[part, pl.ds(2 * at, 2), pl.ds(D * half, D)].astype(bf16)
-
-    dx = block_backward(
-        grad, tokens[...].astype(f32), e_gain[...], e_weight[...], e_out_weight[...], e_qkv, e_probs, dqkv
-    )
-    fill(scratch, dx)
-    scatter_quadrants(scratch, outs, PAIRS, parity)
+        m, n = divmod(q, 2)
+        for half in range(2):
+            rows = coarse_grad[swapped(m, parity), pl.ds(2 * POINTS * n, 2 * POINTS), pl.ds(D * half, D)]
+            ref[pl.ds(COARSE_AT + POINTS * half, POINTS)] = rows.astype(bf16).reshape(POINTS, LEVELS, D)
+    fill(out_tokens, dx)
+    scatter_quadrants(out_tokens, outs, PAIRS, parity)
 
 
 def home_kernel(h0, h1, h3, h2, decoded, tokens_gradient, coarse_gradient, total, sems):
@@ -532,7 +526,6 @@
     )
     parts = exchange(packed, lats, lons, False)
     biases = lookup(relative_index, encoder_table, decoder_table)
-    points = 4 * LEVELS * POINTS
     outs = call(
         functools.partial(main_kernel, lats),
         "main",
@@ -546,13 +539,16 @@
         [s((CLASS_AT, LEVELS, D), bf16)] * 4,
         [
             pltpu.VMEM((2, SPAN // 2, D), f32),
-            pltpu.VMEM((2, points // 2, 2 * D), f32),
-            pltpu.VMEM((points, 4 * D), f32),
-            pltpu.VMEM((SPAN, D), bf16),
+            pltpu.VMEM((2, SPAN // 2, D), f32),
+            pltpu.VMEM((2, SPAN // 2, D), f32),
+            pltpu.VMEM((2, SPAN // 2, D), f32),
+            pltpu.VMEM((2, POINT_ROWS // 2, 2 * D), f32),
+            pltpu.VMEM((2, POINT_ROWS // 2, 2 * D), f32),
             pltpu.VMEM((SPAN, 3 * D), bf16),
             pltpu.VMEM((SPAN, HEADS * SPAN), bf16),
             pltpu.VMEM((SPAN, 3 * D), bf16),
             pltpu.VMEM((SPAN, HEADS * SPAN), bf16),
+            pltpu.VMEM((SPAN, 3 * D), bf16),
             pltpu.VMEM((SPAN, 3 * D), bf16),
         ],
         8_000_000_000,

time: 40.3 us -> 40.1 us (level)
  no operation moved by 1% of the time
where the time goes in v7:
time: 40.1 us; the launch traced here: 39.9 us
  Pallas kernels  16.6 us (41%)
  starting transfers between devices  12.6 us (31%)
  waiting for transfers between devices  8.78 us (22%)
  other arithmetic  0.98 us (2%)
  between operations  0.88 us (2%)
    ppermute x6, starting transfers between devices, exchange(): out[q] = lax.ppermute(pieces[q], ('lat', 'lon'), pairs)  12.6 us
    pallas_call x3, Pallas kernels, call(): pl.pallas_call(kernel, out_shape=outs, in_specs=in_specs or [VM] * len(in...  12.5 us
    ppermute x6, waiting for transfers between devices, exchange(): out[q] = lax.ppermute(pieces[q], ('lat', 'lon'), pairs)  8.78 us
    pallas_call x1, Pallas kernels, lookup(): pl.pallas_call(lookup_kernel, out_shape=[jax.ShapeDtypeStruct((2 * HEADS...  4.07 us
    add x1, other arithmetic, lookup(): placed(relative_index, 0).astype(f32) + placed(encoder_table, SPAN)  0.98 us
  transfers between devices with their start and end apart: 6, of which 3 were waited for; matrix products, arithmetic and copies ran while one was open for 2% of the time, Pallas kernels for 10%

profile of v7, /device:TPU:24, one launch (start us, length us, event | category | flops | bytes accessed | tf_op | source)
XLA Modules:
  0.0 39.9 jit_solution(10722726858376274979)
XLA Ops:
  0.6 1.9 %pack.1 = (bf16[51,2,512]{2,1,0:T(2,128)(2,1)}, bf16[51,2,512]{2,1,0:T(2,128)(2,1)}, bf16[51,2,512]{2,1,0:T(2,128)(2,1)}, bf16[51,2,512]{2,1,0:T(2,128)(2,1)}) custom-call(bf16[6,12,2,512]{3,2,1,0:T(2,128)(2,1)} %bitcast.21, bf16[6,12,2,512]{3,2,1,0:T(2,128)(2,1)} %bitcast.22, bf16[3,6,2,1024]{3,2,1,0:T(2,128)(2,1)} %bitcast.23, s32[6,2,12]{2,1,0:T(2,128)} %bitcast.24), custom_call_target="tpu_custom_call" | custom-call | flops 100000000 | bytes 100000 | tf_op jit(solution)/shard_map/pack/pallas_call | solution.py:462
  2.5 7.8 %collective-permute-start = (bf16[51,2,512]{2,1,0:T(2,128)(2,1)}, bf16[51,2,512]{2,1,0:T(2,128)(2,1)S(1)}, u32[]{:S(2)}, u32[]{:S(2)}) collective-permute-start(bf16[51,2,512]{2,1,0:T(2,128)(2,1)} %get-tuple-element.17), channel_id=1, source_target_pairs={{0,31},{1,0},{2,1},{3,2},{4,3},{5,4},{6,5},{7,6},{8,7},{9,8},{10,9... | collective-permute-start | bytes 313352 | tf_op jit(solution)/shard_map/ppermute | solution.py:486
  10.3 0.1 collective-permute-start.1
  10.4 2.1 %collective-permute-start.2 = (bf16[51,2,512]{2,1,0:T(2,128)(2,1)}, bf16[51,2,512]{2,1,0:T(2,128)(2,1)S(1)}, u32[]{:S(2)}, u32[]{:S(2)}) collective-permute-start(bf16[51,2,512]{2,1,0:T(2,128)(2,1)} %get-tuple-element.19), channel_id=1, source_target_pairs={{0,224},{1,33},{2,226},{3,35},{4,228},{5,37},{6,230},{7,39},{8,232... | collective-permute-start | bytes 313352 | tf_op jit(solution)/shard_map/ppermute | solution.py:486
  12.5 1.0 %pad_add_fusion.inputs_ref = f32[160,768]{1,0:T(8,128)S(1)} fusion(f32[8,759]{1,0:T(8,128)} %param.39, f32[8,759]{1,0:T(8,128)} %param.32, s32[144,144]{1,0:T(8,128)} %param.25), kind=kLoop, calls=%fused_computation | loop fusion | flops 368640 | bytes 623040 | tf_op jit(solution)/shard_map/add | solution.py:334
  13.4 0.0 copy-start
  13.5 0.0 copy-start.1
  13.5 0.0 copy-start.2
  13.5 0.0 copy-start.3
  13.5 0.0 copy-start.4
  13.5 0.0 copy-start.7
  13.5 0.0 copy-start.8
  13.6 0.0 copy-start.10
  13.6 0.0 copy-start.11
  13.6 0.0 copy-start.14
  13.6 4.1 %lookup.1 = (f32[2304,128]{1,0:T(8,128)S(1)}, f32[288,128]{1,0:T(8,128)S(1)}) custom-call(f32[160,768]{1,0:T(8,128)S(1)} %pad_add_fusion.inputs_ref), custom_call_target="tpu_custom_call" | custom-call | flops 3000000000 | bytes 4000000 | tf_op jit(solution)/shard_map/lookup/pallas_call | solution.py:335
  17.7 0.2 collective-permute-done.2.b2
  18.0 9.1 %main.1 = (bf16[48,2,512]{2,1,0:T(2,128)(2,1)S(1)}, bf16[48,2,512]{2,1,0:T(2,128)(2,1)S(1)}, bf16[48,2,512]{2,1,0:T(2,128)(2,1)S(1)}, bf16[48,2,512]{2,1,0:T(2,128)(2,1)S(1)}) custom-call(bf16[51,2,512]{2,1,0:T(2,128)(2,1)S(1)} %copy-done.5, bf16[51,2,512]{2,1,0:T(2,128)(2,1)S(1)} %collective-permute-done.b1, ...), custom_call_target="tpu_custom_call" | custom-call | flops 8000000000 | bytes 8000000 | tf_op jit(solution)/shard_map/main/pallas_call | solution.py:462
  27.1 1.8 %collective-permute-start.3 = (bf16[48,2,512]{2,1,0:T(2,128)(2,1)S(1)}, bf16[48,2,512]{2,1,0:T(2,128)(2,1)S(1)}, u32[]{:S(2)}, u32[]{:S(2)}) collective-permute-start(bf16[48,2,512]{2,1,0:T(2,128)(2,1)S(1)} %get-tuple-element.23), channel_id=1, source_target_pairs={{31,0},{0,1},{1,2},{2,3},{3,4},{4,5},{5,6},{6,7},{7,8},{8,9},{9,10... | collective-permute-start | bytes 294920 | tf_op jit(solution)/shard_map/ppermute | solution.py:486
  28.9 0.6 %collective-permute-start.4 = (bf16[48,2,512]{2,1,0:T(2,128)(2,1)S(1)}, bf16[48,2,512]{2,1,0:T(2,128)(2,1)S(1)}, u32[]{:S(2)}, u32[]{:S(2)}) collective-permute-start(bf16[48,2,512]{2,1,0:T(2,128)(2,1)S(1)} %get-tuple-element.24), channel_id=1, source_target_pairs={{63,0},{224,1},{33,2},{226,3},{35,4},{228,5},{37,6},{230,7},{39,8}... | collective-permute-start | bytes 294920 | tf_op jit(solution)/shard_map/ppermute | solution.py:486
  29.5 0.3 collective-permute-start.5
  29.8 5.1 %collective-permute-done.3.h1 = bf16[48,2,512]{2,1,0:T(2,128)(2,1)S(1)} collective-permute-done((bf16[48,2,512]{2,1,0:T(2,128)(2,1)S(1)}, bf16[48,2,512]{2,1,0:T(2,128)(2,1)S(1)}, u32[]{:S(2)}, u32[]{:S(2)}) %collective-permute-start.3) | collective-permute-done | bytes 98336 | tf_op jit(solution)/shard_map/ppermute | solution.py:486
  34.9 3.5 %collective-permute-done.4.h3 = bf16[48,2,512]{2,1,0:T(2,128)(2,1)S(1)} collective-permute-done((bf16[48,2,512]{2,1,0:T(2,128)(2,1)S(1)}, bf16[48,2,512]{2,1,0:T(2,128)(2,1)S(1)}, u32[]{:S(2)}, u32[]{:S(2)}) %collective-permute-start.4) | collective-permute-done | bytes 98336 | tf_op jit(solution)/shard_map/ppermute | solution.py:486
  38.4 1.5 %home.1 = (bf16[6,12,2,512]{3,2,1,0:T(2,128)(2,1)}, bf16[6,12,2,512]{3,2,1,0:T(2,128)(2,1)}, bf16[3,6,2,1024]{3,2,1,0:T(2,128)(2,1)}) custom-call(bf16[48,2,512]{2,1,0:T(2,128)(2,1)S(1)} %get-tuple-element.22.h0, bf16[48,2,512]{2,1,0:T(2,128)(2,1)S(1)} %collective-permute-done.3.h1, bf16[48,2,512]{2,1,0:T(2,128)(2,1)S(1)} %collective-permute-done.4.h3, ...), custom_call_target="tpu_custom_call" | custom-call | flops 1000000 | bytes 1000 | tf_op jit(solution)/shard_map/home/pallas_call | solution.py:462
  (23 shorter events, 0.1 us)
Async XLA Ops:
  2.5 15.2 %collective-permute-start = (bf16[51,2,512]{2,1,0:T(2,128)(2,1)}, bf16[51,2,512]{2,1,0:T(2,128)(2,1)S(1)}, u32[]{:S(2)}, u32[]{:S(2)}) collective-permute-start(bf16[51,2,512]{2,1,0:T(2,128)(2,1)} %get-tuple-element.17), channel_id=1, source_target_pairs={{0,31},{1,0},{2,1},{3,2},{4,3},{5,4},{6,5},{7,6},{8,7},{9,8},{10,9... | collective-permute-start | bytes 313352 | tf_op jit(solution)/shard_map/ppermute | solution.py:486
  10.3 7.4 %collective-permute-start.1 = (bf16[51,2,512]{2,1,0:T(2,128)(2,1)}, bf16[51,2,512]{2,1,0:T(2,128)(2,1)S(1)}, u32[]{:S(2)}, u32[]{:S(2)}) collective-permute-start(bf16[51,2,512]{2,1,0:T(2,128)(2,1)} %get-tuple-element.18), channel_id=1, source_target_pairs={{0,63},{1,224},{2,33},{3,226},{4,35},{5,228},{6,37},{7,230},{8,39}... | collective-permute-start | bytes 313352 | tf_op jit(solution)/shard_map/ppermute | solution.py:486
  10.4 7.5 %collective-permute-start.2 = (bf16[51,2,512]{2,1,0:T(2,128)(2,1)}, bf16[51,2,512]{2,1,0:T(2,128)(2,1)S(1)}, u32[]{:S(2)}, u32[]{:S(2)}) collective-permute-start(bf16[51,2,512]{2,1,0:T(2,128)(2,1)} %get-tuple-element.19), channel_id=1, source_target_pairs={{0,224},{1,33},{2,226},{3,35},{4,228},{5,37},{6,230},{7,39},{8,232... | collective-permute-start | bytes 313352 | tf_op jit(solution)/shard_map/ppermute | solution.py:486
  13.4 4.4 %copy-start = (bf16[1024,2048]{1,0:T(8,128)(2,1)S(1)}, bf16[1024,2048]{1,0:T(8,128)(2,1)}, u32[]{:S(2)}) copy-start(bf16[1024,2048]{1,0:T(8,128)(2,1)} %split.1) | copy-start | bytes 12582916
  13.5 4.4 %copy-start.1 = (bf16[512,1536]{1,0:T(8,128)(2,1)S(1)}, bf16[512,1536]{1,0:T(8,128)(2,1)}, u32[]{:S(2)}) copy-start(bf16[512,1536]{1,0:T(8,128)(2,1)} %e_weight.1) | copy-start | bytes 4718596
  13.5 4.4 %copy-start.2 = (bf16[512,1536]{1,0:T(8,128)(2,1)S(1)}, bf16[512,1536]{1,0:T(8,128)(2,1)}, u32[]{:S(2)}) copy-start(bf16[512,1536]{1,0:T(8,128)(2,1)} %d_weight.1) | copy-start | bytes 4718596
  13.5 4.4 %copy-start.3 = (bf16[512,512]{1,0:T(8,128)(2,1)S(1)}, bf16[512,512]{1,0:T(8,128)(2,1)}, u32[]{:S(2)}) copy-start(bf16[512,512]{1,0:T(8,128)(2,1)} %e_out_weight.1) | copy-start | bytes 1572868
  13.5 4.4 %copy-start.4 = (bf16[512,512]{1,0:T(8,128)(2,1)S(1)}, bf16[512,512]{1,0:T(8,128)(2,1)}, u32[]{:S(2)}) copy-start(bf16[512,512]{1,0:T(8,128)(2,1)} %d_out_weight.1) | copy-start | bytes 1572868
  13.5 4.4 %copy-start.5 = (bf16[51,2,512]{2,1,0:T(2,128)(2,1)S(1)}, bf16[51,2,512]{2,1,0:T(2,128)(2,1)}, u32[]{:S(2)}) copy-start(bf16[51,2,512]{2,1,0:T(2,128)(2,1)} %get-tuple-element.16.b0) | copy-start | bytes 313348
  13.5 4.4 %copy-start.6 = (f32[1536]{0:T(1024)S(1)}, f32[1536]{0:T(1024)}, u32[]{:S(2)}) copy-start(f32[1536]{0:T(1024)} %e_bias.1) | copy-start | bytes 18436
  13.5 4.4 %copy-start.7 = (f32[1536]{0:T(1024)S(1)}, f32[1536]{0:T(1024)}, u32[]{:S(2)}) copy-start(f32[1536]{0:T(1024)} %d_bias.1) | copy-start | bytes 18436
  13.5 4.4 %copy-start.8 = (f32[2048]{0:T(1024)S(1)}, f32[2048]{0:T(1024)}, u32[]{:S(2)}) copy-start(f32[2048]{0:T(1024)} %param.41) | copy-start | bytes 24580
  13.6 4.4 %copy-start.9 = (f32[512]{0:T(512)S(1)}, f32[512]{0:T(512)}, u32[]{:S(2)}) copy-start(f32[512]{0:T(512)} %param.26) | copy-start | bytes 6148
  13.6 4.4 %copy-start.10 = (f32[512]{0:T(512)S(1)}, f32[512]{0:T(512)}, u32[]{:S(2)}) copy-start(f32[512]{0:T(512)} %param.27) | copy-start | bytes 6148
  13.6 4.4 %copy-start.11 = (f32[512]{0:T(512)S(1)}, f32[512]{0:T(512)}, u32[]{:S(2)}) copy-start(f32[512]{0:T(512)} %param.31) | copy-start | bytes 6148
  13.6 4.4 %copy-start.12 = (f32[512]{0:T(512)S(1)}, f32[512]{0:T(512)}, u32[]{:S(2)}) copy-start(f32[512]{0:T(512)} %param.33) | copy-start | bytes 6148
  13.6 4.4 %copy-start.13 = (f32[512]{0:T(512)S(1)}, f32[512]{0:T(512)}, u32[]{:S(2)}) copy-start(f32[512]{0:T(512)} %param.34) | copy-start | bytes 6148
  13.6 4.4 %copy-start.14 = (f32[512]{0:T(512)S(1)}, f32[512]{0:T(512)}, u32[]{:S(2)}) copy-start(f32[512]{0:T(512)} %param.38) | copy-start | bytes 6148
  27.1 7.7 %collective-permute-start.3 = (bf16[48,2,512]{2,1,0:T(2,128)(2,1)S(1)}, bf16[48,2,512]{2,1,0:T(2,128)(2,1)S(1)}, u32[]{:S(2)}, u32[]{:S(2)}) collective-permute-start(bf16[48,2,512]{2,1,0:T(2,128)(2,1)S(1)} %get-tuple-element.23), channel_id=1, source_target_pairs={{31,0},{0,1},{1,2},{2,3},{3,4},{4,5},{5,6},{6,7},{7,8},{8,9},{9,10... | collective-permute-start | bytes 294920 | tf_op jit(solution)/shard_map/ppermute | solution.py:486
  28.9 9.5 %collective-permute-start.4 = (bf16[48,2,512]{2,1,0:T(2,128)(2,1)S(1)}, bf16[48,2,512]{2,1,0:T(2,128)(2,1)S(1)}, u32[]{:S(2)}, u32[]{:S(2)}) collective-permute-start(bf16[48,2,512]{2,1,0:T(2,128)(2,1)S(1)} %get-tuple-element.24), channel_id=1, source_target_pairs={{63,0},{224,1},{33,2},{226,3},{35,4},{228,5},{37,6},{230,7},{39,8}... | collective-permute-start | bytes 294920 | tf_op jit(solution)/shard_map/ppermute | solution.py:486
  29.5 8.9 %collective-permute-start.5 = (bf16[48,2,512]{2,1,0:T(2,128)(2,1)S(1)}, bf16[48,2,512]{2,1,0:T(2,128)(2,1)S(1)}, u32[]{:S(2)}, u32[]{:S(2)}) collective-permute-start(bf16[48,2,512]{2,1,0:T(2,128)(2,1)S(1)} %get-tuple-element.25), channel_id=1, source_target_pairs={{224,0},{33,1},{226,2},{35,3},{228,4},{37,5},{230,6},{39,7},{232,8... | collective-permute-start | bytes 294920 | tf_op jit(solution)/shard_map/ppermute | solution.py:486

commit v8 on v7

--- a/solution.py
+++ b/solution.py
@@ -49,7 +49,7 @@
 
 
 def piece_cut(m, n):
-    return swapped(1 - m, swapped(n, column_parity())), 1 - n
+    return swapped(1 - m, swapped(n, column_parity())), n
 
 
 def gather_quadrants(refs, base, scratch, parity):
@@ -116,7 +116,7 @@
     lane = lax.broadcasted_iota(jnp.int32, (1, WIDE + FIRST), 1)
     token = jnp.where(lane < WIDE, lane, FIRST + lane % REST)
     quadrant, r, c, level = token_place(token)
-    place = HN * (1 - quadrant % 2) + c
+    place = HN * (quadrant % 2) + c
     hot = lax.broadcasted_iota(jnp.int32, (128, WIDE + FIRST), 0) == place
     rows = jnp.concatenate([ref[CLASS_AT + r, :, :128].astype(f32) for ref in refs for r in range(HL)], axis=0)
     spread = dot(rows.astype(bf16), hot.astype(f32).astype(bf16))
@@ -243,7 +243,7 @@
 def lookup_kernel(inputs_ref, out_ref, rest_ref, low, high, packed_low, packed_high, parts, spots):
     token = lax.broadcasted_iota(jnp.int32, (SPAN, 1), 0)
     quadrant, r, c, level = token_place(token)
-    old = level * (WIN_LAT * WIN_LON) + (quadrant // 2 * HL + r) * WIN_LON + quadrant % 2 * HN + c
+    old = level * (WIN_LAT * WIN_LON) + (quadrant // 2 * HL + r) * WIN_LON + (1 - quadrant % 2) * HN + c
     order = (lax.broadcasted_iota(jnp.int32, (SPAN, SPAN), 1) == old).astype(f32).astype(bf16)
     index = inputs_ref[:SPAN, :SPAN].astype(jnp.int32)
     rest = SPAN - 128
@@ -478,7 +478,7 @@
         pairs = []
         for i in range(lats):
             for j in range(lons):
-                to = (j - n) % lons
+                to = (j + n) % lons
                 step = m * (1 if to % 2 else -1)
                 pairs.append((i * lons + j, (i + step) % lats * lons + to))
         if back:

time: 40.1 us -> 36 us (0.90)
  the two profiles are of different devices: /device:TPU:24 before, /device:TPU:2 now
where the time goes in v8:
time: 36 us; the launch traced here: 35.8 us
  Pallas kernels  16.6 us (46%)
  starting transfers between devices  11.3 us (31%)
  waiting for transfers between devices  5.99 us (17%)
  other arithmetic  0.98 us (3%)
  between operations  0.89 us (2%)
    pallas_call x3, Pallas kernels, call(): pl.pallas_call(kernel, out_shape=outs, in_specs=in_specs or [VM] * len(in...  12.5 us
    ppermute x6, starting transfers between devices, exchange(): out[q] = lax.ppermute(pieces[q], ('lat', 'lon'), pairs)  11.3 us
    ppermute x6, waiting for transfers between devices, exchange(): out[q] = lax.ppermute(pieces[q], ('lat', 'lon'), pairs)  5.99 us
    pallas_call x1, Pallas kernels, lookup(): pl.pallas_call(lookup_kernel, out_shape=[jax.ShapeDtypeStruct((2 * HEADS...  4.08 us
    add x1, other arithmetic, lookup(): placed(relative_index, 0).astype(f32) + placed(encoder_table, SPAN)  0.98 us
  transfers between devices with their start and end apart: 6, of which 3 were waited for; matrix products, arithmetic and copies ran while one was open for 3% of the time, Pallas kernels for 11%

profile of v8, /device:TPU:2, one launch (start us, length us, event | category | flops | bytes accessed | tf_op | source)
XLA Modules:
  0.0 35.8 jit_solution(11735296931339370919)
XLA Ops:
  0.6 1.9 %pack.1 = (bf16[51,2,512]{2,1,0:T(2,128)(2,1)}, bf16[51,2,512]{2,1,0:T(2,128)(2,1)}, bf16[51,2,512]{2,1,0:T(2,128)(2,1)}, bf16[51,2,512]{2,1,0:T(2,128)(2,1)}) custom-call(bf16[6,12,2,512]{3,2,1,0:T(2,128)(2,1)} %bitcast.21, bf16[6,12,2,512]{3,2,1,0:T(2,128)(2,1)} %bitcast.22, bf16[3,6,2,1024]{3,2,1,0:T(2,128)(2,1)} %bitcast.23, s32[6,2,12]{2,1,0:T(2,128)} %bitcast.24), custom_call_target="tpu_custom_call" | custom-call | flops 100000000 | bytes 100000 | tf_op jit(solution)/shard_map/pack/pallas_call | solution.py:462
  2.5 0.1 collective-permute-start
  2.6 3.2 %collective-permute-start.1 = (bf16[51,2,512]{2,1,0:T(2,128)(2,1)}, bf16[51,2,512]{2,1,0:T(2,128)(2,1)S(1)}, u32[]{:S(2)}, u32[]{:S(2)}) collective-permute-start(bf16[51,2,512]{2,1,0:T(2,128)(2,1)} %get-tuple-element.18), channel_id=1, source_target_pairs={{0,33},{1,226},{2,35},{3,228},{4,37},{5,230},{6,39},{7,232},{8,41}... | collective-permute-start | bytes 313352 | tf_op jit(solution)/shard_map/ppermute | solution.py:486
  5.8 2.6 %collective-permute-start.2 = (bf16[51,2,512]{2,1,0:T(2,128)(2,1)}, bf16[51,2,512]{2,1,0:T(2,128)(2,1)S(1)}, u32[]{:S(2)}, u32[]{:S(2)}) collective-permute-start(bf16[51,2,512]{2,1,0:T(2,128)(2,1)} %get-tuple-element.19), channel_id=1, source_target_pairs={{0,224},{1,33},{2,226},{3,35},{4,228},{5,37},{6,230},{7,39},{8,232... | collective-permute-start | bytes 313352 | tf_op jit(solution)/shard_map/ppermute | solution.py:486
  8.3 1.0 %pad_add_fusion.inputs_ref = f32[160,768]{1,0:T(8,128)S(1)} fusion(f32[8,759]{1,0:T(8,128)} %param.39, f32[8,759]{1,0:T(8,128)} %param.32, s32[144,144]{1,0:T(8,128)} %param.25), kind=kLoop, calls=%fused_computation | loop fusion | flops 368640 | bytes 623040 | tf_op jit(solution)/shard_map/add | solution.py:334
  9.3 0.0 copy-start
  9.3 0.0 copy-start.1
  9.4 0.0 copy-start.2
  9.4 0.0 copy-start.3
  9.4 0.0 copy-start.4
  9.4 0.0 copy-start.5
  9.4 0.0 copy-start.8
  9.4 0.0 copy-start.9
  9.5 0.0 copy-start.12
  9.5 0.0 copy-start.13
  9.5 4.1 %lookup.1 = (f32[2304,128]{1,0:T(8,128)S(1)}, f32[288,128]{1,0:T(8,128)S(1)}) custom-call(f32[160,768]{1,0:T(8,128)S(1)} %pad_add_fusion.inputs_ref), custom_call_target="tpu_custom_call" | custom-call | flops 3000000000 | bytes 4000000 | tf_op jit(solution)/shard_map/lookup/pallas_call | solution.py:335
  13.6 0.5 %collective-permute-done.1.b3 = bf16[51,2,512]{2,1,0:T(2,128)(2,1)S(1)} collective-permute-done((bf16[51,2,512]{2,1,0:T(2,128)(2,1)}, bf16[51,2,512]{2,1,0:T(2,128)(2,1)S(1)}, u32[]{:S(2)}, u32[]{:S(2)}) %collective-permute-start.1) | collective-permute-done | bytes 104480 | tf_op jit(solution)/shard_map/ppermute | solution.py:486
  14.3 9.1 %main.1 = (bf16[48,2,512]{2,1,0:T(2,128)(2,1)S(1)}, bf16[48,2,512]{2,1,0:T(2,128)(2,1)S(1)}, bf16[48,2,512]{2,1,0:T(2,128)(2,1)S(1)}, bf16[48,2,512]{2,1,0:T(2,128)(2,1)S(1)}) custom-call(bf16[51,2,512]{2,1,0:T(2,128)(2,1)S(1)} %copy-done.5, bf16[51,2,512]{2,1,0:T(2,128)(2,1)S(1)} %collective-permute-done.b1, ...), custom_call_target="tpu_custom_call" | custom-call | flops 8000000000 | bytes 8000000 | tf_op jit(solution)/shard_map/main/pallas_call | solution.py:462
  23.4 2.5 %collective-permute-start.3 = (bf16[48,2,512]{2,1,0:T(2,128)(2,1)S(1)}, bf16[48,2,512]{2,1,0:T(2,128)(2,1)S(1)}, u32[]{:S(2)}, u32[]{:S(2)}) collective-permute-start(bf16[48,2,512]{2,1,0:T(2,128)(2,1)S(1)} %get-tuple-element.23), channel_id=1, source_target_pairs={{1,0},{2,1},{3,2},{4,3},{5,4},{6,5},{7,6},{8,7},{9,8},{10,9},{11,1... | collective-permute-start | bytes 294920 | tf_op jit(solution)/shard_map/ppermute | solution.py:486
  25.9 1.6 %collective-permute-start.4 = (bf16[48,2,512]{2,1,0:T(2,128)(2,1)S(1)}, bf16[48,2,512]{2,1,0:T(2,128)(2,1)S(1)}, u32[]{:S(2)}, u32[]{:S(2)}) collective-permute-start(bf16[48,2,512]{2,1,0:T(2,128)(2,1)S(1)} %get-tuple-element.24), channel_id=1, source_target_pairs={{33,0},{226,1},{35,2},{228,3},{37,4},{230,5},{39,6},{232,7},{41,8}... | collective-permute-start | bytes 294920 | tf_op jit(solution)/shard_map/ppermute | solution.py:486
  27.6 1.3 %collective-permute-start.5 = (bf16[48,2,512]{2,1,0:T(2,128)(2,1)S(1)}, bf16[48,2,512]{2,1,0:T(2,128)(2,1)S(1)}, u32[]{:S(2)}, u32[]{:S(2)}) collective-permute-start(bf16[48,2,512]{2,1,0:T(2,128)(2,1)S(1)} %get-tuple-element.25), channel_id=1, source_target_pairs={{224,0},{33,1},{226,2},{35,3},{228,4},{37,5},{230,6},{39,7},{232,8... | collective-permute-start | bytes 294920 | tf_op jit(solution)/shard_map/ppermute | solution.py:486
  28.9 1.1 %collective-permute-done.4.h3 = bf16[48,2,512]{2,1,0:T(2,128)(2,1)S(1)} collective-permute-done((bf16[48,2,512]{2,1,0:T(2,128)(2,1)S(1)}, bf16[48,2,512]{2,1,0:T(2,128)(2,1)S(1)}, u32[]{:S(2)}, u32[]{:S(2)}) %collective-permute-start.4) | collective-permute-done | bytes 98336 | tf_op jit(solution)/shard_map/ppermute | solution.py:486
  30.0 4.3 %collective-permute-done.5.h2 = bf16[48,2,512]{2,1,0:T(2,128)(2,1)S(1)} collective-permute-done((bf16[48,2,512]{2,1,0:T(2,128)(2,1)S(1)}, bf16[48,2,512]{2,1,0:T(2,128)(2,1)S(1)}, u32[]{:S(2)}, u32[]{:S(2)}) %collective-permute-start.5) | collective-permute-done | bytes 98336 | tf_op jit(solution)/shard_map/ppermute | solution.py:486
  34.3 1.5 %home.1 = (bf16[6,12,2,512]{3,2,1,0:T(2,128)(2,1)}, bf16[6,12,2,512]{3,2,1,0:T(2,128)(2,1)}, bf16[3,6,2,1024]{3,2,1,0:T(2,128)(2,1)}) custom-call(bf16[48,2,512]{2,1,0:T(2,128)(2,1)S(1)} %get-tuple-element.22.h0, bf16[48,2,512]{2,1,0:T(2,128)(2,1)S(1)} %collective-permute-done.3.h1, bf16[48,2,512]{2,1,0:T(2,128)(2,1)S(1)} %collective-permute-done.4.h3, ...), custom_call_target="tpu_custom_call" | custom-call | flops 1000000 | bytes 1000 | tf_op jit(solution)/shard_map/home/pallas_call | solution.py:462
  (23 shorter events, 0.1 us)
Async XLA Ops:
  2.5 11.1 %collective-permute-start = (bf16[51,2,512]{2,1,0:T(2,128)(2,1)}, bf16[51,2,512]{2,1,0:T(2,128)(2,1)S(1)}, u32[]{:S(2)}, u32[]{:S(2)}) collective-permute-start(bf16[51,2,512]{2,1,0:T(2,128)(2,1)} %get-tuple-element.17), channel_id=1, source_target_pairs={{0,1},{1,2},{2,3},{3,4},{4,5},{5,6},{6,7},{7,8},{8,9},{9,10},{10,1... | collective-permute-start | bytes 313352 | tf_op jit(solution)/shard_map/ppermute | solution.py:486
  2.6 11.6 %collective-permute-start.1 = (bf16[51,2,512]{2,1,0:T(2,128)(2,1)}, bf16[51,2,512]{2,1,0:T(2,128)(2,1)S(1)}, u32[]{:S(2)}, u32[]{:S(2)}) collective-permute-start(bf16[51,2,512]{2,1,0:T(2,128)(2,1)} %get-tuple-element.18), channel_id=1, source_target_pairs={{0,33},{1,226},{2,35},{3,228},{4,37},{5,230},{6,39},{7,232},{8,41}... | collective-permute-start | bytes 313352 | tf_op jit(solution)/shard_map/ppermute | solution.py:486
  5.8 8.4 %collective-permute-start.2 = (bf16[51,2,512]{2,1,0:T(2,128)(2,1)}, bf16[51,2,512]{2,1,0:T(2,128)(2,1)S(1)}, u32[]{:S(2)}, u32[]{:S(2)}) collective-permute-start(bf16[51,2,512]{2,1,0:T(2,128)(2,1)} %get-tuple-element.19), channel_id=1, source_target_pairs={{0,224},{1,33},{2,226},{3,35},{4,228},{5,37},{6,230},{7,39},{8,232... | collective-permute-start | bytes 313352 | tf_op jit(solution)/shard_map/ppermute | solution.py:486
  9.3 4.8 %copy-start = (bf16[1024,2048]{1,0:T(8,128)(2,1)S(1)}, bf16[1024,2048]{1,0:T(8,128)(2,1)}, u32[]{:S(2)}) copy-start(bf16[1024,2048]{1,0:T(8,128)(2,1)} %split.1) | copy-start | bytes 12582916
  9.3 4.8 %copy-start.1 = (bf16[512,1536]{1,0:T(8,128)(2,1)S(1)}, bf16[512,1536]{1,0:T(8,128)(2,1)}, u32[]{:S(2)}) copy-start(bf16[512,1536]{1,0:T(8,128)(2,1)} %e_weight.1) | copy-start | bytes 4718596
  9.4 4.8 %copy-start.2 = (bf16[512,1536]{1,0:T(8,128)(2,1)S(1)}, bf16[512,1536]{1,0:T(8,128)(2,1)}, u32[]{:S(2)}) copy-start(bf16[512,1536]{1,0:T(8,128)(2,1)} %d_weight.1) | copy-start | bytes 4718596
  9.4 4.8 %copy-start.3 = (bf16[512,512]{1,0:T(8,128)(2,1)S(1)}, bf16[512,512]{1,0:T(8,128)(2,1)}, u32[]{:S(2)}) copy-start(bf16[512,512]{1,0:T(8,128)(2,1)} %e_out_weight.1) | copy-start | bytes 1572868
  9.4 4.8 %copy-start.4 = (bf16[512,512]{1,0:T(8,128)(2,1)S(1)}, bf16[512,512]{1,0:T(8,128)(2,1)}, u32[]{:S(2)}) copy-start(bf16[512,512]{1,0:T(8,128)(2,1)} %d_out_weight.1) | copy-start | bytes 1572868
  9.4 4.8 %copy-start.5 = (bf16[51,2,512]{2,1,0:T(2,128)(2,1)S(1)}, bf16[51,2,512]{2,1,0:T(2,128)(2,1)}, u32[]{:S(2)}) copy-start(bf16[51,2,512]{2,1,0:T(2,128)(2,1)} %get-tuple-element.16.b0) | copy-start | bytes 313348
  9.4 4.8 %copy-start.6 = (f32[1536]{0:T(1024)S(1)}, f32[1536]{0:T(1024)}, u32[]{:S(2)}) copy-start(f32[1536]{0:T(1024)} %e_bias.1) | copy-start | bytes 18436
  9.4 4.8 %copy-start.7 = (f32[1536]{0:T(1024)S(1)}, f32[1536]{0:T(1024)}, u32[]{:S(2)}) copy-start(f32[1536]{0:T(1024)} %d_bias.1) | copy-start | bytes 18436
  9.4 4.8 %copy-start.8 = (f32[2048]{0:T(1024)S(1)}, f32[2048]{0:T(1024)}, u32[]{:S(2)}) copy-start(f32[2048]{0:T(1024)} %param.41) | copy-start | bytes 24580
  9.4 4.8 %copy-start.9 = (f32[512]{0:T(512)S(1)}, f32[512]{0:T(512)}, u32[]{:S(2)}) copy-start(f32[512]{0:T(512)} %param.26) | copy-start | bytes 6148
  9.4 4.8 %copy-start.10 = (f32[512]{0:T(512)S(1)}, f32[512]{0:T(512)}, u32[]{:S(2)}) copy-start(f32[512]{0:T(512)} %param.27) | copy-start | bytes 6148
  9.5 4.8 %copy-start.11 = (f32[512]{0:T(512)S(1)}, f32[512]{0:T(512)}, u32[]{:S(2)}) copy-start(f32[512]{0:T(512)} %param.31) | copy-start | bytes 6148
  9.5 4.8 %copy-start.12 = (f32[512]{0:T(512)S(1)}, f32[512]{0:T(512)}, u32[]{:S(2)}) copy-start(f32[512]{0:T(512)} %param.33) | copy-start | bytes 6148
  9.5 4.8 %copy-start.13 = (f32[512]{0:T(512)S(1)}, f32[512]{0:T(512)}, u32[]{:S(2)}) copy-start(f32[512]{0:T(512)} %param.34) | copy-start | bytes 6148
  9.5 4.8 %copy-start.14 = (f32[512]{0:T(512)S(1)}, f32[512]{0:T(512)}, u32[]{:S(2)}) copy-start(f32[512]{0:T(512)} %param.38) | copy-start | bytes 6148
  23.4 5.5 %collective-permute-start.3 = (bf16[48,2,512]{2,1,0:T(2,128)(2,1)S(1)}, bf16[48,2,512]{2,1,0:T(2,128)(2,1)S(1)}, u32[]{:S(2)}, u32[]{:S(2)}) collective-permute-start(bf16[48,2,512]{2,1,0:T(2,128)(2,1)S(1)} %get-tuple-element.23), channel_id=1, source_target_pairs={{1,0},{2,1},{3,2},{4,3},{5,4},{6,5},{7,6},{8,7},{9,8},{10,9},{11,1... | collective-permute-start | bytes 294920 | tf_op jit(solution)/shard_map/ppermute | solution.py:486
  25.9 4.0 %collective-permute-start.4 = (bf16[48,2,512]{2,1,0:T(2,128)(2,1)S(1)}, bf16[48,2,512]{2,1,0:T(2,128)(2,1)S(1)}, u32[]{:S(2)}, u32[]{:S(2)}) collective-permute-start(bf16[48,2,512]{2,1,0:T(2,128)(2,1)S(1)} %get-tuple-element.24), channel_id=1, source_target_pairs={{33,0},{226,1},{35,2},{228,3},{37,4},{230,5},{39,6},{232,7},{41,8}... | collective-permute-start | bytes 294920 | tf_op jit(solution)/shard_map/ppermute | solution.py:486
  27.6 6.7 %collective-permute-start.5 = (bf16[48,2,512]{2,1,0:T(2,128)(2,1)S(1)}, bf16[48,2,512]{2,1,0:T(2,128)(2,1)S(1)}, u32[]{:S(2)}, u32[]{:S(2)}) collective-permute-start(bf16[48,2,512]{2,1,0:T(2,128)(2,1)S(1)} %get-tuple-element.25), channel_id=1, source_target_pairs={{224,0},{33,1},{226,2},{35,3},{228,4},{37,5},{230,6},{39,7},{232,8... | collective-permute-start | bytes 294920 | tf_op jit(solution)/shard_map/ppermute | solution.py:486

commit v9 on v8

--- a/solution.py
+++ b/solution.py
@@ -428,26 +428,29 @@
     scatter_quadrants(out_tokens, outs, PAIRS, parity)
 
 
-def home_kernel(h0, h1, h3, h2, decoded, tokens_gradient, coarse_gradient, total, sems):
+def home_kernel(h0, h1, h3, h2, decoded, tokens_gradient, coarse_gradient, total, rounded, sems):
+    refs = (h0, h1, h2, h3)
     copies = []
-    total[...] = jnp.zeros_like(total)
-    for q, ref in enumerate((h0, h1, h2, h3)):
+
+    def send(src, dst):
+        copy = pltpu.make_async_copy(src, dst, sems.at[len(copies)])
+        copy.start()
+        copies.append(copy)
+
+    for q, ref in enumerate(refs):
         later, right = piece_cut(*divmod(q, 2))
         for n, out in enumerate((decoded, tokens_gradient)):
             for r in range(HL):
-                copy = pltpu.make_async_copy(
-                    ref.at[pl.ds(PAIRS * n + r * HN, HN)],
-                    out.at[HL * later + r, pl.ds(HN * right, HN)],
-                    sems.at[len(copies)],
-                )
-                copy.start()
-                copies.append(copy)
+                send(ref.at[pl.ds(PAIRS * n + r * HN, HN)], out.at[HL * later + r, pl.ds(HN * right, HN)])
+    total[...] = jnp.zeros_like(total)
+    for q, ref in enumerate(refs):
+        later, right = piece_cut(*divmod(q, 2))
         for half in range(2):
             for r in range(COARSE_ROWS):
-                for c in range(COARSE_COLS):
-                    part = ref[COARSE_AT + POINTS * half + r * COARSE_COLS + c].astype(f32)
-                    total[later + r, COARSE_COLS * right + c, :, pl.ds(D * half, D)] += part
-    coarse_gradient[...] = total[...].astype(bf16)
+                part = ref[pl.ds(COARSE_AT + POINTS * half + r * COARSE_COLS, COARSE_COLS)].astype(f32)
+                total[later + r, pl.ds(COARSE_COLS * right, COARSE_COLS), :, pl.ds(D * half, D)] += part
+    rounded[...] = total[...].astype(bf16)
+    send(rounded, coarse_gradient)
     for copy in copies:
         copy.wait()
 
@@ -563,11 +566,12 @@
         [grid, grid, low],
         [
             pltpu.VMEM((WIN_LAT // 2, WIN_LON // 2, LEVELS, 2 * D), f32),
-            pltpu.SemaphoreType.DMA((4 * 2 * HL,)),
+            pltpu.VMEM((WIN_LAT // 2, WIN_LON // 2, LEVELS, 2 * D), bf16),
+            pltpu.SemaphoreType.DMA((4 * 2 * HL + 1,)),
         ],
         1_000_000,
         None,
-        [ANY, ANY, VM],
+        [ANY] * 3,
     )
     return tuple(jnp.transpose(r, (2, 0, 1, 3)) for r in results)
 

time: 36 us -> 35.4 us (0.983)
  Pallas kernels: 16.6 us -> 16 us
    pallas_call x3, Pallas kernels: 12.5 us -> 11.9 us  [call(): pl.pallas_call(kernel, out_shape=outs, in_specs=in_specs or [VM] * len(in...]
  transfers between devices with their start and end apart: 6 -> 6, of which waited for: 3 -> 3; matrix products, arithmetic and copies ran while one was open for 3% -> 3% of each run, Pallas kernels for 11% -> 12%
where the time goes in v9:
time: 35.4 us; the launch traced here: 35.3 us
  Pallas kernels  16 us (45%)
  starting transfers between devices  11.3 us (32%)
  waiting for transfers between devices  5.99 us (17%)
  other arithmetic  0.98 us (3%)
  between operations  0.89 us (3%)
    pallas_call x3, Pallas kernels, call(): pl.pallas_call(kernel, out_shape=outs, in_specs=in_specs or [VM] * len(in...  11.9 us
    ppermute x6, starting transfers between devices, exchange(): out[q] = lax.ppermute(pieces[q], ('lat', 'lon'), pairs)  11.3 us
    ppermute x6, waiting for transfers between devices, exchange(): out[q] = lax.ppermute(pieces[q], ('lat', 'lon'), pairs)  5.99 us
    pallas_call x1, Pallas kernels, lookup(): pl.pallas_call(lookup_kernel, out_shape=[jax.ShapeDtypeStruct((2 * HEADS...  4.08 us
    add x1, other arithmetic, lookup(): placed(relative_index, 0).astype(f32) + placed(encoder_table, SPAN)  0.98 us
  transfers between devices with their start and end apart: 6, of which 3 were waited for; matrix products, arithmetic and copies ran while one was open for 3% of the time, Pallas kernels for 12%

profile of v9, /device:TPU:2, one launch (start us, length us, event | category | flops | bytes accessed | tf_op | source)
XLA Modules:
  0.0 35.3 jit_solution(5051791183791292496)
XLA Ops:
  0.6 1.9 %pack.1 = (bf16[51,2,512]{2,1,0:T(2,128)(2,1)}, bf16[51,2,512]{2,1,0:T(2,128)(2,1)}, bf16[51,2,512]{2,1,0:T(2,128)(2,1)}, bf16[51,2,512]{2,1,0:T(2,128)(2,1)}) custom-call(bf16[6,12,2,512]{3,2,1,0:T(2,128)(2,1)} %bitcast.21, bf16[6,12,2,512]{3,2,1,0:T(2,128)(2,1)} %bitcast.22, bf16[3,6,2,1024]{3,2,1,0:T(2,128)(2,1)} %bitcast.23, s32[6,2,12]{2,1,0:T(2,128)} %bitcast.24), custom_call_target="tpu_custom_call" | custom-call | flops 100000000 | bytes 100000 | tf_op jit(solution)/shard_map/pack/pallas_call | solution.py:465
  2.5 0.1 collective-permute-start
  2.6 3.2 %collective-permute-start.1 = (bf16[51,2,512]{2,1,0:T(2,128)(2,1)}, bf16[51,2,512]{2,1,0:T(2,128)(2,1)S(1)}, u32[]{:S(2)}, u32[]{:S(2)}) collective-permute-start(bf16[51,2,512]{2,1,0:T(2,128)(2,1)} %get-tuple-element.18), channel_id=1, source_target_pairs={{0,33},{1,226},{2,35},{3,228},{4,37},{5,230},{6,39},{7,232},{8,41}... | collective-permute-start | bytes 313352 | tf_op jit(solution)/shard_map/ppermute | solution.py:489
  5.8 2.6 %collective-permute-start.2 = (bf16[51,2,512]{2,1,0:T(2,128)(2,1)}, bf16[51,2,512]{2,1,0:T(2,128)(2,1)S(1)}, u32[]{:S(2)}, u32[]{:S(2)}) collective-permute-start(bf16[51,2,512]{2,1,0:T(2,128)(2,1)} %get-tuple-element.19), channel_id=1, source_target_pairs={{0,224},{1,33},{2,226},{3,35},{4,228},{5,37},{6,230},{7,39},{8,232... | collective-permute-start | bytes 313352 | tf_op jit(solution)/shard_map/ppermute | solution.py:489
  8.3 1.0 %pad_add_fusion.inputs_ref = f32[160,768]{1,0:T(8,128)S(1)} fusion(f32[8,759]{1,0:T(8,128)} %param.39, f32[8,759]{1,0:T(8,128)} %param.32, s32[144,144]{1,0:T(8,128)} %param.25), kind=kLoop, calls=%fused_computation | loop fusion | flops 368640 | bytes 623040 | tf_op jit(solution)/shard_map/add | solution.py:334
  9.3 0.0 copy-start
  9.3 0.0 copy-start.1
  9.4 0.0 copy-start.2
  9.4 0.0 copy-start.3
  9.4 0.0 copy-start.6
  9.4 0.0 copy-start.7
  9.4 0.0 copy-start.9
  9.4 0.0 copy-start.10
  9.5 0.0 copy-start.13
  9.5 0.0 copy-start.14
  9.5 4.1 %lookup.1 = (f32[2304,128]{1,0:T(8,128)S(1)}, f32[288,128]{1,0:T(8,128)S(1)}) custom-call(f32[160,768]{1,0:T(8,128)S(1)} %pad_add_fusion.inputs_ref), custom_call_target="tpu_custom_call" | custom-call | flops 3000000000 | bytes 4000000 | tf_op jit(solution)/shard_map/lookup/pallas_call | solution.py:335
  13.6 0.5 %collective-permute-done.1.b3 = bf16[51,2,512]{2,1,0:T(2,128)(2,1)S(1)} collective-permute-done((bf16[51,2,512]{2,1,0:T(2,128)(2,1)}, bf16[51,2,512]{2,1,0:T(2,128)(2,1)S(1)}, u32[]{:S(2)}, u32[]{:S(2)}) %collective-permute-start.1) | collective-permute-done | bytes 104480 | tf_op jit(solution)/shard_map/ppermute | solution.py:489
  14.3 9.1 %main.1 = (bf16[48,2,512]{2,1,0:T(2,128)(2,1)S(1)}, bf16[48,2,512]{2,1,0:T(2,128)(2,1)S(1)}, bf16[48,2,512]{2,1,0:T(2,128)(2,1)S(1)}, bf16[48,2,512]{2,1,0:T(2,128)(2,1)S(1)}) custom-call(bf16[51,2,512]{2,1,0:T(2,128)(2,1)S(1)} %copy-done.5, bf16[51,2,512]{2,1,0:T(2,128)(2,1)S(1)} %collective-permute-done.b1, ...), custom_call_target="tpu_custom_call" | custom-call | flops 8000000000 | bytes 8000000 | tf_op jit(solution)/shard_map/main/pallas_call | solution.py:465
  23.4 2.5 %collective-permute-start.3 = (bf16[48,2,512]{2,1,0:T(2,128)(2,1)S(1)}, bf16[48,2,512]{2,1,0:T(2,128)(2,1)S(1)}, u32[]{:S(2)}, u32[]{:S(2)}) collective-permute-start(bf16[48,2,512]{2,1,0:T(2,128)(2,1)S(1)} %get-tuple-element.23), channel_id=1, source_target_pairs={{1,0},{2,1},{3,2},{4,3},{5,4},{6,5},{7,6},{8,7},{9,8},{10,9},{11,1... | collective-permute-start | bytes 294920 | tf_op jit(solution)/shard_map/ppermute | solution.py:489
  25.9 1.6 %collective-permute-start.4 = (bf16[48,2,512]{2,1,0:T(2,128)(2,1)S(1)}, bf16[48,2,512]{2,1,0:T(2,128)(2,1)S(1)}, u32[]{:S(2)}, u32[]{:S(2)}) collective-permute-start(bf16[48,2,512]{2,1,0:T(2,128)(2,1)S(1)} %get-tuple-element.24), channel_id=1, source_target_pairs={{33,0},{226,1},{35,2},{228,3},{37,4},{230,5},{39,6},{232,7},{41,8}... | collective-permute-start | bytes 294920 | tf_op jit(solution)/shard_map/ppermute | solution.py:489
  27.6 1.3 %collective-permute-start.5 = (bf16[48,2,512]{2,1,0:T(2,128)(2,1)S(1)}, bf16[48,2,512]{2,1,0:T(2,128)(2,1)S(1)}, u32[]{:S(2)}, u32[]{:S(2)}) collective-permute-start(bf16[48,2,512]{2,1,0:T(2,128)(2,1)S(1)} %get-tuple-element.25), channel_id=1, source_target_pairs={{224,0},{33,1},{226,2},{35,3},{228,4},{37,5},{230,6},{39,7},{232,8... | collective-permute-start | bytes 294920 | tf_op jit(solution)/shard_map/ppermute | solution.py:489
  28.9 1.1 %collective-permute-done.4.h3 = bf16[48,2,512]{2,1,0:T(2,128)(2,1)S(1)} collective-permute-done((bf16[48,2,512]{2,1,0:T(2,128)(2,1)S(1)}, bf16[48,2,512]{2,1,0:T(2,128)(2,1)S(1)}, u32[]{:S(2)}, u32[]{:S(2)}) %collective-permute-start.4) | collective-permute-done | bytes 98336 | tf_op jit(solution)/shard_map/ppermute | solution.py:489
  30.0 4.3 %collective-permute-done.5.h2 = bf16[48,2,512]{2,1,0:T(2,128)(2,1)S(1)} collective-permute-done((bf16[48,2,512]{2,1,0:T(2,128)(2,1)S(1)}, bf16[48,2,512]{2,1,0:T(2,128)(2,1)S(1)}, u32[]{:S(2)}, u32[]{:S(2)}) %collective-permute-start.5) | collective-permute-done | bytes 98336 | tf_op jit(solution)/shard_map/ppermute | solution.py:489
  34.3 1.0 %home.1 = (bf16[6,12,2,512]{3,2,1,0:T(2,128)(2,1)}, bf16[6,12,2,512]{3,2,1,0:T(2,128)(2,1)}, bf16[3,6,2,1024]{3,2,1,0:T(2,128)(2,1)}) custom-call(bf16[48,2,512]{2,1,0:T(2,128)(2,1)S(1)} %get-tuple-element.22.h0, bf16[48,2,512]{2,1,0:T(2,128)(2,1)S(1)} %collective-permute-done.3.h1, bf16[48,2,512]{2,1,0:T(2,128)(2,1)S(1)} %collective-permute-done.4.h3, ...), custom_call_target="tpu_custom_call" | custom-call | flops 1000000 | bytes 1000 | tf_op jit(solution)/shard_map/home/pallas_call | solution.py:465
  (23 shorter events, 0.1 us)
Async XLA Ops:
  2.5 11.1 %collective-permute-start = (bf16[51,2,512]{2,1,0:T(2,128)(2,1)}, bf16[51,2,512]{2,1,0:T(2,128)(2,1)S(1)}, u32[]{:S(2)}, u32[]{:S(2)}) collective-permute-start(bf16[51,2,512]{2,1,0:T(2,128)(2,1)} %get-tuple-element.17), channel_id=1, source_target_pairs={{0,1},{1,2},{2,3},{3,4},{4,5},{5,6},{6,7},{7,8},{8,9},{9,10},{10,1... | collective-permute-start | bytes 313352 | tf_op jit(solution)/shard_map/ppermute | solution.py:489
  2.6 11.6 %collective-permute-start.1 = (bf16[51,2,512]{2,1,0:T(2,128)(2,1)}, bf16[51,2,512]{2,1,0:T(2,128)(2,1)S(1)}, u32[]{:S(2)}, u32[]{:S(2)}) collective-permute-start(bf16[51,2,512]{2,1,0:T(2,128)(2,1)} %get-tuple-element.18), channel_id=1, source_target_pairs={{0,33},{1,226},{2,35},{3,228},{4,37},{5,230},{6,39},{7,232},{8,41}... | collective-permute-start | bytes 313352 | tf_op jit(solution)/shard_map/ppermute | solution.py:489
  5.8 8.4 %collective-permute-start.2 = (bf16[51,2,512]{2,1,0:T(2,128)(2,1)}, bf16[51,2,512]{2,1,0:T(2,128)(2,1)S(1)}, u32[]{:S(2)}, u32[]{:S(2)}) collective-permute-start(bf16[51,2,512]{2,1,0:T(2,128)(2,1)} %get-tuple-element.19), channel_id=1, source_target_pairs={{0,224},{1,33},{2,226},{3,35},{4,228},{5,37},{6,230},{7,39},{8,232... | collective-permute-start | bytes 313352 | tf_op jit(solution)/shard_map/ppermute | solution.py:489
  9.3 4.8 %copy-start = (bf16[1024,2048]{1,0:T(8,128)(2,1)S(1)}, bf16[1024,2048]{1,0:T(8,128)(2,1)}, u32[]{:S(2)}) copy-start(bf16[1024,2048]{1,0:T(8,128)(2,1)} %split.1) | copy-start | bytes 12582916
  9.3 4.8 %copy-start.1 = (bf16[512,1536]{1,0:T(8,128)(2,1)S(1)}, bf16[512,1536]{1,0:T(8,128)(2,1)}, u32[]{:S(2)}) copy-start(bf16[512,1536]{1,0:T(8,128)(2,1)} %e_weight.1) | copy-start | bytes 4718596
  9.4 4.8 %copy-start.2 = (bf16[512,1536]{1,0:T(8,128)(2,1)S(1)}, bf16[512,1536]{1,0:T(8,128)(2,1)}, u32[]{:S(2)}) copy-start(bf16[512,1536]{1,0:T(8,128)(2,1)} %d_weight.1) | copy-start | bytes 4718596
  9.4 4.8 %copy-start.3 = (bf16[512,512]{1,0:T(8,128)(2,1)S(1)}, bf16[512,512]{1,0:T(8,128)(2,1)}, u32[]{:S(2)}) copy-start(bf16[512,512]{1,0:T(8,128)(2,1)} %e_out_weight.1) | copy-start | bytes 1572868
  9.4 4.8 %copy-start.4 = (bf16[512,512]{1,0:T(8,128)(2,1)S(1)}, bf16[512,512]{1,0:T(8,128)(2,1)}, u32[]{:S(2)}) copy-start(bf16[512,512]{1,0:T(8,128)(2,1)} %d_out_weight.1) | copy-start | bytes 1572868
  9.4 4.8 %copy-start.5 = (bf16[51,2,512]{2,1,0:T(2,128)(2,1)S(1)}, bf16[51,2,512]{2,1,0:T(2,128)(2,1)}, u32[]{:S(2)}) copy-start(bf16[51,2,512]{2,1,0:T(2,128)(2,1)} %get-tuple-element.16.b0) | copy-start | bytes 313348
  9.4 4.8 %copy-start.6 = (f32[1536]{0:T(1024)S(1)}, f32[1536]{0:T(1024)}, u32[]{:S(2)}) copy-start(f32[1536]{0:T(1024)} %e_bias.1) | copy-start | bytes 18436
  9.4 4.8 %copy-start.7 = (f32[1536]{0:T(1024)S(1)}, f32[1536]{0:T(1024)}, u32[]{:S(2)}) copy-start(f32[1536]{0:T(1024)} %d_bias.1) | copy-start | bytes 18436
  9.4 4.8 %copy-start.8 = (f32[2048]{0:T(1024)S(1)}, f32[2048]{0:T(1024)}, u32[]{:S(2)}) copy-start(f32[2048]{0:T(1024)} %param.41) | copy-start | bytes 24580
  9.4 4.8 %copy-start.9 = (f32[512]{0:T(512)S(1)}, f32[512]{0:T(512)}, u32[]{:S(2)}) copy-start(f32[512]{0:T(512)} %param.26) | copy-start | bytes 6148
  9.4 4.8 %copy-start.10 = (f32[512]{0:T(512)S(1)}, f32[512]{0:T(512)}, u32[]{:S(2)}) copy-start(f32[512]{0:T(512)} %param.27) | copy-start | bytes 6148
  9.5 4.8 %copy-start.11 = (f32[512]{0:T(512)S(1)}, f32[512]{0:T(512)}, u32[]{:S(2)}) copy-start(f32[512]{0:T(512)} %param.31) | copy-start | bytes 6148
  9.5 4.8 %copy-start.12 = (f32[512]{0:T(512)S(1)}, f32[512]{0:T(512)}, u32[]{:S(2)}) copy-start(f32[512]{0:T(512)} %param.33) | copy-start | bytes 6148
  9.5 4.8 %copy-start.13 = (f32[512]{0:T(512)S(1)}, f32[512]{0:T(512)}, u32[]{:S(2)}) copy-start(f32[512]{0:T(512)} %param.34) | copy-start | bytes 6148
  9.5 4.8 %copy-start.14 = (f32[512]{0:T(512)S(1)}, f32[512]{0:T(512)}, u32[]{:S(2)}) copy-start(f32[512]{0:T(512)} %param.38) | copy-start | bytes 6148
  23.4 5.5 %collective-permute-start.3 = (bf16[48,2,512]{2,1,0:T(2,128)(2,1)S(1)}, bf16[48,2,512]{2,1,0:T(2,128)(2,1)S(1)}, u32[]{:S(2)}, u32[]{:S(2)}) collective-permute-start(bf16[48,2,512]{2,1,0:T(2,128)(2,1)S(1)} %get-tuple-element.23), channel_id=1, source_target_pairs={{1,0},{2,1},{3,2},{4,3},{5,4},{6,5},{7,6},{8,7},{9,8},{10,9},{11,1... | collective-permute-start | bytes 294920 | tf_op jit(solution)/shard_map/ppermute | solution.py:489
  25.9 4.0 %collective-permute-start.4 = (bf16[48,2,512]{2,1,0:T(2,128)(2,1)S(1)}, bf16[48,2,512]{2,1,0:T(2,128)(2,1)S(1)}, u32[]{:S(2)}, u32[]{:S(2)}) collective-permute-start(bf16[48,2,512]{2,1,0:T(2,128)(2,1)S(1)} %get-tuple-element.24), channel_id=1, source_target_pairs={{33,0},{226,1},{35,2},{228,3},{37,4},{230,5},{39,6},{232,7},{41,8}... | collective-permute-start | bytes 294920 | tf_op jit(solution)/shard_map/ppermute | solution.py:489
  27.6 6.7 %collective-permute-start.5 = (bf16[48,2,512]{2,1,0:T(2,128)(2,1)S(1)}, bf16[48,2,512]{2,1,0:T(2,128)(2,1)S(1)}, u32[]{:S(2)}, u32[]{:S(2)}) collective-permute-start(bf16[48,2,512]{2,1,0:T(2,128)(2,1)S(1)} %get-tuple-element.25), channel_id=1, source_target_pairs={{224,0},{33,1},{226,2},{35,3},{228,4},{37,5},{230,6},{39,7},{232,8... | collective-permute-start | bytes 294920 | tf_op jit(solution)/shard_map/ppermute | solution.py:489

commit v10 on v9

--- a/solution.py
+++ b/solution.py
@@ -131,8 +131,10 @@
     return [jnp.where(column == queries, 0.0, BLANK) for queries in (label[:, :FIRST], label[:, WIDE:])]
 
 
-def project(x, gain, offset, weight, bias, qkv_ref):
-    xhat, _ = normalise(x)
+def project(x, gain, offset, weight, bias, qkv_ref, xhat_ref, rstd_ref):
+    xhat, rstd = normalise(x)
+    xhat_ref[...] = xhat
+    rstd_ref[...] = rstd
     normed = (xhat * gain + offset).astype(bf16)
     queries = (dot(normed, weight[:, :D]) + bias[:, :D]).astype(bf16) * jnp.array(HEAD**-0.5, bf16)
     qkv_ref[:, :D] = queries
@@ -161,7 +163,7 @@
     return x + dot(heads_out, out_weight) + out_bias
 
 
-def block_backward(grad, dheads, x, gain, weight, qkv_ref, probs_ref, dqkv_ref):
+def block_backward(grad, dheads, gain, weight, qkv_ref, probs_ref, dqkv_ref, xhat_ref, rstd_ref):
     keys, values = qkv_ref[:, D : 2 * D], qkv_ref[:, 2 * D :]
 
     def harden(dprobs, columns):
@@ -184,9 +186,9 @@
         dv = dot(probs_ref[:, columns_of(g)], do4) + dv_rest[:, lanes]
         dqkv_ref[:, pl.ds(2 * D + g * 256, 256)] = dv.astype(bf16)
     dnormed = dot_nt(dqkv_ref[...], weight)
-    xhat, rstd = normalise(x)
+    xhat = xhat_ref[...]
     dxhat = dnormed * gain
-    dx = rstd * (
+    dx = rstd_ref[...] * (
         dxhat
         - jnp.mean(dxhat, axis=-1, keepdims=True)
         - xhat * jnp.mean(dxhat * xhat, axis=-1, keepdims=True)
@@ -369,7 +371,7 @@
     e_weight, e_out_weight, d_weight, d_out_weight, split,
     o0, o1, o2, o3,
     in_tokens, in_cotangent, out_decoded, out_tokens, coarse, coarse_grad,
-    e_qkv, e_probs, d_qkv, d_probs, d_dqkv, e_dqkv,
+    e_qkv, e_probs, d_qkv, d_probs, d_dqkv, e_dqkv, e_xhat, d_xhat, e_rstd, d_rstd,
 ):
     def bias_tiles(block):
         def tile(h):
@@ -383,7 +385,7 @@
     parts, outs = (b0, b1, b2, b3), (o0, o1, o2, o3)
     gather_quadrants(parts, 0, in_tokens, parity)
     tokens = whole(in_tokens)
-    project(tokens, e_gain[...], e_offset[...], e_weight, e_bias[...].reshape(1, -1), e_qkv)
+    project(tokens, e_gain[...], e_offset[...], e_weight, e_bias[...].reshape(1, -1), e_qkv, e_xhat, e_rstd)
     blank = mask_bias(parts, lats, parity)
 
     for q, ref in enumerate(parts):
@@ -405,9 +407,9 @@
 
     encoded = attend(tokens, blank, bias_tiles(0), e_out_weight[...], e_out_bias[...], e_qkv, e_probs).astype(bf16)
     joined = (encoded.astype(f32) + upsampled).astype(bf16).astype(f32)
-    project(joined, d_gain[...], d_offset[...], d_weight, d_bias[...].reshape(1, -1), d_qkv)
+    project(joined, d_gain[...], d_offset[...], d_weight, d_bias[...].reshape(1, -1), d_qkv, d_xhat, d_rstd)
     decoded = attend(joined, blank, bias_tiles(1), d_out_weight[...], d_out_bias[...], d_qkv, d_probs)
-    dx = block_backward(grad, dheads, joined, d_gain[...], d_weight[...], d_qkv, d_probs, d_dqkv)
+    dx = block_backward(grad, dheads, d_gain[...], d_weight[...], d_qkv, d_probs, d_dqkv, d_xhat, d_rstd)
     fill(out_decoded, decoded)
     scatter_quadrants(out_decoded, outs, 0, parity)
 
@@ -418,7 +420,7 @@
     spread = dot(places, grad).astype(bf16)
     spread = jnp.concatenate([spread[POINT_ROWS * k : POINT_ROWS * (k + 1)] for k in range(4)], axis=1)
     fill(coarse_grad, dot_nt(spread, split[...]))
-    dx = block_backward(grad, dheads, tokens, e_gain[...], e_weight[...], e_qkv, e_probs, e_dqkv)
+    dx = block_backward(grad, dheads, e_gain[...], e_weight[...], e_qkv, e_probs, e_dqkv, e_xhat, e_rstd)
     for q, ref in enumerate(outs):
         m, n = divmod(q, 2)
         for half in range(2):
@@ -553,6 +555,10 @@
             pltpu.VMEM((SPAN, HEADS * SPAN), bf16),
             pltpu.VMEM((SPAN, 3 * D), bf16),
             pltpu.VMEM((SPAN, 3 * D), bf16),
+            pltpu.VMEM((SPAN, D), f32),
+            pltpu.VMEM((SPAN, D), f32),
+            pltpu.VMEM((SPAN, 1), f32),
+            pltpu.VMEM((SPAN, 1), f32),
         ],
         8_000_000_000,
     )

time: 35.4 us -> 35.4 us (level)
  no operation moved by 1% of the time
where the time goes in v10:
time: 35.4 us; the launch traced here: 35.3 us
  Pallas kernels  16 us (45%)
  starting transfers between devices  11.3 us (32%)
  waiting for transfers between devices  5.99 us (17%)
  other arithmetic  0.98 us (3%)
  between operations  0.89 us (3%)
    pallas_call x3, Pallas kernels, call(): pl.pallas_call(kernel, out_shape=outs, in_specs=in_specs or [VM] * len(in...  12 us
    ppermute x6, starting transfers between devices, exchange(): out[q] = lax.ppermute(pieces[q], ('lat', 'lon'), pairs)  11.3 us
    ppermute x6, waiting for transfers between devices, exchange(): out[q] = lax.ppermute(pieces[q], ('lat', 'lon'), pairs)  5.99 us
    pallas_call x1, Pallas kernels, lookup(): pl.pallas_call(lookup_kernel, out_shape=[jax.ShapeDtypeStruct((2 * HEADS...  4.08 us
    add x1, other arithmetic, lookup(): placed(relative_index, 0).astype(f32) + placed(encoder_table, SPAN)  0.98 us
  transfers between devices with their start and end apart: 6, of which 3 were waited for; matrix products, arithmetic and copies ran while one was open for 3% of the time, Pallas kernels for 12%

profile of v10, /device:TPU:2, one launch (start us, length us, event | category | flops | bytes accessed | tf_op | source)
XLA Modules:
  0.0 35.3 jit_solution(8386366992935193323)
XLA Ops:
  0.6 1.9 %pack.1 = (bf16[51,2,512]{2,1,0:T(2,128)(2,1)}, bf16[51,2,512]{2,1,0:T(2,128)(2,1)}, bf16[51,2,512]{2,1,0:T(2,128)(2,1)}, bf16[51,2,512]{2,1,0:T(2,128)(2,1)}) custom-call(bf16[6,12,2,512]{3,2,1,0:T(2,128)(2,1)} %bitcast.21, bf16[6,12,2,512]{3,2,1,0:T(2,128)(2,1)} %bitcast.22, bf16[3,6,2,1024]{3,2,1,0:T(2,128)(2,1)} %bitcast.23, s32[6,2,12]{2,1,0:T(2,128)} %bitcast.24), custom_call_target="tpu_custom_call" | custom-call | flops 100000000 | bytes 100000 | tf_op jit(solution)/shard_map/pack/pallas_call | solution.py:467
  2.5 0.1 collective-permute-start
  2.6 3.2 %collective-permute-start.1 = (bf16[51,2,512]{2,1,0:T(2,128)(2,1)}, bf16[51,2,512]{2,1,0:T(2,128)(2,1)S(1)}, u32[]{:S(2)}, u32[]{:S(2)}) collective-permute-start(bf16[51,2,512]{2,1,0:T(2,128)(2,1)} %get-tuple-element.18), channel_id=1, source_target_pairs={{0,33},{1,226},{2,35},{3,228},{4,37},{5,230},{6,39},{7,232},{8,41}... | collective-permute-start | bytes 313352 | tf_op jit(solution)/shard_map/ppermute | solution.py:491
  5.8 2.6 %collective-permute-start.2 = (bf16[51,2,512]{2,1,0:T(2,128)(2,1)}, bf16[51,2,512]{2,1,0:T(2,128)(2,1)S(1)}, u32[]{:S(2)}, u32[]{:S(2)}) collective-permute-start(bf16[51,2,512]{2,1,0:T(2,128)(2,1)} %get-tuple-element.19), channel_id=1, source_target_pairs={{0,224},{1,33},{2,226},{3,35},{4,228},{5,37},{6,230},{7,39},{8,232... | collective-permute-start | bytes 313352 | tf_op jit(solution)/shard_map/ppermute | solution.py:491
  8.3 1.0 %pad_add_fusion.inputs_ref = f32[160,768]{1,0:T(8,128)S(1)} fusion(f32[8,759]{1,0:T(8,128)} %param.39, f32[8,759]{1,0:T(8,128)} %param.32, s32[144,144]{1,0:T(8,128)} %param.25), kind=kLoop, calls=%fused_computation | loop fusion | flops 368640 | bytes 623040 | tf_op jit(solution)/shard_map/add | solution.py:336
  9.3 0.0 copy-start
  9.3 0.0 copy-start.1
  9.4 0.0 copy-start.2
  9.4 0.0 copy-start.3
  9.4 0.0 copy-start.5
  9.4 0.0 copy-start.6
  9.4 0.0 copy-start.8
  9.4 0.0 copy-start.9
  9.5 0.0 copy-start.12
  9.5 0.0 copy-start.13
  9.5 4.1 %lookup.1 = (f32[2304,128]{1,0:T(8,128)S(1)}, f32[288,128]{1,0:T(8,128)S(1)}) custom-call(f32[160,768]{1,0:T(8,128)S(1)} %pad_add_fusion.inputs_ref), custom_call_target="tpu_custom_call" | custom-call | flops 3000000000 | bytes 4000000 | tf_op jit(solution)/shard_map/lookup/pallas_call | solution.py:337
  13.6 0.5 %collective-permute-done.1.b3 = bf16[51,2,512]{2,1,0:T(2,128)(2,1)S(1)} collective-permute-done((bf16[51,2,512]{2,1,0:T(2,128)(2,1)}, bf16[51,2,512]{2,1,0:T(2,128)(2,1)S(1)}, u32[]{:S(2)}, u32[]{:S(2)}) %collective-permute-start.1) | collective-permute-done | bytes 104480 | tf_op jit(solution)/shard_map/ppermute | solution.py:491
  14.3 9.1 %main.1 = (bf16[48,2,512]{2,1,0:T(2,128)(2,1)S(1)}, bf16[48,2,512]{2,1,0:T(2,128)(2,1)S(1)}, bf16[48,2,512]{2,1,0:T(2,128)(2,1)S(1)}, bf16[48,2,512]{2,1,0:T(2,128)(2,1)S(1)}) custom-call(bf16[51,2,512]{2,1,0:T(2,128)(2,1)S(1)} %copy-done.5, bf16[51,2,512]{2,1,0:T(2,128)(2,1)S(1)} %collective-permute-done.b1, ...), custom_call_target="tpu_custom_call" | custom-call | flops 8000000000 | bytes 8000000 | tf_op jit(solution)/shard_map/main/pallas_call | solution.py:467
  23.4 2.5 %collective-permute-start.3 = (bf16[48,2,512]{2,1,0:T(2,128)(2,1)S(1)}, bf16[48,2,512]{2,1,0:T(2,128)(2,1)S(1)}, u32[]{:S(2)}, u32[]{:S(2)}) collective-permute-start(bf16[48,2,512]{2,1,0:T(2,128)(2,1)S(1)} %get-tuple-element.23), channel_id=1, source_target_pairs={{1,0},{2,1},{3,2},{4,3},{5,4},{6,5},{7,6},{8,7},{9,8},{10,9},{11,1... | collective-permute-start | bytes 294920 | tf_op jit(solution)/shard_map/ppermute | solution.py:491
  25.9 1.6 %collective-permute-start.4 = (bf16[48,2,512]{2,1,0:T(2,128)(2,1)S(1)}, bf16[48,2,512]{2,1,0:T(2,128)(2,1)S(1)}, u32[]{:S(2)}, u32[]{:S(2)}) collective-permute-start(bf16[48,2,512]{2,1,0:T(2,128)(2,1)S(1)} %get-tuple-element.24), channel_id=1, source_target_pairs={{33,0},{226,1},{35,2},{228,3},{37,4},{230,5},{39,6},{232,7},{41,8}... | collective-permute-start | bytes 294920 | tf_op jit(solution)/shard_map/ppermute | solution.py:491
  27.6 1.3 %collective-permute-start.5 = (bf16[48,2,512]{2,1,0:T(2,128)(2,1)S(1)}, bf16[48,2,512]{2,1,0:T(2,128)(2,1)S(1)}, u32[]{:S(2)}, u32[]{:S(2)}) collective-permute-start(bf16[48,2,512]{2,1,0:T(2,128)(2,1)S(1)} %get-tuple-element.25), channel_id=1, source_target_pairs={{224,0},{33,1},{226,2},{35,3},{228,4},{37,5},{230,6},{39,7},{232,8... | collective-permute-start | bytes 294920 | tf_op jit(solution)/shard_map/ppermute | solution.py:491
  28.9 1.1 %collective-permute-done.4.h3 = bf16[48,2,512]{2,1,0:T(2,128)(2,1)S(1)} collective-permute-done((bf16[48,2,512]{2,1,0:T(2,128)(2,1)S(1)}, bf16[48,2,512]{2,1,0:T(2,128)(2,1)S(1)}, u32[]{:S(2)}, u32[]{:S(2)}) %collective-permute-start.4) | collective-permute-done | bytes 98336 | tf_op jit(solution)/shard_map/ppermute | solution.py:491
  30.0 4.3 %collective-permute-done.5.h2 = bf16[48,2,512]{2,1,0:T(2,128)(2,1)S(1)} collective-permute-done((bf16[48,2,512]{2,1,0:T(2,128)(2,1)S(1)}, bf16[48,2,512]{2,1,0:T(2,128)(2,1)S(1)}, u32[]{:S(2)}, u32[]{:S(2)}) %collective-permute-start.5) | collective-permute-done | bytes 98336 | tf_op jit(solution)/shard_map/ppermute | solution.py:491
  34.3 1.0 %home.1 = (bf16[6,12,2,512]{3,2,1,0:T(2,128)(2,1)}, bf16[6,12,2,512]{3,2,1,0:T(2,128)(2,1)}, bf16[3,6,2,1024]{3,2,1,0:T(2,128)(2,1)}) custom-call(bf16[48,2,512]{2,1,0:T(2,128)(2,1)S(1)} %get-tuple-element.22.h0, bf16[48,2,512]{2,1,0:T(2,128)(2,1)S(1)} %collective-permute-done.3.h1, bf16[48,2,512]{2,1,0:T(2,128)(2,1)S(1)} %collective-permute-done.4.h3, ...), custom_call_target="tpu_custom_call" | custom-call | flops 1000000 | bytes 1000 | tf_op jit(solution)/shard_map/home/pallas_call | solution.py:467
  (23 shorter events, 0.1 us)
Async XLA Ops:
  2.5 11.1 %collective-permute-start = (bf16[51,2,512]{2,1,0:T(2,128)(2,1)}, bf16[51,2,512]{2,1,0:T(2,128)(2,1)S(1)}, u32[]{:S(2)}, u32[]{:S(2)}) collective-permute-start(bf16[51,2,512]{2,1,0:T(2,128)(2,1)} %get-tuple-element.17), channel_id=1, source_target_pairs={{0,1},{1,2},{2,3},{3,4},{4,5},{5,6},{6,7},{7,8},{8,9},{9,10},{10,1... | collective-permute-start | bytes 313352 | tf_op jit(solution)/shard_map/ppermute | solution.py:491
  2.6 11.6 %collective-permute-start.1 = (bf16[51,2,512]{2,1,0:T(2,128)(2,1)}, bf16[51,2,512]{2,1,0:T(2,128)(2,1)S(1)}, u32[]{:S(2)}, u32[]{:S(2)}) collective-permute-start(bf16[51,2,512]{2,1,0:T(2,128)(2,1)} %get-tuple-element.18), channel_id=1, source_target_pairs={{0,33},{1,226},{2,35},{3,228},{4,37},{5,230},{6,39},{7,232},{8,41}... | collective-permute-start | bytes 313352 | tf_op jit(solution)/shard_map/ppermute | solution.py:491
  5.8 8.4 %collective-permute-start.2 = (bf16[51,2,512]{2,1,0:T(2,128)(2,1)}, bf16[51,2,512]{2,1,0:T(2,128)(2,1)S(1)}, u32[]{:S(2)}, u32[]{:S(2)}) collective-permute-start(bf16[51,2,512]{2,1,0:T(2,128)(2,1)} %get-tuple-element.19), channel_id=1, source_target_pairs={{0,224},{1,33},{2,226},{3,35},{4,228},{5,37},{6,230},{7,39},{8,232... | collective-permute-start | bytes 313352 | tf_op jit(solution)/shard_map/ppermute | solution.py:491
  9.3 4.8 %copy-start = (bf16[1024,2048]{1,0:T(8,128)(2,1)S(1)}, bf16[1024,2048]{1,0:T(8,128)(2,1)}, u32[]{:S(2)}) copy-start(bf16[1024,2048]{1,0:T(8,128)(2,1)} %split.1) | copy-start | bytes 12582916
  9.3 4.8 %copy-start.1 = (bf16[512,1536]{1,0:T(8,128)(2,1)S(1)}, bf16[512,1536]{1,0:T(8,128)(2,1)}, u32[]{:S(2)}) copy-start(bf16[512,1536]{1,0:T(8,128)(2,1)} %e_weight.1) | copy-start | bytes 4718596
  9.4 4.8 %copy-start.2 = (bf16[512,1536]{1,0:T(8,128)(2,1)S(1)}, bf16[512,1536]{1,0:T(8,128)(2,1)}, u32[]{:S(2)}) copy-start(bf16[512,1536]{1,0:T(8,128)(2,1)} %d_weight.1) | copy-start | bytes 4718596
  9.4 4.8 %copy-start.3 = (bf16[512,512]{1,0:T(8,128)(2,1)S(1)}, bf16[512,512]{1,0:T(8,128)(2,1)}, u32[]{:S(2)}) copy-start(bf16[512,512]{1,0:T(8,128)(2,1)} %e_out_weight.1) | copy-start | bytes 1572868
  9.4 4.8 %copy-start.4 = (bf16[512,512]{1,0:T(8,128)(2,1)S(1)}, bf16[512,512]{1,0:T(8,128)(2,1)}, u32[]{:S(2)}) copy-start(bf16[512,512]{1,0:T(8,128)(2,1)} %d_out_weight.1) | copy-start | bytes 1572868
  9.4 4.8 %copy-start.5 = (bf16[51,2,512]{2,1,0:T(2,128)(2,1)S(1)}, bf16[51,2,512]{2,1,0:T(2,128)(2,1)}, u32[]{:S(2)}) copy-start(bf16[51,2,512]{2,1,0:T(2,128)(2,1)} %get-tuple-element.16.b0) | copy-start | bytes 313348
  9.4 4.8 %copy-start.6 = (f32[1536]{0:T(1024)S(1)}, f32[1536]{0:T(1024)}, u32[]{:S(2)}) copy-start(f32[1536]{0:T(1024)} %e_bias.1) | copy-start | bytes 18436
  9.4 4.8 %copy-start.7 = (f32[1536]{0:T(1024)S(1)}, f32[1536]{0:T(1024)}, u32[]{:S(2)}) copy-start(f32[1536]{0:T(1024)} %d_bias.1) | copy-start | bytes 18436
  9.4 4.8 %copy-start.8 = (f32[2048]{0:T(1024)S(1)}, f32[2048]{0:T(1024)}, u32[]{:S(2)}) copy-start(f32[2048]{0:T(1024)} %param.41) | copy-start | bytes 24580
  9.4 4.8 %copy-start.9 = (f32[512]{0:T(512)S(1)}, f32[512]{0:T(512)}, u32[]{:S(2)}) copy-start(f32[512]{0:T(512)} %param.26) | copy-start | bytes 6148
  9.4 4.8 %copy-start.10 = (f32[512]{0:T(512)S(1)}, f32[512]{0:T(512)}, u32[]{:S(2)}) copy-start(f32[512]{0:T(512)} %param.27) | copy-start | bytes 6148
  9.5 4.8 %copy-start.11 = (f32[512]{0:T(512)S(1)}, f32[512]{0:T(512)}, u32[]{:S(2)}) copy-start(f32[512]{0:T(512)} %param.31) | copy-start | bytes 6148
  9.5 4.8 %copy-start.12 = (f32[512]{0:T(512)S(1)}, f32[512]{0:T(512)}, u32[]{:S(2)}) copy-start(f32[512]{0:T(512)} %param.33) | copy-start | bytes 6148
  9.5 4.8 %copy-start.13 = (f32[512]{0:T(512)S(1)}, f32[512]{0:T(512)}, u32[]{:S(2)}) copy-start(f32[512]{0:T(512)} %param.34) | copy-start | bytes 6148
  9.5 4.8 %copy-start.14 = (f32[512]{0:T(512)S(1)}, f32[512]{0:T(512)}, u32[]{:S(2)}) copy-start(f32[512]{0:T(512)} %param.38) | copy-start | bytes 6148
  23.4 5.4 %collective-permute-start.3 = (bf16[48,2,512]{2,1,0:T(2,128)(2,1)S(1)}, bf16[48,2,512]{2,1,0:T(2,128)(2,1)S(1)}, u32[]{:S(2)}, u32[]{:S(2)}) collective-permute-start(bf16[48,2,512]{2,1,0:T(2,128)(2,1)S(1)} %get-tuple-element.23), channel_id=1, source_target_pairs={{1,0},{2,1},{3,2},{4,3},{5,4},{6,5},{7,6},{8,7},{9,8},{10,9},{11,1... | collective-permute-start | bytes 294920 | tf_op jit(solution)/shard_map/ppermute | solution.py:491
  25.9 4.0 %collective-permute-start.4 = (bf16[48,2,512]{2,1,0:T(2,128)(2,1)S(1)}, bf16[48,2,512]{2,1,0:T(2,128)(2,1)S(1)}, u32[]{:S(2)}, u32[]{:S(2)}) collective-permute-start(bf16[48,2,512]{2,1,0:T(2,128)(2,1)S(1)} %get-tuple-element.24), channel_id=1, source_target_pairs={{33,0},{226,1},{35,2},{228,3},{37,4},{230,5},{39,6},{232,7},{41,8}... | collective-permute-start | bytes 294920 | tf_op jit(solution)/shard_map/ppermute | solution.py:491
  27.6 6.7 %collective-permute-start.5 = (bf16[48,2,512]{2,1,0:T(2,128)(2,1)S(1)}, bf16[48,2,512]{2,1,0:T(2,128)(2,1)S(1)}, u32[]{:S(2)}, u32[]{:S(2)}) collective-permute-start(bf16[48,2,512]{2,1,0:T(2,128)(2,1)S(1)} %get-tuple-element.25), channel_id=1, source_target_pairs={{224,0},{33,1},{226,2},{35,3},{228,4},{37,5},{230,6},{39,7},{232,8... | collective-permute-start | bytes 294920 | tf_op jit(solution)/shard_map/ppermute | solution.py:491

commit v11 on v10

--- a/solution.py
+++ b/solution.py
@@ -430,7 +430,7 @@
     scatter_quadrants(out_tokens, outs, PAIRS, parity)
 
 
-def home_kernel(h0, h1, h3, h2, decoded, tokens_gradient, coarse_gradient, total, rounded, sems):
+def home_kernel(h0, h1, h2, h3, decoded, tokens_gradient, coarse_gradient, total, rounded, sems):
     refs = (h0, h1, h2, h3)
     copies = []
 
@@ -568,7 +568,7 @@
     results = call(
         home_kernel,
         "home",
-        [home[0], home[1], home[3], home[2]],
+        list(home),
         [grid, grid, low],
         [
             pltpu.VMEM((WIN_LAT // 2, WIN_LON // 2, LEVELS, 2 * D), f32),

time: 35.4 us -> 37.1 us (1.048)
  the two profiles are of different devices: /device:TPU:2 before, /device:TPU:97 now
where the time goes in v11:
time: 37.1 us; the launch traced here: 37 us
  Pallas kernels  16 us (43%)
  starting transfers between devices  11.1 us (30%)
  waiting for transfers between devices  7.93 us (21%)
  other arithmetic  0.98 us (3%)
  between operations  0.88 us (2%)
    pallas_call x3, Pallas kernels, call(): pl.pallas_call(kernel, out_shape=outs, in_specs=in_specs or [VM] * len(in...  12 us
    ppermute x6, starting transfers between devices, exchange(): out[q] = lax.ppermute(pieces[q], ('lat', 'lon'), pairs)  11.1 us
    ppermute x6, waiting for transfers between devices, exchange(): out[q] = lax.ppermute(pieces[q], ('lat', 'lon'), pairs)  7.93 us
    pallas_call x1, Pallas kernels, lookup(): pl.pallas_call(lookup_kernel, out_shape=[jax.ShapeDtypeStruct((2 * HEADS...  4.08 us
    add x1, other arithmetic, lookup(): placed(relative_index, 0).astype(f32) + placed(encoder_table, SPAN)  0.98 us
  transfers between devices with their start and end apart: 6, of which 3 were waited for; matrix products, arithmetic and copies ran while one was open for 3% of the time, Pallas kernels for 11%

profile of v11, /device:TPU:97, one launch (start us, length us, event | category | flops | bytes accessed | tf_op | source)
XLA Modules:
  0.0 37.0 jit_solution(15513584132385484016)
XLA Ops:
  0.6 1.9 %pack.1 = (bf16[51,2,512]{2,1,0:T(2,128)(2,1)}, bf16[51,2,512]{2,1,0:T(2,128)(2,1)}, bf16[51,2,512]{2,1,0:T(2,128)(2,1)}, bf16[51,2,512]{2,1,0:T(2,128)(2,1)}) custom-call(bf16[6,12,2,512]{3,2,1,0:T(2,128)(2,1)} %bitcast.21, bf16[6,12,2,512]{3,2,1,0:T(2,128)(2,1)} %bitcast.22, bf16[3,6,2,1024]{3,2,1,0:T(2,128)(2,1)} %bitcast.23, s32[6,2,12]{2,1,0:T(2,128)} %bitcast.24), custom_call_target="tpu_custom_call" | custom-call | flops 100000000 | bytes 100000 | tf_op jit(solution)/shard_map/pack/pallas_call | solution.py:467
  2.5 3.5 %collective-permute-start = (bf16[51,2,512]{2,1,0:T(2,128)(2,1)}, bf16[51,2,512]{2,1,0:T(2,128)(2,1)S(1)}, u32[]{:S(2)}, u32[]{:S(2)}) collective-permute-start(bf16[51,2,512]{2,1,0:T(2,128)(2,1)} %get-tuple-element.17), channel_id=1, source_target_pairs={{0,1},{1,2},{2,3},{3,4},{4,5},{5,6},{6,7},{7,8},{8,9},{9,10},{10,1... | collective-permute-start | bytes 313352 | tf_op jit(solution)/shard_map/ppermute | solution.py:491
  6.0 3.5 %collective-permute-start.1 = (bf16[51,2,512]{2,1,0:T(2,128)(2,1)}, bf16[51,2,512]{2,1,0:T(2,128)(2,1)S(1)}, u32[]{:S(2)}, u32[]{:S(2)}) collective-permute-start(bf16[51,2,512]{2,1,0:T(2,128)(2,1)} %get-tuple-element.18), channel_id=1, source_target_pairs={{0,33},{1,226},{2,35},{3,228},{4,37},{5,230},{6,39},{7,232},{8,41}... | collective-permute-start | bytes 313352 | tf_op jit(solution)/shard_map/ppermute | solution.py:491
  9.5 1.0 %pad_add_fusion.inputs_ref = f32[160,768]{1,0:T(8,128)S(1)} fusion(f32[8,759]{1,0:T(8,128)} %param.39, f32[8,759]{1,0:T(8,128)} %param.32, s32[144,144]{1,0:T(8,128)} %param.25), kind=kLoop, calls=%fused_computation | loop fusion | flops 368640 | bytes 623040 | tf_op jit(solution)/shard_map/add | solution.py:336
  10.4 0.0 copy-start
  10.4 0.0 copy-start.1
  10.5 0.0 copy-start.2
  10.5 0.0 copy-start.3
  10.5 0.0 copy-start.4
  10.5 0.0 copy-start.5
  10.5 0.0 copy-start.6
  10.5 0.0 copy-start.9
  10.6 0.0 copy-start.10
  10.6 0.0 copy-start.13
  10.6 0.0 copy-start.14
  10.6 4.1 %lookup.1 = (f32[2304,128]{1,0:T(8,128)S(1)}, f32[288,128]{1,0:T(8,128)S(1)}) custom-call(f32[160,768]{1,0:T(8,128)S(1)} %pad_add_fusion.inputs_ref), custom_call_target="tpu_custom_call" | custom-call | flops 3000000000 | bytes 4000000 | tf_op jit(solution)/shard_map/lookup/pallas_call | solution.py:337
  14.7 0.6 %collective-permute-done.2.b2 = bf16[51,2,512]{2,1,0:T(2,128)(2,1)S(1)} collective-permute-done((bf16[51,2,512]{2,1,0:T(2,128)(2,1)}, bf16[51,2,512]{2,1,0:T(2,128)(2,1)S(1)}, u32[]{:S(2)}, u32[]{:S(2)}) %collective-permute-start.2) | collective-permute-done | bytes 104480 | tf_op jit(solution)/shard_map/ppermute | solution.py:491
  15.4 9.1 %main.1 = (bf16[48,2,512]{2,1,0:T(2,128)(2,1)S(1)}, bf16[48,2,512]{2,1,0:T(2,128)(2,1)S(1)}, bf16[48,2,512]{2,1,0:T(2,128)(2,1)S(1)}, bf16[48,2,512]{2,1,0:T(2,128)(2,1)S(1)}) custom-call(bf16[51,2,512]{2,1,0:T(2,128)(2,1)S(1)} %copy-done.5, bf16[51,2,512]{2,1,0:T(2,128)(2,1)S(1)} %collective-permute-done.b1, ...), custom_call_target="tpu_custom_call" | custom-call | flops 8000000000 | bytes 8000000 | tf_op jit(solution)/shard_map/main/pallas_call | solution.py:467
  24.6 0.3 collective-permute-start.3
  24.8 2.9 %collective-permute-start.4 = (bf16[48,2,512]{2,1,0:T(2,128)(2,1)S(1)}, bf16[48,2,512]{2,1,0:T(2,128)(2,1)S(1)}, u32[]{:S(2)}, u32[]{:S(2)}) collective-permute-start(bf16[48,2,512]{2,1,0:T(2,128)(2,1)S(1)} %get-tuple-element.24), channel_id=1, source_target_pairs={{224,0},{33,1},{226,2},{35,3},{228,4},{37,5},{230,6},{39,7},{232,8... | collective-permute-start | bytes 294920 | tf_op jit(solution)/shard_map/ppermute | solution.py:491
  27.7 0.9 %collective-permute-start.5 = (bf16[48,2,512]{2,1,0:T(2,128)(2,1)S(1)}, bf16[48,2,512]{2,1,0:T(2,128)(2,1)S(1)}, u32[]{:S(2)}, u32[]{:S(2)}) collective-permute-start(bf16[48,2,512]{2,1,0:T(2,128)(2,1)S(1)} %get-tuple-element.25), channel_id=1, source_target_pairs={{33,0},{226,1},{35,2},{228,3},{37,4},{230,5},{39,6},{232,7},{41,8}... | collective-permute-start | bytes 294920 | tf_op jit(solution)/shard_map/ppermute | solution.py:491
  28.7 1.2 %collective-permute-done.3.h1 = bf16[48,2,512]{2,1,0:T(2,128)(2,1)S(1)} collective-permute-done((bf16[48,2,512]{2,1,0:T(2,128)(2,1)S(1)}, bf16[48,2,512]{2,1,0:T(2,128)(2,1)S(1)}, u32[]{:S(2)}, u32[]{:S(2)}) %collective-permute-start.3) | collective-permute-done | bytes 98336 | tf_op jit(solution)/shard_map/ppermute | solution.py:491
  29.9 6.1 %collective-permute-done.5.h3 = bf16[48,2,512]{2,1,0:T(2,128)(2,1)S(1)} collective-permute-done((bf16[48,2,512]{2,1,0:T(2,128)(2,1)S(1)}, bf16[48,2,512]{2,1,0:T(2,128)(2,1)S(1)}, u32[]{:S(2)}, u32[]{:S(2)}) %collective-permute-start.5) | collective-permute-done | bytes 98336 | tf_op jit(solution)/shard_map/ppermute | solution.py:491
  36.0 1.0 %home.1 = (bf16[6,12,2,512]{3,2,1,0:T(2,128)(2,1)}, bf16[6,12,2,512]{3,2,1,0:T(2,128)(2,1)}, bf16[3,6,2,1024]{3,2,1,0:T(2,128)(2,1)}) custom-call(bf16[48,2,512]{2,1,0:T(2,128)(2,1)S(1)} %get-tuple-element.22.h0, bf16[48,2,512]{2,1,0:T(2,128)(2,1)S(1)} %collective-permute-done.3.h1, bf16[48,2,512]{2,1,0:T(2,128)(2,1)S(1)} %collective-permute-done.4.h2, ...), custom_call_target="tpu_custom_call" | custom-call | flops 1000000 | bytes 1000 | tf_op jit(solution)/shard_map/home/pallas_call | solution.py:467
  (23 shorter events, 0.1 us)
Async XLA Ops:
  2.5 12.2 %collective-permute-start = (bf16[51,2,512]{2,1,0:T(2,128)(2,1)}, bf16[51,2,512]{2,1,0:T(2,128)(2,1)S(1)}, u32[]{:S(2)}, u32[]{:S(2)}) collective-permute-start(bf16[51,2,512]{2,1,0:T(2,128)(2,1)} %get-tuple-element.17), channel_id=1, source_target_pairs={{0,1},{1,2},{2,3},{3,4},{4,5},{5,6},{6,7},{7,8},{8,9},{9,10},{10,1... | collective-permute-start | bytes 313352 | tf_op jit(solution)/shard_map/ppermute | solution.py:491
  6.0 8.7 %collective-permute-start.1 = (bf16[51,2,512]{2,1,0:T(2,128)(2,1)}, bf16[51,2,512]{2,1,0:T(2,128)(2,1)S(1)}, u32[]{:S(2)}, u32[]{:S(2)}) collective-permute-start(bf16[51,2,512]{2,1,0:T(2,128)(2,1)} %get-tuple-element.18), channel_id=1, source_target_pairs={{0,33},{1,226},{2,35},{3,228},{4,37},{5,230},{6,39},{7,232},{8,41}... | collective-permute-start | bytes 313352 | tf_op jit(solution)/shard_map/ppermute | solution.py:491
  9.4 5.9 %collective-permute-start.2 = (bf16[51,2,512]{2,1,0:T(2,128)(2,1)}, bf16[51,2,512]{2,1,0:T(2,128)(2,1)S(1)}, u32[]{:S(2)}, u32[]{:S(2)}) collective-permute-start(bf16[51,2,512]{2,1,0:T(2,128)(2,1)} %get-tuple-element.19), channel_id=1, source_target_pairs={{0,224},{1,33},{2,226},{3,35},{4,228},{5,37},{6,230},{7,39},{8,232... | collective-permute-start | bytes 313352 | tf_op jit(solution)/shard_map/ppermute | solution.py:491
  10.4 4.9 %copy-start = (bf16[1024,2048]{1,0:T(8,128)(2,1)S(1)}, bf16[1024,2048]{1,0:T(8,128)(2,1)}, u32[]{:S(2)}) copy-start(bf16[1024,2048]{1,0:T(8,128)(2,1)} %split.1) | copy-start | bytes 12582916
  10.4 4.9 %copy-start.1 = (bf16[512,1536]{1,0:T(8,128)(2,1)S(1)}, bf16[512,1536]{1,0:T(8,128)(2,1)}, u32[]{:S(2)}) copy-start(bf16[512,1536]{1,0:T(8,128)(2,1)} %e_weight.1) | copy-start | bytes 4718596
  10.5 4.9 %copy-start.2 = (bf16[512,1536]{1,0:T(8,128)(2,1)S(1)}, bf16[512,1536]{1,0:T(8,128)(2,1)}, u32[]{:S(2)}) copy-start(bf16[512,1536]{1,0:T(8,128)(2,1)} %d_weight.1) | copy-start | bytes 4718596
  10.5 4.8 %copy-start.3 = (bf16[512,512]{1,0:T(8,128)(2,1)S(1)}, bf16[512,512]{1,0:T(8,128)(2,1)}, u32[]{:S(2)}) copy-start(bf16[512,512]{1,0:T(8,128)(2,1)} %e_out_weight.1) | copy-start | bytes 1572868
  10.5 4.8 %copy-start.4 = (bf16[512,512]{1,0:T(8,128)(2,1)S(1)}, bf16[512,512]{1,0:T(8,128)(2,1)}, u32[]{:S(2)}) copy-start(bf16[512,512]{1,0:T(8,128)(2,1)} %d_out_weight.1) | copy-start | bytes 1572868
  10.5 4.8 %copy-start.5 = (bf16[51,2,512]{2,1,0:T(2,128)(2,1)S(1)}, bf16[51,2,512]{2,1,0:T(2,128)(2,1)}, u32[]{:S(2)}) copy-start(bf16[51,2,512]{2,1,0:T(2,128)(2,1)} %get-tuple-element.16.b0) | copy-start | bytes 313348
  10.5 4.8 %copy-start.6 = (f32[1536]{0:T(1024)S(1)}, f32[1536]{0:T(1024)}, u32[]{:S(2)}) copy-start(f32[1536]{0:T(1024)} %e_bias.1) | copy-start | bytes 18436
  10.5 4.8 %copy-start.7 = (f32[1536]{0:T(1024)S(1)}, f32[1536]{0:T(1024)}, u32[]{:S(2)}) copy-start(f32[1536]{0:T(1024)} %d_bias.1) | copy-start | bytes 18436
  10.5 4.8 %copy-start.8 = (f32[2048]{0:T(1024)S(1)}, f32[2048]{0:T(1024)}, u32[]{:S(2)}) copy-start(f32[2048]{0:T(1024)} %param.41) | copy-start | bytes 24580
  10.5 4.8 %copy-start.9 = (f32[512]{0:T(512)S(1)}, f32[512]{0:T(512)}, u32[]{:S(2)}) copy-start(f32[512]{0:T(512)} %param.26) | copy-start | bytes 6148
  10.6 4.8 %copy-start.10 = (f32[512]{0:T(512)S(1)}, f32[512]{0:T(512)}, u32[]{:S(2)}) copy-start(f32[512]{0:T(512)} %param.27) | copy-start | bytes 6148
  10.6 4.8 %copy-start.11 = (f32[512]{0:T(512)S(1)}, f32[512]{0:T(512)}, u32[]{:S(2)}) copy-start(f32[512]{0:T(512)} %param.31) | copy-start | bytes 6148
  10.6 4.8 %copy-start.12 = (f32[512]{0:T(512)S(1)}, f32[512]{0:T(512)}, u32[]{:S(2)}) copy-start(f32[512]{0:T(512)} %param.33) | copy-start | bytes 6148
  10.6 4.8 %copy-start.13 = (f32[512]{0:T(512)S(1)}, f32[512]{0:T(512)}, u32[]{:S(2)}) copy-start(f32[512]{0:T(512)} %param.34) | copy-start | bytes 6148
  10.6 4.8 %copy-start.14 = (f32[512]{0:T(512)S(1)}, f32[512]{0:T(512)}, u32[]{:S(2)}) copy-start(f32[512]{0:T(512)} %param.38) | copy-start | bytes 6148
  24.6 5.3 %collective-permute-start.3 = (bf16[48,2,512]{2,1,0:T(2,128)(2,1)S(1)}, bf16[48,2,512]{2,1,0:T(2,128)(2,1)S(1)}, u32[]{:S(2)}, u32[]{:S(2)}) collective-permute-start(bf16[48,2,512]{2,1,0:T(2,128)(2,1)S(1)} %get-tuple-element.23), channel_id=1, source_target_pairs={{1,0},{2,1},{3,2},{4,3},{5,4},{6,5},{7,6},{8,7},{9,8},{10,9},{11,1... | collective-permute-start | bytes 294920 | tf_op jit(solution)/shard_map/ppermute | solution.py:491
  24.8 5.1 %collective-permute-start.4 = (bf16[48,2,512]{2,1,0:T(2,128)(2,1)S(1)}, bf16[48,2,512]{2,1,0:T(2,128)(2,1)S(1)}, u32[]{:S(2)}, u32[]{:S(2)}) collective-permute-start(bf16[48,2,512]{2,1,0:T(2,128)(2,1)S(1)} %get-tuple-element.24), channel_id=1, source_target_pairs={{224,0},{33,1},{226,2},{35,3},{228,4},{37,5},{230,6},{39,7},{232,8... | collective-permute-start | bytes 294920 | tf_op jit(solution)/shard_map/ppermute | solution.py:491
  27.7 8.3 %collective-permute-start.5 = (bf16[48,2,512]{2,1,0:T(2,128)(2,1)S(1)}, bf16[48,2,512]{2,1,0:T(2,128)(2,1)S(1)}, u32[]{:S(2)}, u32[]{:S(2)}) collective-permute-start(bf16[48,2,512]{2,1,0:T(2,128)(2,1)S(1)} %get-tuple-element.25), channel_id=1, source_target_pairs={{33,0},{226,1},{35,2},{228,3},{37,4},{230,5},{39,6},{232,7},{41,8}... | collective-permute-start | bytes 294920 | tf_op jit(solution)/shard_map/ppermute | solution.py:491
